TPU v7x, 32 devices: a whole 2x2x4 slice. The times are simulated.
32 devices in a mesh: crops: 2 (over x), dap: 16 (over z, y, core).
Axes of the slice: x: 2, y: 2, z: 4, core: 2. Of those that a mesh axis runs over, the one named last changes fastest.
Arguments:
- homolog_embedding: bfloat16 [64, 128, 256], P(('crops', 'dap')), parts along dimension 0, may hold values from -6 to 6
- coverage_indicator: int32 [64, 128], P(('crops', 'dap')), parts along dimension 0, may hold values from 0 to 1, as said below
- genuine_amino_flag: int32 [256], P('crops'), parts along dimension 0, may hold values 0 or 1
- couple_embedding: bfloat16 [256, 128, 128], P(('crops', 'dap')), parts along dimension 0, may hold values from -6 to 6
- pairing_entry_matrices: bfloat16 [256, 2, 32], replicated, may hold values from -0.375 to 0.375
- pairing_exit_matrix: bfloat16 [1024, 128], replicated, may hold values from -0.75 to 0.75
- trilateral_entry_matrices: bfloat16 [2, 128, 5, 128], replicated, may hold values from -0.5 to 0.5
- trilateral_exit_matrices: bfloat16 [2, 128, 128], replicated, may hold values from -0.5 to 0.5
Outputs:
- pair_out: bfloat16 [256, 128, 128], P(('crops', 'dap')), parts along dimension 0
There are 2 independent parts, one for each index of `crops`. A program takes and returns all parts, laid end to end along the dimension named above; an argument that names none is the same for every part. Nothing has to cross between parts.
Inputs may be any that keep to these rules, and one draw needn't show every extreme that they name: `coverage_indicator`: row 0 is all ones (the query sequence); every other row is one run of ones over consecutive residues, zeros elsewhere.
All inputs are finite; a program needn't handle non-finite values.
Results may differ from a plain program's by a relative error of at most 0.0085.
Values may be sent and summed in bfloat16 or wider, within the bound.
No kernel may reach another device: no remote copies, remote signals or barrier semaphores. Data moves between devices by JAX's collectives and lax.ppermute only.
A program may use at most 128 MiB of HBM per device.

v0:
```python
import math

import jax
import jax.numpy as jnp
from jax import lax
from jax.sharding import PartitionSpec as P


def standardize_features(values, axis):
    average = jnp.mean(values, axis=axis, keepdims=True)
    centered = values - average
    variance = jnp.mean(centered * centered, axis=axis, keepdims=True)
    return centered * lax.rsqrt(variance + 1e-05)


def outer_update(
    left_local, mask_local, right_cols, mask_cols, couple_embedding, pairing_exit_matrix
):
    proj_width = left_local.shape[1]
    local_rows = left_local.shape[2]
    col_total = right_cols.shape[2]
    block_size = col_total if col_total <= 256 else math.gcd(col_total, 256)
    result = jnp.zeros((local_rows, col_total, couple_embedding.shape[2]), jnp.bfloat16)

    def one_block(block_index, result):
        col_begin = block_index * block_size
        columns = lax.dynamic_slice_in_dim(right_cols, col_begin, block_size, 2)
        column_mask = lax.dynamic_slice_in_dim(mask_cols, col_begin, block_size, 2)
        tensor_accumulant = jnp.einsum(
            "rzp,rej->pjze", left_local, columns, preferred_element_type=jnp.float32
        )
        tensor_accumulant = tensor_accumulant.astype(jnp.bfloat16).reshape(
            local_rows, block_size, proj_width * proj_width
        )
        pair_update = jnp.einsum(
            "ijf,fc->ijc",
            tensor_accumulant,
            pairing_exit_matrix,
            preferred_element_type=jnp.float32,
        )
        pair_count = jnp.einsum(
            "si,sj->ij", mask_local[:, 0], column_mask[:, 0], preferred_element_type=jnp.float32
        )
        pair_rows = lax.dynamic_slice_in_dim(couple_embedding, col_begin, block_size, 1).astype(
            jnp.float32
        )
        new_rows = (pair_rows + pair_update / pair_count[:, :, None]).astype(jnp.bfloat16)
        return lax.dynamic_update_slice_in_dim(result, new_rows, col_begin, 1)

    return lax.fori_loop(0, col_total // block_size, one_block, result)


def triangle(pair_now, row_mask, weights, out_weight, incoming):
    normalized = standardize_features(pair_now.astype(jnp.float32), -1).astype(jnp.bfloat16)
    projections = jnp.einsum(
        "ijc,ckh->khij", normalized, weights[:, :4], preferred_element_type=jnp.float32
    )
    left_proj = (jax.nn.sigmoid(projections[0]) * projections[1] * row_mask).astype(jnp.bfloat16)
    right_proj = (jax.nn.sigmoid(projections[2]) * projections[3] * row_mask).astype(jnp.bfloat16)
    gate_val = jax.nn.sigmoid(
        jnp.einsum("ijc,ch->ijh", normalized, weights[:, 4], preferred_element_type=jnp.float32)
    )
    einsum_form = "hki,hkj->hij" if incoming else "hik,hjk->hij"
    left_full, right_full = (
        lax.all_to_all(left_proj, "dap", split_axis=0, concat_axis=1, tiled=True),
        lax.all_to_all(right_proj, "dap", split_axis=0, concat_axis=1, tiled=True),
    )
    products = jnp.einsum(einsum_form, left_full, right_full, preferred_element_type=jnp.float32)
    returned = lax.all_to_all(
        products.astype(jnp.bfloat16), "dap", split_axis=1, concat_axis=0, tiled=True
    )
    normed_products = standardize_features(returned.astype(jnp.float32), 0).astype(jnp.bfloat16)
    pair_update = jnp.einsum(
        "hij,hc->ijc", normed_products, out_weight, preferred_element_type=jnp.float32
    )
    return (pair_now.astype(jnp.float32) + gate_val * pair_update).astype(jnp.bfloat16)


def local(
    homolog_embedding,
    coverage_indicator,
    genuine_amino_flag,
    couple_embedding,
    pairing_entry_matrices,
    pairing_exit_matrix,
    trilateral_entry_matrices,
    trilateral_exit_matrices,
):
    local_rows = couple_embedding.shape[0]
    sequence_mask = coverage_indicator.astype(jnp.float32)
    coverage_norm_factor = standardize_features(homolog_embedding.astype(jnp.float32), -1).astype(
        jnp.bfloat16
    )
    mapped_entries = jnp.einsum(
        "rgl,loe->roeg",
        coverage_norm_factor,
        pairing_entry_matrices,
        preferred_element_type=jnp.float32,
    )
    mapped_entries = (mapped_entries * sequence_mask[:, None, None, :]).astype(jnp.bfloat16)
    mask_flat = sequence_mask.astype(jnp.bfloat16)[:, None, :]
    received, mask_rows = (
        lax.all_to_all(mapped_entries, "dap", split_axis=3, concat_axis=0, tiled=True),
        lax.all_to_all(mask_flat[:, None], "dap", split_axis=3, concat_axis=0, tiled=True),
    )
    left_local = received[:, 0]
    mask_local = mask_rows[:, 0]
    pieces = lax.all_gather((received[:, 1], mask_local), "dap", axis=2, tiled=True)
    pair_one = outer_update(
        left_local, mask_local, pieces[0], pieces[1], couple_embedding, pairing_exit_matrix
    )
    residues = genuine_amino_flag.astype(jnp.float32)
    first_row = lax.axis_index("dap") * local_rows
    row_mask = (
        lax.dynamic_slice_in_dim(residues, first_row, local_rows, 0)[:, None] * residues[None, :]
    )
    pair_two = triangle(
        pair_one, row_mask, trilateral_entry_matrices[0], trilateral_exit_matrices[0], False
    )
    return triangle(
        pair_two, row_mask, trilateral_entry_matrices[1], trilateral_exit_matrices[1], True
    )


def solution(mesh):
    return jax.shard_map(
        local,
        mesh=mesh,
        in_specs=(
            P(("crops", "dap"), None, None),
            P(("crops", "dap"), None),
            P("crops"),
            P(("crops", "dap"), None, None),
            P(),
            P(),
            P(),
            P(),
        ),
        out_specs=P(("crops", "dap"), None, None),
        check_vma=False,
    )
```

profile of v0, /device:TPU:0, one launch (start us, length us, event | category | flops | bytes accessed | tf_op | source)
XLA Modules:
  0.0 157.6 jit_solution(8602774494638855187)
XLA Ops:
  0.0 0.7 convert_bitcast_fusion.3
  0.7 0.8 copy.125
  1.5 7.4 %all-to-all-start.1 = ((bf16[2,1,1,128]{0,2,1,3:T(2,128)(2,1)}), bf16[2,1,1,128]{0,2,1,3:T(2,128)(2,1)S(1)}, u32[]{:S(2)}, u32[]{:S(2)}) async-start(bf16[2,1,1,128]{0,2,1,3:T(2,128)(2,1)} %copy.125), calls=%async_computation.1 | async-start | bytes 131072 | tf_op jit(solution)/shard_map/all_to_all | solution.py:104
  8.9 1.0 convert_reduce_fusion
  9.9 1.1 fusion.58
  11.0 1.0 slice_bitcast_fusion.3
  12.1 0.7 convert_element_type.122
  12.8 1.2 fusion.15
  14.2 0.8 reshape.146
  14.9 1.1 copy.115
  16.2 6.0 %all-to-all-start = ((bf16[16,2,512]{2,1,0:T(2,128)(2,1)}), bf16[16,2,512]{2,1,0:T(2,128)(2,1)S(1)}, u32[]{:S(2)}, u32[]{:S(2)}) async-start(bf16[16,2,512]{2,1,0:T(2,128)(2,1)} %reshape.146), calls=%async_computation | async-start | bytes 65536 | tf_op jit(solution)/shard_map/all_to_all | solution.py:103
  22.5 21.8 %all_gather.7 = bf16[32,1,128]{0,2,1:T(8,128)(2,1)S(1)} all-gather(bf16[32,1,8]{0,2,1:T(8,128)(2,1)S(1)} %copy.129), channel_id=1, replica_groups=mesh['crops'=2,'dap'=16] {'dap'}, dimensions={2}, use_global_device_ids=true | all-gather | bytes 8704 | tf_op jit(solution)/shard_map/all_gather | solution.py:108
  44.8 20.5 %all-gather = bf16[32,1,32,128]{2,0,1,3:T(8,128)(2,1)S(1)} all-gather(bf16[32,1,32,8]{2,0,1,3:T(8,128)(2,1)S(1)} %copy.119), channel_id=2, replica_groups=mesh['crops'=2,'dap'=16] {'dap'}, dimensions={3}, use_global_device_ids=true | all-gather | bytes 278528 | tf_op jit(solution)/shard_map/all_gather | solution.py:108
  65.3 1.3 copy.162
  66.7 0.7 convert_bitcast_fusion
  67.4 1.4 copy.122
  68.7 0.5 fusion.87
  70.1 0.9 copy.137
  71.0 4.1 %all-to-all-start.2 = ((bf16[128,8,128]{2,1,0:T(8,128)(2,1)}), bf16[128,8,128]{2,1,0:T(8,128)(2,1)S(1)}, u32[]{:S(2)}, u32[]{:S(2)}) async-start(bf16[128,8,128]{2,1,0:T(8,128)(2,1)} %copy.137), calls=%async_computation.2 | async-start | bytes 524288 | tf_op jit(solution)/shard_map/all_to_all | solution.py:65
  75.3 9.9 %all-to-all-done.2 = bf16[128,8,128]{2,1,0:T(8,128)(2,1)S(1)} async-done(((bf16[128,8,128]{2,1,0:T(8,128)(2,1)}), bf16[128,8,128]{2,1,0:T(8,128)(2,1)S(1)}, u32[]{:S(2)}, u32[]{:S(2)}) %all-to-all-start.2) | async-done | bytes 262176 | tf_op jit(solution)/shard_map/all_to_all | solution.py:65
  85.2 12.8 %all_to_all.123 = bf16[128,8,128]{2,1,0:T(8,128)(2,1)S(1)} all-to-all(bf16[128,8,128]{2,1,0:T(8,128)(2,1)S(1)} %copy.141), channel_id=1, replica_groups=mesh['crops'=2,'dap'=16] {'dap'}, dimensions={0} | all-to-all | bytes 524288 | tf_op jit(solution)/shard_map/all_to_all | solution.py:66
  98.3 0.9 copy.143
  99.2 3.5 %all-to-all-start.4 = ((bf16[8,128,128]{2,0,1:T(8,128)(2,1)}), bf16[8,128,128]{2,0,1:T(8,128)(2,1)S(1)}, u32[]{:S(2)}, u32[]{:S(2)}) async-start(bf16[8,128,128]{2,0,1:T(8,128)(2,1)} %copy.143), calls=%async_computation.4 | async-start | bytes 524288 | tf_op jit(solution)/shard_map/all_to_all | solution.py:69
  103.0 9.7 %all-to-all-done.4 = bf16[8,128,128]{2,0,1:T(8,128)(2,1)S(1)} async-done(((bf16[8,128,128]{2,0,1:T(8,128)(2,1)}), bf16[8,128,128]{2,0,1:T(8,128)(2,1)S(1)}, u32[]{:S(2)}, u32[]{:S(2)}) %all-to-all-start.4) | async-done | bytes 262176 | tf_op jit(solution)/shard_map/all_to_all | solution.py:69
  114.1 0.9 copy.150
  114.9 3.5 %all-to-all-start.5 = ((bf16[128,8,128]{2,1,0:T(8,128)(2,1)}), bf16[128,8,128]{2,1,0:T(8,128)(2,1)S(1)}, u32[]{:S(2)}, u32[]{:S(2)}) async-start(bf16[128,8,128]{2,1,0:T(8,128)(2,1)} %copy.150), calls=%async_computation.5 | async-start | bytes 524288 | tf_op jit(solution)/shard_map/all_to_all | solution.py:65
  118.7 9.8 %all-to-all-done.5 = bf16[128,8,128]{2,1,0:T(8,128)(2,1)S(1)} async-done(((bf16[128,8,128]{2,1,0:T(8,128)(2,1)}), bf16[128,8,128]{2,1,0:T(8,128)(2,1)S(1)}, u32[]{:S(2)}, u32[]{:S(2)}) %all-to-all-start.5) | async-done | bytes 262176 | tf_op jit(solution)/shard_map/all_to_all | solution.py:65
  128.5 12.8 %all_to_all.124 = bf16[128,8,128]{2,1,0:T(8,128)(2,1)S(1)} all-to-all(bf16[128,8,128]{2,1,0:T(8,128)(2,1)S(1)} %copy.152), channel_id=1, replica_groups=mesh['crops'=2,'dap'=16] {'dap'}, dimensions={0} | all-to-all | bytes 524288 | tf_op jit(solution)/shard_map/all_to_all | solution.py:66
  141.6 0.9 copy.155
  142.5 3.5 %all-to-all-start.7 = ((bf16[8,128,128]{2,0,1:T(8,128)(2,1)}), bf16[8,128,128]{2,0,1:T(8,128)(2,1)S(1)}, u32[]{:S(2)}, u32[]{:S(2)}) async-start(bf16[8,128,128]{2,0,1:T(8,128)(2,1)} %copy.155), calls=%async_computation.7 | async-start | bytes 524288 | tf_op jit(solution)/shard_map/all_to_all | solution.py:69
  146.3 9.7 %all-to-all-done.7 = bf16[8,128,128]{2,0,1:T(8,128)(2,1)S(1)} async-done(((bf16[8,128,128]{2,0,1:T(8,128)(2,1)}), bf16[8,128,128]{2,0,1:T(8,128)(2,1)S(1)}, u32[]{:S(2)}, u32[]{:S(2)}) %all-to-all-start.7) | async-done | bytes 262176 | tf_op jit(solution)/shard_map/all_to_all | solution.py:69
  156.7 0.9 copy.160
  (51 shorter events, 5.7 us)
Async XLA Ops:
  0.0 68.7 %copy-start = (bf16[1024,128]{1,0:T(8,128)(2,1)S(1)}, bf16[1024,128]{1,0:T(8,128)(2,1)}, u32[]{:S(2)}) copy-start(bf16[1024,128]{1,0:T(8,128)(2,1)} %param.13) | copy-start | bytes 786436
  1.5 14.7 %all-to-all-start.1 = ((bf16[2,1,1,128]{0,2,1,3:T(2,128)(2,1)}), bf16[2,1,1,128]{0,2,1,3:T(2,128)(2,1)S(1)}, u32[]{:S(2)}, u32[]{:S(2)}) async-start(bf16[2,1,1,128]{0,2,1,3:T(2,128)(2,1)} %copy.125), calls=%async_computation.1 | async-start | bytes 131072 | tf_op jit(solution)/shard_map/all_to_all | solution.py:104
  16.2 28.3 %all-to-all-start = ((bf16[16,2,512]{2,1,0:T(2,128)(2,1)}), bf16[16,2,512]{2,1,0:T(2,128)(2,1)S(1)}, u32[]{:S(2)}, u32[]{:S(2)}) async-start(bf16[16,2,512]{2,1,0:T(2,128)(2,1)} %reshape.146), calls=%async_computation | async-start | bytes 65536 | tf_op jit(solution)/shard_map/all_to_all | solution.py:103
  71.0 14.1 %all-to-all-start.2 = ((bf16[128,8,128]{2,1,0:T(8,128)(2,1)}), bf16[128,8,128]{2,1,0:T(8,128)(2,1)S(1)}, u32[]{:S(2)}, u32[]{:S(2)}) async-start(bf16[128,8,128]{2,1,0:T(8,128)(2,1)} %copy.137), calls=%async_computation.2 | async-start | bytes 524288 | tf_op jit(solution)/shard_map/all_to_all | solution.py:65
  98.3 14.6 %copy-start.1 = (bf16[2,128,128]{2,1,0:T(8,128)(2,1)S(1)}, bf16[2,128,128]{2,1,0:T(8,128)(2,1)}, u32[]{:S(2)}) copy-start(bf16[2,128,128]{2,1,0:T(8,128)(2,1)} %param.15) | copy-start | bytes 196612
  99.2 13.5 %all-to-all-start.4 = ((bf16[8,128,128]{2,0,1:T(8,128)(2,1)}), bf16[8,128,128]{2,0,1:T(8,128)(2,1)S(1)}, u32[]{:S(2)}, u32[]{:S(2)}) async-start(bf16[8,128,128]{2,0,1:T(8,128)(2,1)} %copy.143), calls=%async_computation.4 | async-start | bytes 524288 | tf_op jit(solution)/shard_map/all_to_all | solution.py:69
  114.9 13.5 %all-to-all-start.5 = ((bf16[128,8,128]{2,1,0:T(8,128)(2,1)}), bf16[128,8,128]{2,1,0:T(8,128)(2,1)S(1)}, u32[]{:S(2)}, u32[]{:S(2)}) async-start(bf16[128,8,128]{2,1,0:T(8,128)(2,1)} %copy.150), calls=%async_computation.5 | async-start | bytes 524288 | tf_op jit(solution)/shard_map/all_to_all | solution.py:65
  142.5 13.5 %all-to-all-start.7 = ((bf16[8,128,128]{2,0,1:T(8,128)(2,1)}), bf16[8,128,128]{2,0,1:T(8,128)(2,1)S(1)}, u32[]{:S(2)}, u32[]{:S(2)}) async-start(bf16[8,128,128]{2,0,1:T(8,128)(2,1)} %copy.155), calls=%async_computation.7 | async-start | bytes 524288 | tf_op jit(solution)/shard_map/all_to_all | solution.py:69
where the time goes:
time: 158 us
  blocking collectives  67.9 us (43%)
  waiting for transfers between devices  39 us (25%)
  starting transfers between devices  28.1 us (18%)
  local copies, waits for them, and re-layouts  12.1 us (8%)
  matrix products  5.19 us (3%)
  other arithmetic  4.86 us (3%)
    all_gather x2, blocking collectives, local(): lax.all_gather((received[:, 1], mask_local), 'dap', axis=2, tiled=True)  42.3 us
    all_to_all x2, blocking collectives, triangle(): lax.all_to_all(right_proj, 'dap', split_axis=0, concat_axis=1, tiled=True)  25.6 us
    all_to_all x2, waiting for transfers between devices, triangle(): lax.all_to_all(left_proj, 'dap', split_axis=0, concat_axis=1, tiled=True)  19.7 us
    all_to_all x2, waiting for transfers between devices, triangle(): lax.all_to_all(products.astype(jnp.bfloat16), 'dap', split_axis=1, concat...  19.4 us
    all_to_all x2, starting transfers between devices, triangle(): lax.all_to_all(left_proj, 'dap', split_axis=0, concat_axis=1, tiled=True)  7.63 us
    all_to_all x1, starting transfers between devices, local(): lax.all_to_all(mask_flat[:, None], 'dap', split_axis=3, concat_axis=0, ti...  7.39 us
    all_to_all x2, starting transfers between devices, triangle(): lax.all_to_all(products.astype(jnp.bfloat16), 'dap', split_axis=1, concat...  7.07 us
    all_to_all x1, starting transfers between devices, local(): lax.all_to_all(mapped_entries, 'dap', split_axis=3, concat_axis=0, tiled=...  6.02 us
  transfers between devices with their start and end apart: 6, of which 4 were waited for; matrix products, arithmetic and copies ran while one was open for 5% of the time, Pallas kernels for 0%

commit v1 on v0

v1 whole, which is shorter than its diff:
```python
import jax
import jax.numpy as jnp
from jax import lax
from jax.sharding import PartitionSpec as P


def standardize_features(values, axis):
    average = jnp.mean(values, axis=axis, keepdims=True)
    centered = values - average
    variance = jnp.mean(centered * centered, axis=axis, keepdims=True)
    return centered * lax.rsqrt(variance + 1e-05)


def exchange(blocks):
    return lax.all_to_all(blocks, "dap", split_axis=0, concat_axis=0, tiled=True)


def outer_update(left_local, mask_local, right_cols, mask_cols, couple_embedding, pairing_exit_matrix):
    proj_width = left_local.shape[1]
    local_rows = left_local.shape[2]
    col_total = right_cols.shape[2]
    outer = jnp.einsum("rzp,rej->pjze", left_local, right_cols, preferred_element_type=jnp.float32)
    outer = outer.astype(jnp.bfloat16).reshape(local_rows, col_total, proj_width * proj_width)
    pair_update = jnp.einsum("ijf,fc->ijc", outer, pairing_exit_matrix, preferred_element_type=jnp.float32)
    pair_count = jnp.einsum("si,sj->ij", mask_local, mask_cols, preferred_element_type=jnp.float32)
    return (couple_embedding.astype(jnp.float32) + pair_update / pair_count[:, :, None]).astype(jnp.bfloat16)


def triangle(pair_now, row_mask, weights, out_weight, incoming, devices):
    rows, cols, channels = pair_now.shape
    part = channels // devices
    normalized = standardize_features(pair_now.astype(jnp.float32), -1).astype(jnp.bfloat16)
    projections = jnp.einsum("ijc,ckh->khij", normalized, weights[:, :4], preferred_element_type=jnp.float32)
    left_proj = (jax.nn.sigmoid(projections[0]) * projections[1] * row_mask).astype(jnp.bfloat16)
    right_proj = (jax.nn.sigmoid(projections[2]) * projections[3] * row_mask).astype(jnp.bfloat16)
    gate_val = jax.nn.sigmoid(
        jnp.einsum("ijc,ch->ijh", normalized, weights[:, 4], preferred_element_type=jnp.float32)
    )
    both = jnp.stack(
        [left_proj.reshape(devices, part, rows, cols), right_proj.reshape(devices, part, rows, cols)], axis=1
    )
    both = exchange(both)
    both = jnp.transpose(both, (1, 2, 0, 3, 4)).reshape(2, part, devices * rows, cols)
    einsum_form = "hki,hkj->hij" if incoming else "hik,hjk->hij"
    products = jnp.einsum(einsum_form, both[0], both[1], preferred_element_type=jnp.float32).astype(jnp.bfloat16)
    products = jnp.transpose(products.reshape(part, devices, rows, cols), (1, 0, 2, 3))
    returned = exchange(products).reshape(channels, rows, cols)
    normed_products = standardize_features(returned.astype(jnp.float32), 0).astype(jnp.bfloat16)
    pair_update = jnp.einsum("hij,hc->ijc", normed_products, out_weight, preferred_element_type=jnp.float32)
    return (pair_now.astype(jnp.float32) + gate_val * pair_update).astype(jnp.bfloat16)


def local(
    devices,
    homolog_embedding,
    coverage_indicator,
    genuine_amino_flag,
    couple_embedding,
    pairing_entry_matrices,
    pairing_exit_matrix,
    trilateral_entry_matrices,
    trilateral_exit_matrices,
):
    rows, cols, _ = couple_embedding.shape
    held = homolog_embedding.shape[0]
    width = pairing_entry_matrices.shape[2]
    sequence_mask = coverage_indicator.astype(jnp.float32)
    msa_norm = standardize_features(homolog_embedding.astype(jnp.float32), -1).astype(jnp.bfloat16)
    entries = jnp.einsum("rgl,loe->roeg", msa_norm, pairing_entry_matrices, preferred_element_type=jnp.float32)
    entries = (entries * sequence_mask[:, None, None, :]).astype(jnp.bfloat16)
    own = jnp.transpose(entries[:, 0].reshape(held, width, devices, rows), (2, 0, 1, 3))
    shared = jnp.concatenate([entries[:, 1].reshape(held, width * cols), sequence_mask.astype(jnp.bfloat16)], axis=1)
    packed = jnp.concatenate(
        [jnp.broadcast_to(shared[None], (devices,) + shared.shape), own.reshape(devices, held, width * rows)], axis=2
    )
    packed = exchange(packed).reshape(devices * held, -1)
    right_cols = packed[:, : width * cols].reshape(-1, width, cols)
    mask_cols = packed[:, width * cols : (width + 1) * cols]
    left_local = packed[:, (width + 1) * cols :].reshape(-1, width, rows)
    first_row = lax.axis_index("dap") * rows
    mask_local = lax.dynamic_slice_in_dim(mask_cols, first_row, rows, 1)
    pair_one = outer_update(left_local, mask_local, right_cols, mask_cols, couple_embedding, pairing_exit_matrix)
    residues = genuine_amino_flag.astype(jnp.float32)
    row_mask = lax.dynamic_slice_in_dim(residues, first_row, rows, 0)[:, None] * residues[None, :]
    pair_two = triangle(
        pair_one, row_mask, trilateral_entry_matrices[0], trilateral_exit_matrices[0], False, devices
    )
    return triangle(pair_two, row_mask, trilateral_entry_matrices[1], trilateral_exit_matrices[1], True, devices)


def solution(mesh):
    devices = mesh.shape["dap"]
    return jax.shard_map(
        lambda *arrays: local(devices, *arrays),
        mesh=mesh,
        in_specs=(
            P(("crops", "dap"), None, None),
            P(("crops", "dap"), None),
            P("crops"),
            P(("crops", "dap"), None, None),
            P(),
            P(),
            P(),
            P(),
        ),
        out_specs=P(("crops", "dap"), None, None),
        check_vma=False,
    )
```

time: 158 us -> 97.8 us (0.62)
  blocking collectives: 67.9 us -> 34.6 us
  starting transfers between devices: 28.1 us -> 15.7 us
  waiting for transfers between devices: 39 us -> 29.3 us
  local copies, waits for them, and re-layouts: 12.1 us -> 5.2 us
  other arithmetic: 4.86 us -> 6.73 us
    all_gather x2 -> x0, blocking collectives: 42.3 us -> none  [local(): lax.all_gather((received[:, 1], mask_local), 'dap', axis=2, tiled=True)]
    all_to_all x6 -> x3, starting transfers between devices: 28.1 us -> 15.7 us  [exchange(): lax.all_to_all(blocks, 'dap', split_axis=0, concat_axis=0, tiled=True)]
    all_to_all x6 -> x3, waiting for transfers between devices: 39 us -> 29.3 us  [exchange(): lax.all_to_all(blocks, 'dap', split_axis=0, concat_axis=0, tiled=True)]
    all_to_all x2, blocking collectives: 25.6 us -> 34.6 us  [exchange(): lax.all_to_all(blocks, 'dap', split_axis=0, concat_axis=0, tiled=True)]
    convert_element_type x9 -> x1, local copies, waits for them, and re-layouts: 5.44 us -> 1.35 us  [outer_update(): outer.astype(jnp.bfloat16)]
    unnamed x9 -> x16, local copies, waits for them, and re-layouts: 2.33 us -> 0.45 us
    reshape x0 -> x4, local copies, waits for them, and re-layouts: none -> 1.74 us  [the longest x2 1.54 us: triangle(): products.reshape(part, devices, rows, cols)]
  transfers between devices with their start and end apart: 6 -> 3, of which waited for: 4 -> 3; matrix products, arithmetic and copies ran while one was open for 5% -> 1% of each run, Pallas kernels for 0% -> 0%
where the time goes in v1:
time: 97.8 us; the launch traced here: 97.2 us
  blocking collectives  34.6 us (35%)
  waiting for transfers between devices  29.3 us (30%)
  starting transfers between devices  15.7 us (16%)
  other arithmetic  6.73 us (7%)
  matrix products  5.27 us (5%)
  local copies, waits for them, and re-layouts  5.2 us (5%)
    all_to_all x2, blocking collectives, exchange(): lax.all_to_all(blocks, 'dap', split_axis=0, concat_axis=0, tiled=True)  34.6 us
    all_to_all x3, waiting for transfers between devices, exchange(): lax.all_to_all(blocks, 'dap', split_axis=0, concat_axis=0, tiled=True)  29.3 us
    all_to_all x3, starting transfers between devices, exchange(): lax.all_to_all(blocks, 'dap', split_axis=0, concat_axis=0, tiled=True)  15.7 us
  transfers between devices with their start and end apart: 3, of which 3 were waited for; matrix products, arithmetic and copies ran while one was open for 1% of the time, Pallas kernels for 0%

profile of v1, /device:TPU:0, one launch (start us, length us, event | category | flops | bytes accessed | tf_op | source)
XLA Modules:
  0.0 97.2 jit_solution(15802482440592365732)
XLA Ops:
  0.0 1.1 %convert_reduce_fusion.2 = f32[2,128]{1,0:T(2,128)S(1)} fusion(bf16[2,128,256]{2,1,0:T(8,128)(2,1)} %param.8), kind=kLoop, calls=%fused_computation.81 | loop fusion | flops 130816 | bytes 132096 | tf_op jit(solution)/shard_map/reduce_sum | solution.py:8
  1.1 1.1 %fusion.48 = f32[2,128]{1,0:T(2,128)S(1)} fusion(bf16[2,128,256]{2,1,0:T(8,128)(2,1)} %param.8, f32[2,128]{1,0:T(2,128)S(1)} %broadcast_multiply_fusion.5), kind=kLoop, calls=%fused_computation.85 | loop fusion | flops 261888 | bytes 133120 | tf_op jit(solution)/shard_map/reduce_sum | solution.py:10
  2.2 0.7 convert_convert_fusion
  2.9 1.2 %fusion.17 = bf16[2,2,32,128]{3,2,1,0:T(8,128)(2,1)S(1)} fusion(bf16[2,128,256]{2,1,0:T(8,128)(2,1)} %param.8, f32[2,128]{1,0:T(2,128)S(1)} %add_rsqrt_fusion.4, f32[2,128]{1,0:T(2,128)S(1)} %broadcast_multiply_fusion.5, bf16[256,2,32]{0,2,1:T(8,128)(2,1)} %param.12, f32[2,128]{1,0:T(2,128)S(1)} %get-tuple-element.20), kind=kOutput, calls=%fused_computation.28 | convolution fusion | flops 8683520 | bytes 199680 | tf_op jit(solution)/shard_map/rgl,loe->roeg/dot_general | solution.py:69
  4.7 1.0 pad_maximum_fusion.2
  5.6 7.4 %all-to-all-start = ((bf16[16,2,4480]{2,1,0:T(2,128)(2,1)}), bf16[16,2,4480]{2,1,0:T(2,128)(2,1)S(1)}, u32[]{:S(2)}, u32[]{:S(2)}) async-start(bf16[16,2,4480]{2,1,0:T(2,128)(2,1)} %pad_maximum_fusion.2), calls=%async_computation | async-start | bytes 573440 | tf_op jit(solution)/shard_map/all_to_all | solution.py:15
  13.6 9.9 %all-to-all-done = bf16[16,2,4480]{2,1,0:T(2,128)(2,1)S(1)} async-done(((bf16[16,2,4480]{2,1,0:T(2,128)(2,1)}), bf16[16,2,4480]{2,1,0:T(2,128)(2,1)S(1)}, u32[]{:S(2)}, u32[]{:S(2)}) %all-to-all-start) | async-done | bytes 286752 | tf_op jit(solution)/shard_map/all_to_all | solution.py:15
  23.6 0.3 fusion.71
  24.1 0.7 convert_bitcast_fusion
  24.8 1.4 %copy.91 = bf16[8,128,32,32]{1,3,2,0:T(8,128)(2,1)S(1)} copy(bf16[8,128,32,32]{1,2,0,3:T(8,128)(2,1)S(1)} %convert_bitcast_fusion) | data formatting | bytes 4194304 | tf_op jit(solution)/shard_map/convert_element_type | solution.py:23
  26.1 0.5 fusion.75
  26.8 0.4 convolution_bitcast_fusion.1
  27.2 0.3 fusion.38
  27.5 0.6 fusion.45
  28.2 17.3 %all_to_all.25 = bf16[16,2,8,8,128]{4,3,2,1,0:T(8,128)(2,1)S(1)} all-to-all(bf16[16,2,8,8,128]{4,3,2,1,0:T(8,128)(2,1)S(1)} %pad_maximum_fusion), channel_id=1, replica_groups=mesh['crops'=2,'dap'=16] {'dap'}, dimensions={0} | all-to-all | bytes 1048576 | tf_op jit(solution)/shard_map/all_to_all | solution.py:15
  45.6 0.3 fusion.14
  45.9 0.8 copy.178
  46.6 4.2 %all-to-all-start.2 = ((bf16[16,8,8,128]{3,2,1,0:T(8,128)(2,1)}), bf16[16,8,8,128]{3,2,1,0:T(8,128)(2,1)S(1)}, u32[]{:S(2)}, u32[]{:S(2)}) async-start(bf16[16,8,8,128]{3,2,1,0:T(8,128)(2,1)} %bitcast.115), calls=%async_computation.2 | async-start | bytes 524288 | tf_op jit(solution)/shard_map/all_to_all | solution.py:15
  50.9 0.3 fusion.2
  51.2 9.7 %all-to-all-done.2 = bf16[16,8,8,128]{3,2,1,0:T(8,128)(2,1)S(1)} async-done(((bf16[16,8,8,128]{3,2,1,0:T(8,128)(2,1)}), bf16[16,8,8,128]{3,2,1,0:T(8,128)(2,1)S(1)}, u32[]{:S(2)}, u32[]{:S(2)}) %all-to-all-start.2) | async-done | bytes 262176 | tf_op jit(solution)/shard_map/all_to_all | solution.py:15
  61.3 0.3 fusion.76
  61.7 0.5 convolution_bitcast_fusion
  62.2 0.3 fusion.30
  62.4 0.6 fusion.43
  63.1 17.2 %all_to_all.26 = bf16[16,2,8,8,128]{4,3,2,1,0:T(8,128)(2,1)S(1)} all-to-all(bf16[16,2,8,8,128]{4,3,2,1,0:T(8,128)(2,1)S(1)} %pad_maximum_fusion.1), channel_id=1, replica_groups=mesh['crops'=2,'dap'=16] {'dap'}, dimensions={0} | all-to-all | bytes 1048576 | tf_op jit(solution)/shard_map/all_to_all | solution.py:15
  80.5 0.3 fusion.15
  80.8 0.8 copy.177
  81.5 4.1 %all-to-all-start.4 = ((bf16[16,8,8,128]{3,2,1,0:T(8,128)(2,1)}), bf16[16,8,8,128]{3,2,1,0:T(8,128)(2,1)S(1)}, u32[]{:S(2)}, u32[]{:S(2)}) async-start(bf16[16,8,8,128]{3,2,1,0:T(8,128)(2,1)} %bitcast.114), calls=%async_computation.4 | async-start | bytes 524288 | tf_op jit(solution)/shard_map/all_to_all | solution.py:15
  85.7 0.3 fusion.5
  86.0 9.7 %all-to-all-done.4 = bf16[16,8,8,128]{3,2,1,0:T(8,128)(2,1)S(1)} async-done(((bf16[16,8,8,128]{3,2,1,0:T(8,128)(2,1)}), bf16[16,8,8,128]{3,2,1,0:T(8,128)(2,1)S(1)}, u32[]{:S(2)}, u32[]{:S(2)}) %all-to-all-start.4) | async-done | bytes 262176 | tf_op jit(solution)/shard_map/all_to_all | solution.py:15
  96.1 0.3 fusion.11
  96.4 0.9 copy.115
  (51 shorter events, 2.6 us)
Async XLA Ops:
  0.0 26.1 %copy-start = (bf16[1024,128]{1,0:T(8,128)(2,1)S(1)}, bf16[1024,128]{1,0:T(8,128)(2,1)}, u32[]{:S(2)}) copy-start(bf16[1024,128]{1,0:T(8,128)(2,1)} %param.13) | copy-start | bytes 786436
  0.0 13.0 %copy-start.2 = (bf16[8,128,128]{2,1,0:T(8,128)(2,1)S(1)}, bf16[8,128,128]{2,1,0:T(8,128)(2,1)}, u32[]{:S(2)}) copy-start(bf16[8,128,128]{2,1,0:T(8,128)(2,1)} %param.11) | copy-start | bytes 786436
  0.0 13.2 %copy-start.1 = (bf16[2,128,5,128]{3,1,2,0:T(8,128)(2,1)S(1)}, bf16[2,128,5,128]{3,1,2,0:T(8,128)(2,1)}, u32[]{:S(2)}) copy-start(bf16[2,128,5,128]{3,1,2,0:T(8,128)(2,1)} %param.14) | copy-start | bytes 983044
  0.0 13.5 %copy-start.4 = (s32[128]{0:T(128)S(1)}, s32[128]{0:T(128)}, u32[]{:S(2)}) copy-start(s32[128]{0:T(128)} %param.10) | copy-start | bytes 1540
  5.6 17.8 %all-to-all-start = ((bf16[16,2,4480]{2,1,0:T(2,128)(2,1)}), bf16[16,2,4480]{2,1,0:T(2,128)(2,1)S(1)}, u32[]{:S(2)}, u32[]{:S(2)}) async-start(bf16[16,2,4480]{2,1,0:T(2,128)(2,1)} %pad_maximum_fusion.2), calls=%async_computation | async-start | bytes 573440 | tf_op jit(solution)/shard_map/all_to_all | solution.py:15
  46.6 14.7 %copy-start.3 = (bf16[2,128,128]{2,1,0:T(8,128)(2,1)S(1)}, bf16[2,128,128]{2,1,0:T(8,128)(2,1)}, u32[]{:S(2)}) copy-start(bf16[2,128,128]{2,1,0:T(8,128)(2,1)} %param.15) | copy-start | bytes 196612
  46.6 14.3 %all-to-all-start.2 = ((bf16[16,8,8,128]{3,2,1,0:T(8,128)(2,1)}), bf16[16,8,8,128]{3,2,1,0:T(8,128)(2,1)S(1)}, u32[]{:S(2)}, u32[]{:S(2)}) async-start(bf16[16,8,8,128]{3,2,1,0:T(8,128)(2,1)} %bitcast.115), calls=%async_computation.2 | async-start | bytes 524288 | tf_op jit(solution)/shard_map/all_to_all | solution.py:15
  81.5 14.2 %all-to-all-start.4 = ((bf16[16,8,8,128]{3,2,1,0:T(8,128)(2,1)}), bf16[16,8,8,128]{3,2,1,0:T(8,128)(2,1)S(1)}, u32[]{:S(2)}, u32[]{:S(2)}) async-start(bf16[16,8,8,128]{3,2,1,0:T(8,128)(2,1)} %bitcast.114), calls=%async_computation.4 | async-start | bytes 524288 | tf_op jit(solution)/shard_map/all_to_all | solution.py:15

commit v2 on v1

--- a/solution.py
+++ b/solution.py
@@ -1,7 +1,35 @@
+import functools
+
 import jax
 import jax.numpy as jnp
 from jax import lax
+from jax.experimental import pallas as pl
+from jax.experimental.pallas import tpu as pltpu
 from jax.sharding import PartitionSpec as P
+
+F32 = jnp.float32
+BF16 = jnp.bfloat16
+EPS = 1e-05
+LANES = 128
+VMEM = pl.BlockSpec(memory_space=pltpu.VMEM)
+SMEM = pl.BlockSpec(memory_space=pltpu.SMEM)
+PARAMS = pltpu.CompilerParams(vmem_limit_bytes=40 * 1024 * 1024)
+
+
+def dot(a, b, left=1, right=0):
+    return lax.dot_general(a, b, (((left,), (right,)), ((), ())), preferred_element_type=F32)
+
+
+def sigmoid(values):
+    return 0.5 * jnp.tanh(0.5 * values) + 0.5
+
+
+def norm(values, axis):
+    size = values.shape[axis]
+    average = jnp.sum(values, axis=axis, keepdims=True) * (1.0 / size)
+    centered = values - average
+    variance = jnp.sum(centered * centered, axis=axis, keepdims=True) * (1.0 / size)
+    return (centered * lax.rsqrt(variance + EPS)).astype(BF16)
 
 
 def standardize_features(values, axis):
@@ -88,10 +116,266 @@
     return triangle(pair_two, row_mask, trilateral_entry_matrices[1], trilateral_exit_matrices[1], True, devices)
 
 
+def entry_kernel(x_ref, cover_ref, own_weight_ref, shared_weight_ref, out_ref):
+    held, cols, _ = x_ref.shape
+    width = shared_weight_ref.shape[0]
+    devices = out_ref.shape[0]
+    cover = cover_ref[...].astype(F32)
+    columns = jnp.transpose(jnp.concatenate([cover, jnp.zeros((8 - held, cols), F32)], axis=0))
+    own = jnp.zeros((cols, LANES), F32)
+    marks = []
+    for s in range(held):
+        normalized = norm(x_ref[s].astype(F32), -1)
+        shared = (dot(shared_weight_ref[...], normalized, 1, 1) * cover[s : s + 1]).astype(BF16)
+        for peer in range(devices):
+            out_ref[peer, s * width : (s + 1) * width, :] = shared
+        own = own + dot(normalized, own_weight_ref[s]) * columns[:, s : s + 1]
+        marks += [pltpu.roll(cover[s : s + 1], LANES // 2, 1), cover[s : s + 1]]
+    marks = jnp.concatenate(marks + [jnp.zeros((8 - 2 * held, cols), F32)], axis=0)
+    lane = lax.broadcasted_iota(jnp.int32, (8, LANES), 1)
+    for peer in range(devices):
+        block = jnp.where(lane < held * width, own[peer * 8 : peer * 8 + 8], marks)
+        out_ref[peer, held * width :, :] = block.astype(BF16)
+
+
+def project(pair_tile, weight_ref, mask_ref, out_ref, gate_ref, first, devices):
+    cols = pair_tile.shape[1] // 2
+    both = 2 * pair_tile.shape[0]
+    normalized = norm(pair_tile, 0)
+    mask = jnp.concatenate([mask_ref[first : first + 1], mask_ref[first + 1 : first + 2]], axis=1)
+    gates = sigmoid(dot(weight_ref[0:both], normalized))
+    values = dot(weight_ref[both : 2 * both], normalized)
+    sides = (gates * values * mask).astype(BF16)
+    gate_ref[:, first * cols : (first + 2) * cols] = sigmoid(dot(weight_ref[2 * both :], normalized))
+    share = both // devices
+    for peer in range(devices):
+        for row in range(2):
+            at = (first + row) * share
+            out_ref[peer, at : at + share, :] = sides[peer * share : (peer + 1) * share, row * cols : (row + 1) * cols]
+
+
+def outer_kernel(
+    place_ref, got_ref, couple_ref, exit_ref, weight_ref, mask_ref,
+    out_ref, pair_ref, gate_ref, shared_ref, aux_ref, outer_ref,
+):
+    devices, _, cols = got_ref.shape
+    channels = couple_ref.shape[0]
+    rows = mask_ref.shape[0]
+    held, width = 2, 32
+    shared_ref[...] = got_ref[:, : held * width, :].astype(F32).reshape(devices * held * width, cols)
+    aux_ref[...] = got_ref[:, held * width :, :].astype(F32).reshape(devices * 8, cols)
+    lane = lax.broadcasted_iota(jnp.int32, (devices, LANES), 1)
+    cover = []
+    for s in range(held):
+        low = aux_ref[pl.ds(2 * s, devices, stride=8), :]
+        high = aux_ref[pl.ds(2 * s + 1, devices, stride=8), :]
+        cover.append(jnp.where(lane < LANES // 2, pltpu.roll(low, LANES // 2, 1), high))
+    cover = jnp.concatenate(cover, axis=0).astype(BF16)
+    chosen = lax.broadcasted_iota(jnp.int32, (rows, LANES), 1) == (
+        lax.broadcasted_iota(jnp.int32, (rows, LANES), 0) + place_ref[0] * rows
+    )
+    cover_rows = dot(chosen.astype(BF16), cover, 1, 1).astype(BF16)
+    scale = 1.0 / dot(cover_rows, cover)
+    per_tile = LANES // width
+    tiles = []
+    for tile in range(rows // per_tile):
+        sides = [jnp.zeros((devices, LANES), F32) for _ in range(held)]
+        for place in range(per_tile):
+            values = aux_ref[pl.ds(tile * per_tile + place, devices, stride=8), :]
+            here = (lane >= place * width) & (lane < (place + 1) * width)
+            for s in range(held):
+                turn = ((place - s) * width) % LANES
+                turned = pltpu.roll(values, turn, 1) if turn else values
+                sides[s] = jnp.where(here, turned, sides[s])
+        tiles.append(jnp.concatenate(sides, axis=0))
+    own = jnp.transpose(jnp.concatenate(tiles, axis=1)).astype(BF16)
+    for e in range(0, width, 2):
+        parts = []
+        for step in range(2):
+            parts.append(
+                jnp.concatenate(
+                    [
+                        shared_ref[pl.ds(s * width + e + step, devices, stride=held * width), :]
+                        for s in range(held)
+                    ],
+                    axis=0,
+                )
+            )
+        result = dot(own, jnp.concatenate(parts, axis=1).astype(BF16)).astype(BF16)
+        for step in range(2):
+            for i in range(rows):
+                outer_ref[(e + step) * width : (e + step + 1) * width, i * cols : (i + 1) * cols] = result[
+                    i * width : (i + 1) * width, step * cols : (step + 1) * cols
+                ]
+    for first in range(0, rows, 2):
+        at = slice(first * cols, (first + 2) * cols)
+        update = dot(exit_ref[...], outer_ref[:, at])
+        per_pair = jnp.concatenate([scale[first : first + 1], scale[first + 1 : first + 2]], axis=1)
+        pair = (couple_ref[:, at].astype(F32) + update * per_pair).astype(BF16)
+        pair_ref[:, at] = pair
+        project(pair.astype(F32), weight_ref, mask_ref, out_ref, gate_ref, first, devices)
+
+
+def product_kernel(incoming, got_ref, out_ref, sides_ref, products_ref):
+    devices, _, cols = got_ref.shape
+    part = 8
+    total = sides_ref.shape[0] // (2 * part)
+    sides_ref[...] = got_ref[...].astype(F32).reshape(total * 2 * part, cols)
+    for h in range(part):
+        left = sides_ref[pl.ds(h, total, stride=2 * part), :].astype(BF16)
+        right = sides_ref[pl.ds(part + h, total, stride=2 * part), :].astype(BF16)
+        result = dot(left, right, 0, 0) if incoming else dot(left, right, 1, 1)
+        products_ref[pl.ds(h, total, stride=part), :] = result
+    out_ref[...] = products_ref[...].astype(BF16).reshape(out_ref.shape)
+
+
+def updated(got_ref, pair_ref, gate_ref, exit_ref, first):
+    devices, _, cols = got_ref.shape
+    part = 8
+    channels = devices * part
+    got = got_ref[:, first * part : (first + 2) * part, :].astype(F32)
+    products = jnp.concatenate(
+        [got[:, :part].reshape(channels, cols), got[:, part:].reshape(channels, cols)], axis=1
+    )
+    at = slice(first * cols, (first + 2) * cols)
+    update = dot(exit_ref[...], norm(products, 0))
+    return pair_ref[:, at].astype(F32) + gate_ref[:, at] * update
+
+
+def middle_kernel(got_ref, pair_ref, gate_ref, exit_ref, weight_ref, mask_ref, out_ref, next_ref, next_gate_ref):
+    devices, _, cols = got_ref.shape
+    for first in range(0, mask_ref.shape[0], 2):
+        pair = updated(got_ref, pair_ref, gate_ref, exit_ref, first).astype(BF16)
+        next_ref[:, first * cols : (first + 2) * cols] = pair
+        project(pair.astype(F32), weight_ref, mask_ref, out_ref, next_gate_ref, first, devices)
+
+
+def last_kernel(got_ref, pair_ref, gate_ref, exit_ref, out_ref):
+    rows, cols, _ = out_ref.shape
+    for first in range(0, rows, 2):
+        pair = updated(got_ref, pair_ref, gate_ref, exit_ref, first)
+        for row in range(2):
+            out_ref[first + row] = jnp.transpose(pair[:, row * cols : (row + 1) * cols]).astype(BF16)
+
+
+def call(kernel, inputs, outputs, scratch=(), in_specs=None):
+    return pl.pallas_call(
+        kernel,
+        out_shape=outputs,
+        in_specs=in_specs or [VMEM] * len(inputs),
+        out_specs=[VMEM] * len(outputs),
+        scratch_shapes=list(scratch),
+        compiler_params=PARAMS,
+    )(*inputs)
+
+
+def shape(dims, kind=BF16):
+    return jax.ShapeDtypeStruct(dims, kind)
+
+
+def fast(
+    devices,
+    homolog_embedding,
+    coverage_indicator,
+    genuine_amino_flag,
+    couple_embedding,
+    pairing_entry_matrices,
+    pairing_exit_matrix,
+    trilateral_entry_matrices,
+    trilateral_exit_matrices,
+):
+    rows, cols, channels = couple_embedding.shape
+    held = homolog_embedding.shape[0]
+    width = pairing_entry_matrices.shape[2]
+    part = channels // devices
+    blank = jnp.zeros_like(pairing_entry_matrices[:, 0])
+    own_weight = jnp.stack(
+        [
+            jnp.concatenate([pairing_entry_matrices[:, 0] if at == s else blank for at in range(LANES // width)], axis=1)
+            for s in range(held)
+        ]
+    )
+    shared_weight = jnp.transpose(pairing_entry_matrices[:, 1])
+    (packed,) = call(
+        entry_kernel,
+        (homolog_embedding, coverage_indicator, own_weight, shared_weight),
+        [shape((devices, held * width + 8, cols))],
+    )
+    packed, entry, leave, exit_weight, couple, residues = lax.optimization_barrier(
+        (
+            packed,
+            trilateral_entry_matrices,
+            trilateral_exit_matrices,
+            pairing_exit_matrix,
+            couple_embedding,
+            genuine_amino_flag,
+        )
+    )
+    got = exchange(packed)
+    place = lax.axis_index("dap")
+    residues = residues.astype(F32)
+    row_mask = lax.dynamic_slice_in_dim(residues, place * rows, rows, 0)[:, None] * residues[None, :]
+    sides = entry[:, :, :4].reshape(2, channels, 2, 2, devices, part)
+    sides = jnp.transpose(sides, (0, 3, 4, 2, 5, 1)).reshape(2, 4 * channels, channels)
+    entry = jnp.concatenate([sides, jnp.transpose(entry[:, :, 4], (0, 2, 1))], axis=1)
+    leave = jnp.transpose(leave, (0, 2, 1))
+    exit_weight = jnp.transpose(exit_weight.reshape(width, width, channels), (2, 1, 0)).reshape(channels, width * width)
+    couple = jnp.transpose(couple, (2, 0, 1)).reshape(channels, rows * cols)
+
+    projected = [
+        shape((devices, rows * 2 * part, cols)),
+        shape((channels, rows * cols)),
+        shape((channels, rows * cols), F32),
+    ]
+    both, pair, gate = call(
+        outer_kernel,
+        (place.astype(jnp.int32).reshape(1), got, couple, exit_weight, entry[0], row_mask),
+        projected,
+        [
+            pltpu.VMEM((devices * held * width, cols), F32),
+            pltpu.VMEM((devices * 8, cols), F32),
+            pltpu.VMEM((width * width, rows * cols), BF16),
+        ],
+        [SMEM] + [VMEM] * 5,
+    )
+
+    def multiply(both, incoming):
+        (products,) = call(
+            functools.partial(product_kernel, incoming),
+            (exchange(both),),
+            [shape((devices, rows * part, cols))],
+            [pltpu.VMEM((devices * rows * 2 * part, cols), F32), pltpu.VMEM((devices * rows * part, cols), F32)],
+        )
+        return exchange(products)
+
+    got = multiply(both, False)
+    both, pair, gate = call(middle_kernel, (got, pair, gate, leave[0], entry[1], row_mask), projected)
+    got = multiply(both, True)
+    (pair_out,) = call(last_kernel, (got, pair, gate, leave[1]), [shape((rows, cols, channels))])
+    return pair_out
+
+
+def fits(devices, homolog_embedding, couple_embedding, pairing_entry_matrices):
+    rows, cols, channels = couple_embedding.shape
+    return (
+        homolog_embedding.shape[0] == 2
+        and rows == 8
+        and cols == LANES
+        and channels == 8 * devices
+        and channels == LANES
+        and pairing_entry_matrices.shape[2] == 32
+    )
+
+
 def solution(mesh):
     devices = mesh.shape["dap"]
+
+    def one_device(*arrays):
+        chosen = fast if fits(devices, arrays[0], arrays[3], arrays[4]) else local
+        return chosen(devices, *arrays)
+
     return jax.shard_map(
-        lambda *arrays: local(devices, *arrays),
+        one_device,
         mesh=mesh,
         in_specs=(
             P(("crops", "dap"), None, None),

time: 97.8 us -> 91.7 us (0.938)
  blocking collectives: 34.6 us -> 48.6 us
  waiting for transfers between devices: 29.3 us -> 17.8 us
  Pallas kernels: 0 us -> 8.18 us
  other arithmetic: 6.73 us -> 0.21 us
  matrix products: 5.27 us -> 0 us
  starting transfers between devices: 15.7 us -> 11.7 us
    all_to_all x2 -> x3, blocking collectives: 34.6 us -> 48.6 us  [exchange(): lax.all_to_all(blocks, 'dap', split_axis=0, concat_axis=0, tiled=True)]
    all_to_all x3 -> x2, waiting for transfers between devices: 29.3 us -> 17.8 us  [exchange(): lax.all_to_all(blocks, 'dap', split_axis=0, concat_axis=0, tiled=True)]
    pallas_call x0 -> x6, Pallas kernels: none -> 8.18 us  [call(): pl.pallas_call(kernel, out_shape=outputs, in_specs=in_specs or [VMEM] * l...]
    dot_general x12 -> x0, matrix products: 5.27 us -> none  [the longest x1 1.16 us: local(): jnp.einsum('rgl,loe->roeg', msa_norm, pairing_entry_matrices, preferred_e...]
    all_to_all x3 -> x2, starting transfers between devices: 15.7 us -> 11.7 us  [exchange(): lax.all_to_all(blocks, 'dap', split_axis=0, concat_axis=0, tiled=True)]
    reduce_sum x8 -> x0, other arithmetic: 2.86 us -> none  [the longest x5 1.5 us: standardize_features(): variance = jnp.mean(centered * centered, axis=axis, keepdims=True)]
    convert_element_type x2 -> x0, local copies, waits for them, and re-layouts: 2.2 us -> none  [the longest x1 1.35 us: outer_update(): outer.astype(jnp.bfloat16)]
    convert_element_type x6 -> x1, other arithmetic: 2.09 us -> 0.01 us  [fast(): residues = residues.astype(F32)]
  transfers between devices with their start and end apart: 3 -> 2, of which waited for: 3 -> 2; matrix products, arithmetic and copies ran while one was open for 1% -> 1% of each run, Pallas kernels for 0% -> 0%
where the time goes in v2:
time: 91.7 us; the launch traced here: 91.1 us
  blocking collectives  48.6 us (53%)
  waiting for transfers between devices  17.8 us (19%)
  starting transfers between devices  11.7 us (13%)
  Pallas kernels  8.18 us (9%)
  local copies, waits for them, and re-layouts  4.44 us (5%)
    all_to_all x3, blocking collectives, exchange(): lax.all_to_all(blocks, 'dap', split_axis=0, concat_axis=0, tiled=True)  48.6 us
    all_to_all x2, waiting for transfers between devices, exchange(): lax.all_to_all(blocks, 'dap', split_axis=0, concat_axis=0, tiled=True)  17.8 us
    all_to_all x2, starting transfers between devices, exchange(): lax.all_to_all(blocks, 'dap', split_axis=0, concat_axis=0, tiled=True)  11.7 us
    pallas_call x6, Pallas kernels, call(): pl.pallas_call(kernel, out_shape=outputs, in_specs=in_specs or [VMEM] * l...  8.18 us
    unnamed x15, local copies, waits for them, and re-layouts  2.51 us
  transfers between devices with their start and end apart: 2, of which 2 were waited for; matrix products, arithmetic and copies ran while one was open for 1% of the time, Pallas kernels for 0%

profile of v2, /device:TPU:0, one launch (start us, length us, event | category | flops | bytes accessed | tf_op | source)
XLA Modules:
  0.0 91.1 jit_solution(17864426100785760743)
XLA Ops:
  0.0 0.1 pad.7.clone
  0.1 0.7 slice_bitcast_fusion.3
  0.8 0.1 copy.31
  1.0 0.1 pad_bitcast_fusion
  1.1 0.0 copy-start
  1.1 0.0 copy-start.1
  1.1 0.9 copy-done
  2.0 1.1 %shard_map.82 = bf16[16,72,128]{2,1,0:T(8,128)(2,1)} custom-call(bf16[2,128,256]{2,1,0:T(8,128)(2,1)S(1)} %copy-done, s32[2,128]{1,0:T(2,128)S(1)} %copy-done.1, bf16[2,256,128]{2,1,0:T(8,128)(2,1)S(1)} %pad_maximum_fusion.1.own_weight_ref, bf16[32,256]{1,0:T(8,128)(2,1)S(1)} %get-tuple-element.35.shared_weight_ref), custom_call_target="tpu_custom_call" | custom-call | tf_op jit(solution)/shard_map/pallas_call | solution.py:262
  3.1 7.5 %all-to-all-start = ((bf16[16,72,128]{2,1,0:T(8,128)(2,1)}), bf16[16,72,128]{2,1,0:T(8,128)(2,1)S(1)}, u32[]{:S(2)}, u32[]{:S(2)}) async-start(bf16[16,72,128]{2,1,0:T(8,128)(2,1)} %shard_map.82), calls=%async_computation | async-start | bytes 589824 | tf_op jit(solution)/shard_map/all_to_all | solution.py:43
  10.7 0.2 copy.27
  10.9 0.2 copy.25
  11.1 0.0 copy-start.6
  11.1 0.6 copy-done.6
  11.8 0.1 copy-done.3
  11.8 0.1 copy.30.couple_ref
  12.0 0.8 copy-done.4
  12.8 0.1 copy.24
  12.9 0.1 copy.28.exit_ref
  13.1 0.1 dynamic_slice.3
  13.2 0.1 broadcast_multiply_fusion.mask_ref
  13.3 7.9 %all-to-all-done.got_ref = bf16[16,72,128]{2,1,0:T(8,128)(2,1)S(1)} async-done(((bf16[16,72,128]{2,1,0:T(8,128)(2,1)}), bf16[16,72,128]{2,1,0:T(8,128)(2,1)S(1)}, u32[]{:S(2)}, u32[]{:S(2)}) %all-to-all-start) | async-done | bytes 294944 | tf_op jit(solution)/shard_map/all_to_all | solution.py:43
  21.2 2.7 %shard_map.83 = (bf16[16,128,128]{2,1,0:T(8,128)(2,1)S(1)}, bf16[128,1024]{1,0:T(8,128)(2,1)S(1)}, f32[128,1024]{1,0:T(8,128)S(1)}) custom-call(s32[1]{0:T(128)} %bitcast.place_ref, bf16[16,72,128]{2,1,0:T(8,128)(2,1)S(1)} %all-to-all-done.got_ref, bf16[128,1024]{1,0:T(8,128)(2,1)S(1)} %copy.30.couple_ref, bf16[128,1024]{1,0:T(8,128)(2,1)S(1)} %copy.28.exit_ref, ...), custom_call_target="tpu_custom_call" | custom-call | tf_op jit(solution)/shard_map/pallas_call | solution.py:262
  24.0 17.4 %all_to_all.25.got_ref = bf16[16,128,128]{2,1,0:T(8,128)(2,1)S(1)} all-to-all(bf16[16,128,128]{2,1,0:T(8,128)(2,1)S(1)} %get-tuple-element.22), channel_id=1, replica_groups=mesh['crops'=2,'dap'=16] {'dap'}, dimensions={0} | all-to-all | bytes 1048576 | tf_op jit(solution)/shard_map/all_to_all | solution.py:43
  41.4 1.2 %shard_map.84 = bf16[16,64,128]{2,1,0:T(8,128)(2,1)} custom-call(bf16[16,128,128]{2,1,0:T(8,128)(2,1)S(1)} %all_to_all.25.got_ref), custom_call_target="tpu_custom_call" | custom-call | tf_op jit(solution)/shard_map/pallas_call | solution.py:262
  42.5 4.2 %all-to-all-start.2 = ((bf16[16,64,128]{2,1,0:T(8,128)(2,1)}), bf16[16,64,128]{2,1,0:T(8,128)(2,1)S(1)}, u32[]{:S(2)}, u32[]{:S(2)}) async-start(bf16[16,64,128]{2,1,0:T(8,128)(2,1)} %shard_map.84), calls=%async_computation.2 | async-start | bytes 524288 | tf_op jit(solution)/shard_map/all_to_all | solution.py:43
  46.8 0.1 copy.29
  46.9 9.9 %all-to-all-done.2.got_ref = bf16[16,64,128]{2,1,0:T(8,128)(2,1)S(1)} async-done(((bf16[16,64,128]{2,1,0:T(8,128)(2,1)}), bf16[16,64,128]{2,1,0:T(8,128)(2,1)S(1)}, u32[]{:S(2)}, u32[]{:S(2)}) %all-to-all-start.2) | async-done | bytes 262176 | tf_op jit(solution)/shard_map/all_to_all | solution.py:43
  56.8 1.5 %shard_map.85 = (bf16[16,128,128]{2,1,0:T(8,128)(2,1)S(1)}, bf16[128,1024]{1,0:T(8,128)(2,1)S(1)}, f32[128,1024]{1,0:T(8,128)S(1)}) custom-call(bf16[16,64,128]{2,1,0:T(8,128)(2,1)S(1)} %all-to-all-done.2.got_ref, bf16[128,1024]{1,0:T(8,128)(2,1)S(1)} %get-tuple-element.23.pair_ref, f32[128,1024]{1,0:T(8,128)S(1)} %get-tuple-element.24.gate_ref, ...), custom_call_target="tpu_custom_call" | custom-call | tf_op jit(solution)/shard_map/pallas_call | solution.py:262
  58.3 17.2 %all_to_all.26.got_ref = bf16[16,128,128]{2,1,0:T(8,128)(2,1)S(1)} all-to-all(bf16[16,128,128]{2,1,0:T(8,128)(2,1)S(1)} %get-tuple-element.26), channel_id=1, replica_groups=mesh['crops'=2,'dap'=16] {'dap'}, dimensions={0} | all-to-all | bytes 1048576 | tf_op jit(solution)/shard_map/all_to_all | solution.py:43
  75.5 0.5 shard_map.86
  76.1 13.9 %all_to_all.27.got_ref = bf16[16,64,128]{2,1,0:T(8,128)(2,1)S(1)} all-to-all(bf16[16,64,128]{2,1,0:T(8,128)(2,1)S(1)} %shard_map.86), channel_id=1, replica_groups=mesh['crops'=2,'dap'=16] {'dap'}, dimensions={0} | all-to-all | bytes 524288 | tf_op jit(solution)/shard_map/all_to_all | solution.py:43
  90.0 1.1 %shard_map.87 = bf16[8,128,128]{2,1,0:T(8,128)(2,1)} custom-call(bf16[16,64,128]{2,1,0:T(8,128)(2,1)S(1)} %all_to_all.27.got_ref, bf16[128,1024]{1,0:T(8,128)(2,1)S(1)} %get-tuple-element.27.pair_ref, f32[128,1024]{1,0:T(8,128)S(1)} %get-tuple-element.28.gate_ref, bf16[128,128]{1,0:T(8,128)(2,1)S(1)} %get-tuple-element.31.exit_ref), custom_call_target="tpu_custom_call" | custom-call | tf_op jit(solution)/shard_map/pallas_call | solution.py:262
  (17 shorter events, 0.1 us)
Async XLA Ops:
  1.1 0.9 copy-start
  1.1 0.9 copy-start.1
  3.1 7.5 %copy-start.2 = (bf16[2,128,5,128]{3,1,2,0:T(8,128)(2,1)S(1)}, bf16[2,128,5,128]{3,1,2,0:T(8,128)(2,1)}, u32[]{:S(2)}) copy-start(bf16[2,128,5,128]{3,1,2,0:T(8,128)(2,1)} %param.14) | copy-start | bytes 983044
  3.1 18.1 %all-to-all-start = ((bf16[16,72,128]{2,1,0:T(8,128)(2,1)}), bf16[16,72,128]{2,1,0:T(8,128)(2,1)S(1)}, u32[]{:S(2)}, u32[]{:S(2)}) async-start(bf16[16,72,128]{2,1,0:T(8,128)(2,1)} %shard_map.82), calls=%async_computation | async-start | bytes 589824 | tf_op jit(solution)/shard_map/all_to_all | solution.py:43
  10.9 1.0 %copy-start.3 = (bf16[8,128,128]{2,1,0:T(8,128)(2,1)S(1)}, bf16[8,128,128]{2,1,0:T(8,128)(2,1)}, u32[]{:S(2)}) copy-start(bf16[8,128,128]{2,1,0:T(8,128)(2,1)} %param.11) | copy-start | bytes 786436
  11.1 0.7 copy-start.6
  11.8 0.9 %copy-start.4 = (bf16[1024,128]{1,0:T(8,128)(2,1)S(1)}, bf16[1024,128]{1,0:T(8,128)(2,1)}, u32[]{:S(2)}) copy-start(bf16[1024,128]{1,0:T(8,128)(2,1)} %param.13) | copy-start | bytes 786436
  42.5 4.2 %copy-start.5 = (bf16[2,128,128]{2,1,0:T(8,128)(2,1)S(1)}, bf16[2,128,128]{2,1,0:T(8,128)(2,1)}, u32[]{:S(2)}) copy-start(bf16[2,128,128]{2,1,0:T(8,128)(2,1)} %param.15) | copy-start | bytes 196612
  42.5 14.3 %all-to-all-start.2 = ((bf16[16,64,128]{2,1,0:T(8,128)(2,1)}), bf16[16,64,128]{2,1,0:T(8,128)(2,1)S(1)}, u32[]{:S(2)}, u32[]{:S(2)}) async-start(bf16[16,64,128]{2,1,0:T(8,128)(2,1)} %shard_map.84), calls=%async_computation.2 | async-start | bytes 524288 | tf_op jit(solution)/shard_map/all_to_all | solution.py:43

commit v3 on v2

--- a/solution.py
+++ b/solution.py
@@ -116,20 +116,22 @@
     return triangle(pair_two, row_mask, trilateral_entry_matrices[1], trilateral_exit_matrices[1], True, devices)
 
 
-def entry_kernel(x_ref, cover_ref, own_weight_ref, shared_weight_ref, out_ref):
+def entry_kernel(x_ref, cover_ref, weight_ref, out_ref):
     held, cols, _ = x_ref.shape
-    width = shared_weight_ref.shape[0]
+    width = weight_ref.shape[1]
     devices = out_ref.shape[0]
     cover = cover_ref[...].astype(F32)
     columns = jnp.transpose(jnp.concatenate([cover, jnp.zeros((8 - held, cols), F32)], axis=0))
+    blank = jnp.zeros_like(weight_ref[0])
     own = jnp.zeros((cols, LANES), F32)
     marks = []
     for s in range(held):
         normalized = norm(x_ref[s].astype(F32), -1)
-        shared = (dot(shared_weight_ref[...], normalized, 1, 1) * cover[s : s + 1]).astype(BF16)
+        shared = (dot(weight_ref[1], normalized, 1, 1) * cover[s : s + 1]).astype(BF16)
         for peer in range(devices):
             out_ref[peer, s * width : (s + 1) * width, :] = shared
-        own = own + dot(normalized, own_weight_ref[s]) * columns[:, s : s + 1]
+        weight = jnp.concatenate([weight_ref[0] if at == s else blank for at in range(LANES // width)], axis=0)
+        own = own + dot(normalized, weight, 1, 1) * columns[:, s : s + 1]
         marks += [pltpu.roll(cover[s : s + 1], LANES // 2, 1), cover[s : s + 1]]
     marks = jnp.concatenate(marks + [jnp.zeros((8 - 2 * held, cols), F32)], axis=0)
     lane = lax.broadcasted_iota(jnp.int32, (8, LANES), 1)
@@ -138,29 +140,34 @@
         out_ref[peer, held * width :, :] = block.astype(BF16)
 
 
-def project(pair_tile, weight_ref, mask_ref, out_ref, gate_ref, first, devices):
+def project(pair_tile, weights, mask_ref, out_ref, gate_ref, first, devices):
     cols = pair_tile.shape[1] // 2
-    both = 2 * pair_tile.shape[0]
+    share = pair_tile.shape[0] // devices
     normalized = norm(pair_tile, 0)
     mask = jnp.concatenate([mask_ref[first : first + 1], mask_ref[first + 1 : first + 2]], axis=1)
-    gates = sigmoid(dot(weight_ref[0:both], normalized))
-    values = dot(weight_ref[both : 2 * both], normalized)
-    sides = (gates * values * mask).astype(BF16)
-    gate_ref[:, first * cols : (first + 2) * cols] = sigmoid(dot(weight_ref[2 * both :], normalized))
-    share = both // devices
+    left, right = (
+        sigmoid(dot(weights[k], normalized)) * dot(weights[k + 1], normalized) * mask for k in (0, 2)
+    )
+    gate_ref[:, first * cols : (first + 2) * cols] = sigmoid(dot(weights[4], normalized))
     for peer in range(devices):
         for row in range(2):
-            at = (first + row) * share
-            out_ref[peer, at : at + share, :] = sides[peer * share : (peer + 1) * share, row * cols : (row + 1) * cols]
+            block = [
+                side[peer * share : (peer + 1) * share, row * cols : (row + 1) * cols] for side in (left, right)
+            ]
+            at = (first + row) * 2 * share
+            out_ref[peer, at : at + 2 * share, :] = jnp.concatenate(block, axis=0).astype(BF16)
+
+
+def turned(weight_ref, t):
+    return [jnp.transpose(weight_ref[t, k]) for k in range(weight_ref.shape[1])]
 
 
 def outer_kernel(
-    place_ref, got_ref, couple_ref, exit_ref, weight_ref, mask_ref,
-    out_ref, pair_ref, gate_ref, shared_ref, aux_ref, outer_ref,
+    place_ref, got_ref, couple_ref, exit_ref, weight_ref, flag_ref,
+    out_ref, pair_ref, gate_ref, mask_ref, shared_ref, aux_ref, outer_ref,
 ):
     devices, _, cols = got_ref.shape
-    channels = couple_ref.shape[0]
-    rows = mask_ref.shape[0]
+    rows, _, channels = couple_ref.shape
     held, width = 2, 32
     shared_ref[...] = got_ref[:, : held * width, :].astype(F32).reshape(devices * held * width, cols)
     aux_ref[...] = got_ref[:, held * width :, :].astype(F32).reshape(devices * 8, cols)
@@ -176,6 +183,8 @@
     )
     cover_rows = dot(chosen.astype(BF16), cover, 1, 1).astype(BF16)
     scale = 1.0 / dot(cover_rows, cover)
+    flags = flag_ref[...].astype(F32)
+    mask_ref[...] = jnp.sum(jnp.where(chosen, flags, 0.0), axis=1, keepdims=True) * flags
     per_tile = LANES // width
     tiles = []
     for tile in range(rows // per_tile):
@@ -185,8 +194,8 @@
             here = (lane >= place * width) & (lane < (place + 1) * width)
             for s in range(held):
                 turn = ((place - s) * width) % LANES
-                turned = pltpu.roll(values, turn, 1) if turn else values
-                sides[s] = jnp.where(here, turned, sides[s])
+                moved = pltpu.roll(values, turn, 1) if turn else values
+                sides[s] = jnp.where(here, moved, sides[s])
         tiles.append(jnp.concatenate(sides, axis=0))
     own = jnp.transpose(jnp.concatenate(tiles, axis=1)).astype(BF16)
     for e in range(0, width, 2):
@@ -207,13 +216,18 @@
                 outer_ref[(e + step) * width : (e + step + 1) * width, i * cols : (i + 1) * cols] = result[
                     i * width : (i + 1) * width, step * cols : (step + 1) * cols
                 ]
+    shared_ref[...] = exit_ref[...].astype(F32)
+    leave = jnp.concatenate([shared_ref[pl.ds(e, width, stride=width), :] for e in range(width)], axis=0)
+    leave = jnp.transpose(leave.astype(BF16))
+    weights = turned(weight_ref, 0)
     for first in range(0, rows, 2):
         at = slice(first * cols, (first + 2) * cols)
-        update = dot(exit_ref[...], outer_ref[:, at])
+        update = dot(leave, outer_ref[:, at])
         per_pair = jnp.concatenate([scale[first : first + 1], scale[first + 1 : first + 2]], axis=1)
-        pair = (couple_ref[:, at].astype(F32) + update * per_pair).astype(BF16)
+        couple = jnp.concatenate([jnp.transpose(couple_ref[first + row].astype(F32)) for row in range(2)], axis=1)
+        pair = (couple + update * per_pair).astype(BF16)
         pair_ref[:, at] = pair
-        project(pair.astype(F32), weight_ref, mask_ref, out_ref, gate_ref, first, devices)
+        project(pair.astype(F32), weights, mask_ref, out_ref, gate_ref, first, devices)
 
 
 def product_kernel(incoming, got_ref, out_ref, sides_ref, products_ref):
@@ -229,7 +243,7 @@
     out_ref[...] = products_ref[...].astype(BF16).reshape(out_ref.shape)
 
 
-def updated(got_ref, pair_ref, gate_ref, exit_ref, first):
+def updated(got_ref, pair_ref, gate_ref, leave, first):
     devices, _, cols = got_ref.shape
     part = 8
     channels = devices * part
@@ -238,22 +252,25 @@
         [got[:, :part].reshape(channels, cols), got[:, part:].reshape(channels, cols)], axis=1
     )
     at = slice(first * cols, (first + 2) * cols)
-    update = dot(exit_ref[...], norm(products, 0))
+    update = dot(leave, norm(products, 0))
     return pair_ref[:, at].astype(F32) + gate_ref[:, at] * update
 
 
-def middle_kernel(got_ref, pair_ref, gate_ref, exit_ref, weight_ref, mask_ref, out_ref, next_ref, next_gate_ref):
+def middle_kernel(got_ref, pair_ref, gate_ref, leave_ref, weight_ref, mask_ref, out_ref, next_ref, next_gate_ref):
     devices, _, cols = got_ref.shape
+    leave = jnp.transpose(leave_ref[0])
+    weights = turned(weight_ref, 1)
     for first in range(0, mask_ref.shape[0], 2):
-        pair = updated(got_ref, pair_ref, gate_ref, exit_ref, first).astype(BF16)
+        pair = updated(got_ref, pair_ref, gate_ref, leave, first).astype(BF16)
         next_ref[:, first * cols : (first + 2) * cols] = pair
-        project(pair.astype(F32), weight_ref, mask_ref, out_ref, next_gate_ref, first, devices)
-
-
-def last_kernel(got_ref, pair_ref, gate_ref, exit_ref, out_ref):
+        project(pair.astype(F32), weights, mask_ref, out_ref, next_gate_ref, first, devices)
+
+
+def last_kernel(got_ref, pair_ref, gate_ref, leave_ref, out_ref):
     rows, cols, _ = out_ref.shape
+    leave = jnp.transpose(leave_ref[1])
     for first in range(0, rows, 2):
-        pair = updated(got_ref, pair_ref, gate_ref, exit_ref, first)
+        pair = updated(got_ref, pair_ref, gate_ref, leave, first)
         for row in range(2):
             out_ref[first + row] = jnp.transpose(pair[:, row * cols : (row + 1) * cols]).astype(BF16)
 
@@ -288,49 +305,29 @@
     held = homolog_embedding.shape[0]
     width = pairing_entry_matrices.shape[2]
     part = channels // devices
-    blank = jnp.zeros_like(pairing_entry_matrices[:, 0])
-    own_weight = jnp.stack(
-        [
-            jnp.concatenate([pairing_entry_matrices[:, 0] if at == s else blank for at in range(LANES // width)], axis=1)
-            for s in range(held)
-        ]
-    )
-    shared_weight = jnp.transpose(pairing_entry_matrices[:, 1])
     (packed,) = call(
         entry_kernel,
-        (homolog_embedding, coverage_indicator, own_weight, shared_weight),
+        (homolog_embedding, coverage_indicator, jnp.transpose(pairing_entry_matrices, (1, 2, 0))),
         [shape((devices, held * width + 8, cols))],
     )
-    packed, entry, leave, exit_weight, couple, residues = lax.optimization_barrier(
-        (
-            packed,
-            trilateral_entry_matrices,
-            trilateral_exit_matrices,
-            pairing_exit_matrix,
-            couple_embedding,
-            genuine_amino_flag,
-        )
-    )
-    got = exchange(packed)
-    place = lax.axis_index("dap")
-    residues = residues.astype(F32)
-    row_mask = lax.dynamic_slice_in_dim(residues, place * rows, rows, 0)[:, None] * residues[None, :]
-    sides = entry[:, :, :4].reshape(2, channels, 2, 2, devices, part)
-    sides = jnp.transpose(sides, (0, 3, 4, 2, 5, 1)).reshape(2, 4 * channels, channels)
-    entry = jnp.concatenate([sides, jnp.transpose(entry[:, :, 4], (0, 2, 1))], axis=1)
-    leave = jnp.transpose(leave, (0, 2, 1))
-    exit_weight = jnp.transpose(exit_weight.reshape(width, width, channels), (2, 1, 0)).reshape(channels, width * width)
-    couple = jnp.transpose(couple, (2, 0, 1)).reshape(channels, rows * cols)
-
+    entry = jnp.transpose(trilateral_entry_matrices, (0, 2, 1, 3))
+    leave = trilateral_exit_matrices
     projected = [
         shape((devices, rows * 2 * part, cols)),
         shape((channels, rows * cols)),
         shape((channels, rows * cols), F32),
     ]
-    both, pair, gate = call(
+    both, pair, gate, row_mask = call(
         outer_kernel,
-        (place.astype(jnp.int32).reshape(1), got, couple, exit_weight, entry[0], row_mask),
-        projected,
+        (
+            lax.axis_index("dap").astype(jnp.int32).reshape(1),
+            exchange(packed),
+            couple_embedding,
+            pairing_exit_matrix,
+            entry,
+            genuine_amino_flag.reshape(1, cols),
+        ),
+        projected + [shape((rows, cols), F32)],
         [
             pltpu.VMEM((devices * held * width, cols), F32),
             pltpu.VMEM((devices * 8, cols), F32),
@@ -349,9 +346,9 @@
         return exchange(products)
 
     got = multiply(both, False)
-    both, pair, gate = call(middle_kernel, (got, pair, gate, leave[0], entry[1], row_mask), projected)
+    both, pair, gate = call(middle_kernel, (got, pair, gate, leave, entry, row_mask), projected)
     got = multiply(both, True)
-    (pair_out,) = call(last_kernel, (got, pair, gate, leave[1]), [shape((rows, cols, channels))])
+    (pair_out,) = call(last_kernel, (got, pair, gate, leave), [shape((rows, cols, channels))])
     return pair_out
 
 

time: 91.7 us -> 92.1 us (level)
  blocking collectives: 48.6 us -> 62.6 us
  waiting for transfers between devices: 17.8 us -> 10.6 us
  starting transfers between devices: 11.7 us -> 7.52 us
  local copies, waits for them, and re-layouts: 4.44 us -> 3 us
    all_to_all x3 -> x4, blocking collectives: 48.6 us -> 62.6 us  [exchange(): lax.all_to_all(blocks, 'dap', split_axis=0, concat_axis=0, tiled=True)]
    all_to_all x2 -> x1, waiting for transfers between devices: 17.8 us -> 10.6 us  [exchange(): lax.all_to_all(blocks, 'dap', split_axis=0, concat_axis=0, tiled=True)]
    all_to_all x2 -> x1, starting transfers between devices: 11.7 us -> 7.52 us  [exchange(): lax.all_to_all(blocks, 'dap', split_axis=0, concat_axis=0, tiled=True)]
    unnamed x15 -> x16, local copies, waits for them, and re-layouts: 2.51 us -> 3 us
  transfers between devices with their start and end apart: 2 -> 1, of which waited for: 2 -> 1; matrix products, arithmetic and copies ran while one was open for 1% -> 0% of each run, Pallas kernels for 0% -> 0%
where the time goes in v3:
time: 92.1 us; the launch traced here: 91.6 us
  blocking collectives  62.6 us (68%)
  waiting for transfers between devices  10.6 us (12%)
  Pallas kernels  7.76 us (8%)
  starting transfers between devices  7.52 us (8%)
  local copies, waits for them, and re-layouts  3 us (3%)
    all_to_all x4, blocking collectives, exchange(): lax.all_to_all(blocks, 'dap', split_axis=0, concat_axis=0, tiled=True)  62.6 us
    all_to_all x1, waiting for transfers between devices, exchange(): lax.all_to_all(blocks, 'dap', split_axis=0, concat_axis=0, tiled=True)  10.6 us
    pallas_call x6, Pallas kernels, call(): pl.pallas_call(kernel, out_shape=outputs, in_specs=in_specs or [VMEM] * l...  7.76 us
    all_to_all x1, starting transfers between devices, exchange(): lax.all_to_all(blocks, 'dap', split_axis=0, concat_axis=0, tiled=True)  7.52 us
    unnamed x16, local copies, waits for them, and re-layouts  3 us
  transfers between devices with their start and end apart: 1, of which 1 were waited for; matrix products, arithmetic and copies ran while one was open for 0% of the time, Pallas kernels for 0%

profile of v3, /device:TPU:0, one launch (start us, length us, event | category | flops | bytes accessed | tf_op | source)
XLA Modules:
  0.0 91.6 jit_solution(453587709443992422)
XLA Ops:
  0.0 0.0 copy-start.6
  0.0 0.7 copy-done.6
  0.7 0.0 copy-start.4
  0.7 0.9 copy-done.4
  1.6 0.0 copy-start.5
  1.6 0.8 copy-done.5
  2.3 0.0 copy-start.2
  2.3 1.1 %shard_map.82 = bf16[16,72,128]{2,1,0:T(8,128)(2,1)} custom-call(bf16[2,128,256]{2,1,0:T(8,128)(2,1)S(1)} %copy-done.4, s32[2,128]{1,0:T(2,128)S(1)} %copy-done.6, bf16[2,32,256]{2,1,0:T(8,128)(2,1)S(1)} %bitcast.6), custom_call_target="tpu_custom_call" | custom-call | tf_op jit(solution)/shard_map/pallas_call | solution.py:279
  3.5 0.0 copy-start
  3.5 0.0 copy-start.1
  3.5 7.5 %all-to-all-start = ((bf16[16,72,128]{2,1,0:T(8,128)(2,1)}), bf16[16,72,128]{2,1,0:T(8,128)(2,1)S(1)}, u32[]{:S(2)}, u32[]{:S(2)}) async-start(bf16[16,72,128]{2,1,0:T(8,128)(2,1)} %shard_map.82), calls=%async_computation | async-start | bytes 589824 | tf_op jit(solution)/shard_map/all_to_all | solution.py:43
  11.0 10.6 %all-to-all-done.got_ref = bf16[16,72,128]{2,1,0:T(8,128)(2,1)S(1)} async-done(((bf16[16,72,128]{2,1,0:T(8,128)(2,1)}), bf16[16,72,128]{2,1,0:T(8,128)(2,1)S(1)}, u32[]{:S(2)}, u32[]{:S(2)}) %all-to-all-start) | async-done | bytes 294944 | tf_op jit(solution)/shard_map/all_to_all | solution.py:43
  21.6 0.0 copy-start.7
  21.6 0.0 copy-done.2
  21.6 0.0 copy-done
  21.6 0.0 copy-done.1
  21.6 0.6 copy-done.7
  22.2 3.1 %shard_map.83 = (bf16[16,128,128]{2,1,0:T(8,128)(2,1)S(1)}, bf16[128,1024]{1,0:T(8,128)(2,1)S(1)}, f32[128,1024]{1,0:T(8,128)S(1)}, f32[8,128]{1,0:T(8,128)S(1)}) custom-call(s32[1]{0:T(128)} %bitcast.place_ref, bf16[16,72,128]{2,1,0:T(8,128)(2,1)S(1)} %all-to-all-done.got_ref, bf16[8,128,128]{2,1,0:T(8,128)(2,1)S(1)} %copy-done.1, ...), custom_call_target="tpu_custom_call" | custom-call | tf_op jit(solution)/shard_map/pallas_call | solution.py:279
  25.3 17.4 %all_to_all.25.got_ref = bf16[16,128,128]{2,1,0:T(8,128)(2,1)S(1)} all-to-all(bf16[16,128,128]{2,1,0:T(8,128)(2,1)S(1)} %get-tuple-element.12), channel_id=1, replica_groups=mesh['crops'=2,'dap'=16] {'dap'}, dimensions={0} | all-to-all | bytes 1048576 | tf_op jit(solution)/shard_map/all_to_all | solution.py:43
  42.7 0.5 shard_map.84
  43.1 0.0 copy-start.3
  43.2 14.1 %all_to_all.26.got_ref = bf16[16,64,128]{2,1,0:T(8,128)(2,1)S(1)} all-to-all(bf16[16,64,128]{2,1,0:T(8,128)(2,1)S(1)} %shard_map.84), channel_id=1, replica_groups=mesh['crops'=2,'dap'=16] {'dap'}, dimensions={0} | all-to-all | bytes 524288 | tf_op jit(solution)/shard_map/all_to_all | solution.py:43
  57.2 0.0 copy-done.3
  57.2 1.5 %shard_map.85 = (bf16[16,128,128]{2,1,0:T(8,128)(2,1)S(1)}, bf16[128,1024]{1,0:T(8,128)(2,1)S(1)}, f32[128,1024]{1,0:T(8,128)S(1)}) custom-call(bf16[16,64,128]{2,1,0:T(8,128)(2,1)S(1)} %all_to_all.26.got_ref, bf16[128,1024]{1,0:T(8,128)(2,1)S(1)} %get-tuple-element.13.pair_ref, f32[128,1024]{1,0:T(8,128)S(1)} %get-tuple-element.14.gate_ref, ...), custom_call_target="tpu_custom_call" | custom-call | tf_op jit(solution)/shard_map/pallas_call | solution.py:279
  58.7 17.2 %all_to_all.27.got_ref = bf16[16,128,128]{2,1,0:T(8,128)(2,1)S(1)} all-to-all(bf16[16,128,128]{2,1,0:T(8,128)(2,1)S(1)} %get-tuple-element.16), channel_id=1, replica_groups=mesh['crops'=2,'dap'=16] {'dap'}, dimensions={0} | all-to-all | bytes 1048576 | tf_op jit(solution)/shard_map/all_to_all | solution.py:43
  75.9 0.5 shard_map.86
  76.5 13.9 %all_to_all.28.got_ref = bf16[16,64,128]{2,1,0:T(8,128)(2,1)S(1)} all-to-all(bf16[16,64,128]{2,1,0:T(8,128)(2,1)S(1)} %shard_map.86), channel_id=1, replica_groups=mesh['crops'=2,'dap'=16] {'dap'}, dimensions={0} | all-to-all | bytes 524288 | tf_op jit(solution)/shard_map/all_to_all | solution.py:43
  90.4 1.1 %shard_map.87 = bf16[8,128,128]{2,1,0:T(8,128)(2,1)} custom-call(bf16[16,64,128]{2,1,0:T(8,128)(2,1)S(1)} %all_to_all.28.got_ref, bf16[128,1024]{1,0:T(8,128)(2,1)S(1)} %get-tuple-element.17.pair_ref, f32[128,1024]{1,0:T(8,128)S(1)} %get-tuple-element.18.gate_ref, bf16[2,128,128]{2,1,0:T(8,128)(2,1)S(1)} %copy-done.3), custom_call_target="tpu_custom_call" | custom-call | tf_op jit(solution)/shard_map/pallas_call | solution.py:279
Async XLA Ops:
  0.0 0.7 copy-start.6
  0.7 0.9 copy-start.4
  1.6 0.8 copy-start.5
  2.3 19.2 %copy-start.2 = (bf16[1024,128]{1,0:T(8,128)(2,1)S(1)}, bf16[1024,128]{1,0:T(8,128)(2,1)}, u32[]{:S(2)}) copy-start(bf16[1024,128]{1,0:T(8,128)(2,1)} %exit_ref.1) | copy-start | bytes 786436
  3.5 18.1 %copy-start = (bf16[2,128,5,128]{3,1,2,0:T(8,128)(2,1)S(1)}, bf16[2,128,5,128]{3,1,2,0:T(8,128)(2,1)}, u32[]{:S(2)}) copy-start(bf16[2,128,5,128]{3,1,2,0:T(8,128)(2,1)} %param.14) | copy-start | bytes 983044
  3.5 18.1 %copy-start.1 = (bf16[8,128,128]{2,1,0:T(8,128)(2,1)S(1)}, bf16[8,128,128]{2,1,0:T(8,128)(2,1)}, u32[]{:S(2)}) copy-start(bf16[8,128,128]{2,1,0:T(8,128)(2,1)} %couple_ref.1) | copy-start | bytes 786436
  3.5 18.1 %all-to-all-start = ((bf16[16,72,128]{2,1,0:T(8,128)(2,1)}), bf16[16,72,128]{2,1,0:T(8,128)(2,1)S(1)}, u32[]{:S(2)}, u32[]{:S(2)}) async-start(bf16[16,72,128]{2,1,0:T(8,128)(2,1)} %shard_map.82), calls=%async_computation | async-start | bytes 589824 | tf_op jit(solution)/shard_map/all_to_all | solution.py:43
  21.6 0.7 copy-start.7
  43.1 14.1 %copy-start.3 = (bf16[2,128,128]{2,1,0:T(8,128)(2,1)S(1)}, bf16[2,128,128]{2,1,0:T(8,128)(2,1)}, u32[]{:S(2)}) copy-start(bf16[2,128,128]{2,1,0:T(8,128)(2,1)} %leave_ref.3) | copy-start | bytes 196612

commit v4 on v3

--- a/solution.py
+++ b/solution.py
@@ -12,8 +12,7 @@
 EPS = 1e-05
 LANES = 128
 VMEM = pl.BlockSpec(memory_space=pltpu.VMEM)
-SMEM = pl.BlockSpec(memory_space=pltpu.SMEM)
-PARAMS = pltpu.CompilerParams(vmem_limit_bytes=40 * 1024 * 1024)
+HBM = pl.BlockSpec(memory_space=pltpu.HBM)
 
 
 def dot(a, b, left=1, right=0):
@@ -116,7 +115,23 @@
     return triangle(pair_two, row_mask, trilateral_entry_matrices[1], trilateral_exit_matrices[1], True, devices)
 
 
-def entry_kernel(x_ref, cover_ref, weight_ref, out_ref):
+def start_copies(pairs, sems):
+    copies = [pltpu.make_async_copy(source, target, sems.at[at]) for at, (source, target) in enumerate(pairs)]
+    for copy in copies:
+        copy.start()
+    return copies
+
+
+def halves(row):
+    return [pltpu.roll(row, LANES // 2, 1), row]
+
+
+def entry_kernel(x_hbm, cover_hbm, flag_hbm, weight_hbm, out_ref, x_ref, cover_ref, flag_ref, weight_ref, sems):
+    copies = start_copies(
+        [(x_hbm, x_ref), (weight_hbm, weight_ref), (cover_hbm, cover_ref), (flag_hbm, flag_ref)], sems
+    )
+    for copy in copies:
+        copy.wait()
     held, cols, _ = x_ref.shape
     width = weight_ref.shape[1]
     devices = out_ref.shape[0]
@@ -126,14 +141,16 @@
     own = jnp.zeros((cols, LANES), F32)
     marks = []
     for s in range(held):
+        marks += halves(cover[s : s + 1])
+    marks += halves(flag_ref[...].astype(F32))
+    marks = jnp.concatenate(marks + [jnp.zeros((8 - len(marks), cols), F32)], axis=0)
+    for s in range(held):
         normalized = norm(x_ref[s].astype(F32), -1)
         shared = (dot(weight_ref[1], normalized, 1, 1) * cover[s : s + 1]).astype(BF16)
         for peer in range(devices):
             out_ref[peer, s * width : (s + 1) * width, :] = shared
         weight = jnp.concatenate([weight_ref[0] if at == s else blank for at in range(LANES // width)], axis=0)
         own = own + dot(normalized, weight, 1, 1) * columns[:, s : s + 1]
-        marks += [pltpu.roll(cover[s : s + 1], LANES // 2, 1), cover[s : s + 1]]
-    marks = jnp.concatenate(marks + [jnp.zeros((8 - 2 * held, cols), F32)], axis=0)
     lane = lax.broadcasted_iota(jnp.int32, (8, LANES), 1)
     for peer in range(devices):
         block = jnp.where(lane < held * width, own[peer * 8 : peer * 8 + 8], marks)
@@ -158,13 +175,14 @@
             out_ref[peer, at : at + 2 * share, :] = jnp.concatenate(block, axis=0).astype(BF16)
 
 
-def turned(weight_ref, t):
-    return [jnp.transpose(weight_ref[t, k]) for k in range(weight_ref.shape[1])]
+def turned(weight_ref):
+    return [jnp.transpose(weight_ref[k]) for k in range(weight_ref.shape[0])]
 
 
 def outer_kernel(
-    place_ref, got_ref, couple_ref, exit_ref, weight_ref, flag_ref,
-    out_ref, pair_ref, gate_ref, mask_ref, shared_ref, aux_ref, outer_ref,
+    got_ref, couple_ref, exit_ref, weight_ref,
+    out_ref, pair_ref, gate_ref, mask_ref,
+    shared_ref, aux_ref, outer_ref,
 ):
     devices, _, cols = got_ref.shape
     rows, _, channels = couple_ref.shape
@@ -172,18 +190,18 @@
     shared_ref[...] = got_ref[:, : held * width, :].astype(F32).reshape(devices * held * width, cols)
     aux_ref[...] = got_ref[:, held * width :, :].astype(F32).reshape(devices * 8, cols)
     lane = lax.broadcasted_iota(jnp.int32, (devices, LANES), 1)
-    cover = []
-    for s in range(held):
-        low = aux_ref[pl.ds(2 * s, devices, stride=8), :]
-        high = aux_ref[pl.ds(2 * s + 1, devices, stride=8), :]
-        cover.append(jnp.where(lane < LANES // 2, pltpu.roll(low, LANES // 2, 1), high))
-    cover = jnp.concatenate(cover, axis=0).astype(BF16)
+    marks = []
+    for row in range(0, 2 * held + 2, 2):
+        low = aux_ref[pl.ds(row, devices, stride=8), :]
+        high = aux_ref[pl.ds(row + 1, devices, stride=8), :]
+        marks.append(jnp.where(lane < LANES // 2, pltpu.roll(low, LANES // 2, 1), high))
+    cover = jnp.concatenate(marks[:held], axis=0).astype(BF16)
+    flags = marks[held][0:1]
     chosen = lax.broadcasted_iota(jnp.int32, (rows, LANES), 1) == (
-        lax.broadcasted_iota(jnp.int32, (rows, LANES), 0) + place_ref[0] * rows
+        lax.broadcasted_iota(jnp.int32, (rows, LANES), 0) + lax.axis_index("dap") * rows
     )
     cover_rows = dot(chosen.astype(BF16), cover, 1, 1).astype(BF16)
     scale = 1.0 / dot(cover_rows, cover)
-    flags = flag_ref[...].astype(F32)
     mask_ref[...] = jnp.sum(jnp.where(chosen, flags, 0.0), axis=1, keepdims=True) * flags
     per_tile = LANES // width
     tiles = []
@@ -219,7 +237,7 @@
     shared_ref[...] = exit_ref[...].astype(F32)
     leave = jnp.concatenate([shared_ref[pl.ds(e, width, stride=width), :] for e in range(width)], axis=0)
     leave = jnp.transpose(leave.astype(BF16))
-    weights = turned(weight_ref, 0)
+    weights = turned(weight_ref.at[0])
     for first in range(0, rows, 2):
         at = slice(first * cols, (first + 2) * cols)
         update = dot(leave, outer_ref[:, at])
@@ -259,30 +277,36 @@
 def middle_kernel(got_ref, pair_ref, gate_ref, leave_ref, weight_ref, mask_ref, out_ref, next_ref, next_gate_ref):
     devices, _, cols = got_ref.shape
     leave = jnp.transpose(leave_ref[0])
-    weights = turned(weight_ref, 1)
+    weights = turned(weight_ref.at[1])
     for first in range(0, mask_ref.shape[0], 2):
         pair = updated(got_ref, pair_ref, gate_ref, leave, first).astype(BF16)
         next_ref[:, first * cols : (first + 2) * cols] = pair
         project(pair.astype(F32), weights, mask_ref, out_ref, next_gate_ref, first, devices)
 
 
-def last_kernel(got_ref, pair_ref, gate_ref, leave_ref, out_ref):
+def last_kernel(got_ref, pair_ref, gate_ref, leave_ref, out_hbm, out_ref, sems):
     rows, cols, _ = out_ref.shape
     leave = jnp.transpose(leave_ref[1])
+    copies = []
     for first in range(0, rows, 2):
         pair = updated(got_ref, pair_ref, gate_ref, leave, first)
         for row in range(2):
             out_ref[first + row] = jnp.transpose(pair[:, row * cols : (row + 1) * cols]).astype(BF16)
-
-
-def call(kernel, inputs, outputs, scratch=(), in_specs=None):
+        part = pl.ds(first, 2)
+        copies.append(pltpu.make_async_copy(out_ref.at[part], out_hbm.at[part], sems.at[first // 2]))
+        copies[-1].start()
+    for copy in copies:
+        copy.wait()
+
+
+def call(kernel, inputs, outputs, scratch=(), in_specs=None, out_specs=None, limit=40):
     return pl.pallas_call(
         kernel,
         out_shape=outputs,
         in_specs=in_specs or [VMEM] * len(inputs),
-        out_specs=[VMEM] * len(outputs),
+        out_specs=out_specs or [VMEM] * len(outputs),
         scratch_shapes=list(scratch),
-        compiler_params=PARAMS,
+        compiler_params=pltpu.CompilerParams(vmem_limit_bytes=limit * 1024 * 1024),
     )(*inputs)
 
 
@@ -307,8 +331,22 @@
     part = channels // devices
     (packed,) = call(
         entry_kernel,
-        (homolog_embedding, coverage_indicator, jnp.transpose(pairing_entry_matrices, (1, 2, 0))),
+        (
+            homolog_embedding,
+            coverage_indicator,
+            genuine_amino_flag.reshape(1, cols),
+            jnp.transpose(pairing_entry_matrices, (1, 2, 0)),
+        ),
         [shape((devices, held * width + 8, cols))],
+        [
+            pltpu.VMEM(homolog_embedding.shape, BF16),
+            pltpu.VMEM(coverage_indicator.shape, jnp.int32),
+            pltpu.VMEM((1, cols), jnp.int32),
+            pltpu.VMEM((2, width, homolog_embedding.shape[2]), BF16),
+            pltpu.SemaphoreType.DMA((4,)),
+        ],
+        [HBM] * 4,
+        limit=60,
     )
     entry = jnp.transpose(trilateral_entry_matrices, (0, 2, 1, 3))
     leave = trilateral_exit_matrices
@@ -319,21 +357,13 @@
     ]
     both, pair, gate, row_mask = call(
         outer_kernel,
-        (
-            lax.axis_index("dap").astype(jnp.int32).reshape(1),
-            exchange(packed),
-            couple_embedding,
-            pairing_exit_matrix,
-            entry,
-            genuine_amino_flag.reshape(1, cols),
-        ),
+        (exchange(packed), couple_embedding, pairing_exit_matrix, entry),
         projected + [shape((rows, cols), F32)],
         [
             pltpu.VMEM((devices * held * width, cols), F32),
             pltpu.VMEM((devices * 8, cols), F32),
             pltpu.VMEM((width * width, rows * cols), BF16),
         ],
-        [SMEM] + [VMEM] * 5,
     )
 
     def multiply(both, incoming):
@@ -348,7 +378,13 @@
     got = multiply(both, False)
     both, pair, gate = call(middle_kernel, (got, pair, gate, leave, entry, row_mask), projected)
     got = multiply(both, True)
-    (pair_out,) = call(last_kernel, (got, pair, gate, leave), [shape((rows, cols, channels))])
+    (pair_out,) = call(
+        last_kernel,
+        (got, pair, gate, leave),
+        [shape((rows, cols, channels))],
+        [pltpu.VMEM((rows, cols, channels), BF16), pltpu.SemaphoreType.DMA((rows // 2,))],
+        out_specs=[HBM],
+    )
     return pair_out
 
 

time: 92.1 us -> 90 us (0.977)
  blocking collectives: 62.6 us -> 80.7 us
  waiting for transfers between devices: 10.6 us -> 0 us
  starting transfers between devices: 7.52 us -> 0 us
  local copies, waits for them, and re-layouts: 3 us -> 0.02 us
  Pallas kernels: 7.76 us -> 8.74 us
    all_to_all x4 -> x5, blocking collectives: 62.6 us -> 80.7 us  [exchange(): lax.all_to_all(blocks, 'dap', split_axis=0, concat_axis=0, tiled=True)]
    all_to_all x1 -> x0, waiting for transfers between devices: 10.6 us -> none  [exchange(): lax.all_to_all(blocks, 'dap', split_axis=0, concat_axis=0, tiled=True)]
    all_to_all x1 -> x0, starting transfers between devices: 7.52 us -> none  [exchange(): lax.all_to_all(blocks, 'dap', split_axis=0, concat_axis=0, tiled=True)]
    unnamed x16 -> x8, local copies, waits for them, and re-layouts: 3 us -> 0.02 us
    pallas_call x6, Pallas kernels: 7.76 us -> 8.74 us  [call(): pl.pallas_call(kernel, out_shape=outputs, in_specs=in_specs or [VMEM] * l...]
  transfers between devices with their start and end apart: 1 -> 0, of which waited for: 1 -> 0; matrix products, arithmetic and copies ran while one was open for 0% -> 0% of each run, Pallas kernels for 0% -> 0%
where the time goes in v4:
time: 90 us; the launch traced here: 89.6 us
  blocking collectives  80.7 us (90%)
  Pallas kernels  8.74 us (10%)
    all_to_all x5, blocking collectives, exchange(): lax.all_to_all(blocks, 'dap', split_axis=0, concat_axis=0, tiled=True)  80.7 us
    pallas_call x6, Pallas kernels, call(): pl.pallas_call(kernel, out_shape=outputs, in_specs=in_specs or [VMEM] * l...  8.74 us

profile of v4, /device:TPU:0, one launch (start us, length us, event | category | flops | bytes accessed | tf_op | source)
XLA Modules:
  0.0 89.6 jit_solution(631374841991017207)
XLA Ops:
  0.0 0.0 copy-start.2
  0.0 2.1 %shard_map.82 = bf16[16,72,128]{2,1,0:T(8,128)(2,1)} custom-call(bf16[2,128,256]{2,1,0:T(8,128)(2,1)} %x_hbm.1, s32[2,128]{1,0:T(2,128)} %cover_hbm.1, s32[1,128]{1,0:T(1,128)} %bitcast.6, bf16[2,32,256]{2,1,0:T(8,128)(2,1)} %bitcast.5), custom_call_target="tpu_custom_call" | custom-call | tf_op jit(solution)/shard_map/pallas_call | solution.py:303
  2.1 0.0 copy-start
  2.1 0.0 copy-start.1
  2.1 18.1 %all_to_all.25.got_ref = bf16[16,72,128]{2,1,0:T(8,128)(2,1)S(1)} all-to-all(bf16[16,72,128]{2,1,0:T(8,128)(2,1)} %shard_map.82), channel_id=1, replica_groups=mesh['crops'=2,'dap'=16] {'dap'}, dimensions={0} | all-to-all | bytes 589824 | tf_op jit(solution)/shard_map/all_to_all | solution.py:42
  20.2 0.0 copy-done.2
  20.2 0.0 copy-done
  20.3 0.0 copy-done.1
  20.3 3.1 %shard_map.83 = (bf16[16,128,128]{2,1,0:T(8,128)(2,1)S(1)}, bf16[128,1024]{1,0:T(8,128)(2,1)S(1)}, f32[128,1024]{1,0:T(8,128)S(1)}, f32[8,128]{1,0:T(8,128)S(1)}) custom-call(bf16[16,72,128]{2,1,0:T(8,128)(2,1)S(1)} %all_to_all.25.got_ref, bf16[8,128,128]{2,1,0:T(8,128)(2,1)S(1)} %copy-done.1, bf16[1024,128]{1,0:T(8,128)(2,1)S(1)} %copy-done.2, ...), custom_call_target="tpu_custom_call" | custom-call | tf_op jit(solution)/shard_map/pallas_call | solution.py:303
  23.3 17.4 %all_to_all.26.got_ref = bf16[16,128,128]{2,1,0:T(8,128)(2,1)S(1)} all-to-all(bf16[16,128,128]{2,1,0:T(8,128)(2,1)S(1)} %get-tuple-element.12), channel_id=1, replica_groups=mesh['crops'=2,'dap'=16] {'dap'}, dimensions={0} | all-to-all | bytes 1048576 | tf_op jit(solution)/shard_map/all_to_all | solution.py:42
  40.7 0.5 shard_map.84
  41.2 0.0 copy-start.3
  41.2 14.1 %all_to_all.27.got_ref = bf16[16,64,128]{2,1,0:T(8,128)(2,1)S(1)} all-to-all(bf16[16,64,128]{2,1,0:T(8,128)(2,1)S(1)} %shard_map.84), channel_id=1, replica_groups=mesh['crops'=2,'dap'=16] {'dap'}, dimensions={0} | all-to-all | bytes 524288 | tf_op jit(solution)/shard_map/all_to_all | solution.py:42
  55.3 0.0 copy-done.3
  55.3 1.5 %shard_map.85 = (bf16[16,128,128]{2,1,0:T(8,128)(2,1)S(1)}, bf16[128,1024]{1,0:T(8,128)(2,1)S(1)}, f32[128,1024]{1,0:T(8,128)S(1)}) custom-call(bf16[16,64,128]{2,1,0:T(8,128)(2,1)S(1)} %all_to_all.27.got_ref, bf16[128,1024]{1,0:T(8,128)(2,1)S(1)} %get-tuple-element.13.pair_ref, f32[128,1024]{1,0:T(8,128)S(1)} %get-tuple-element.14.gate_ref, ...), custom_call_target="tpu_custom_call" | custom-call | tf_op jit(solution)/shard_map/pallas_call | solution.py:303
  56.8 17.2 %all_to_all.28.got_ref = bf16[16,128,128]{2,1,0:T(8,128)(2,1)S(1)} all-to-all(bf16[16,128,128]{2,1,0:T(8,128)(2,1)S(1)} %get-tuple-element.16), channel_id=1, replica_groups=mesh['crops'=2,'dap'=16] {'dap'}, dimensions={0} | all-to-all | bytes 1048576 | tf_op jit(solution)/shard_map/all_to_all | solution.py:42
  74.0 0.5 shard_map.86
  74.6 13.9 %all_to_all.29.got_ref = bf16[16,64,128]{2,1,0:T(8,128)(2,1)S(1)} all-to-all(bf16[16,64,128]{2,1,0:T(8,128)(2,1)S(1)} %shard_map.86), channel_id=1, replica_groups=mesh['crops'=2,'dap'=16] {'dap'}, dimensions={0} | all-to-all | bytes 524288 | tf_op jit(solution)/shard_map/all_to_all | solution.py:42
  88.5 1.1 %shard_map.87 = bf16[8,128,128]{2,1,0:T(8,128)(2,1)} custom-call(bf16[16,64,128]{2,1,0:T(8,128)(2,1)S(1)} %all_to_all.29.got_ref, bf16[128,1024]{1,0:T(8,128)(2,1)S(1)} %get-tuple-element.17.pair_ref, f32[128,1024]{1,0:T(8,128)S(1)} %get-tuple-element.18.gate_ref, bf16[2,128,128]{2,1,0:T(8,128)(2,1)S(1)} %copy-done.3), custom_call_target="tpu_custom_call" | custom-call | tf_op jit(solution)/shard_map/pallas_call | solution.py:303
Async XLA Ops:
  0.0 20.2 %copy-start.2 = (bf16[1024,128]{1,0:T(8,128)(2,1)S(1)}, bf16[1024,128]{1,0:T(8,128)(2,1)}, u32[]{:S(2)}) copy-start(bf16[1024,128]{1,0:T(8,128)(2,1)} %exit_ref.1) | copy-start | bytes 786436
  2.1 18.1 %copy-start = (bf16[2,128,5,128]{3,1,2,0:T(8,128)(2,1)S(1)}, bf16[2,128,5,128]{3,1,2,0:T(8,128)(2,1)}, u32[]{:S(2)}) copy-start(bf16[2,128,5,128]{3,1,2,0:T(8,128)(2,1)} %param.14) | copy-start | bytes 983044
  2.1 18.1 %copy-start.1 = (bf16[8,128,128]{2,1,0:T(8,128)(2,1)S(1)}, bf16[8,128,128]{2,1,0:T(8,128)(2,1)}, u32[]{:S(2)}) copy-start(bf16[8,128,128]{2,1,0:T(8,128)(2,1)} %couple_ref.1) | copy-start | bytes 786436
  41.2 14.1 %copy-start.3 = (bf16[2,128,128]{2,1,0:T(8,128)(2,1)S(1)}, bf16[2,128,128]{2,1,0:T(8,128)(2,1)}, u32[]{:S(2)}) copy-start(bf16[2,128,128]{2,1,0:T(8,128)(2,1)} %leave_ref.3) | copy-start | bytes 196612

commit v5 on v4

--- a/solution.py
+++ b/solution.py
@@ -122,6 +122,12 @@
     return copies
 
 
+def two_level(blocks, devices):
+    groups = [list(range(parity, devices, 2)) for parity in range(2)]
+    got = lax.all_to_all(blocks, "dap", split_axis=0, concat_axis=0, tiled=True, axis_index_groups=groups)
+    return got, lax.ppermute(got, "dap", [(at, at ^ 1) for at in range(devices)])
+
+
 def halves(row):
     return [pltpu.roll(row, LANES // 2, 1), row]
 
@@ -134,7 +140,7 @@
         copy.wait()
     held, cols, _ = x_ref.shape
     width = weight_ref.shape[1]
-    devices = out_ref.shape[0]
+    pairs = out_ref.shape[0]
     cover = cover_ref[...].astype(F32)
     columns = jnp.transpose(jnp.concatenate([cover, jnp.zeros((8 - held, cols), F32)], axis=0))
     blank = jnp.zeros_like(weight_ref[0])
@@ -147,14 +153,15 @@
     for s in range(held):
         normalized = norm(x_ref[s].astype(F32), -1)
         shared = (dot(weight_ref[1], normalized, 1, 1) * cover[s : s + 1]).astype(BF16)
-        for peer in range(devices):
-            out_ref[peer, s * width : (s + 1) * width, :] = shared
+        for pair in range(pairs):
+            out_ref[pair, s * width : (s + 1) * width, :] = shared
         weight = jnp.concatenate([weight_ref[0] if at == s else blank for at in range(LANES // width)], axis=0)
         own = own + dot(normalized, weight, 1, 1) * columns[:, s : s + 1]
-    lane = lax.broadcasted_iota(jnp.int32, (8, LANES), 1)
-    for peer in range(devices):
-        block = jnp.where(lane < held * width, own[peer * 8 : peer * 8 + 8], marks)
-        out_ref[peer, held * width :, :] = block.astype(BF16)
+    lane = lax.broadcasted_iota(jnp.int32, (16, LANES), 1)
+    marks = jnp.concatenate([marks, marks], axis=0)
+    for pair in range(pairs):
+        block = jnp.where(lane < held * width, own[pair * 16 : pair * 16 + 16], marks)
+        out_ref[pair, held * width :, :] = block.astype(BF16)
 
 
 def project(pair_tile, weights, mask_ref, out_ref, gate_ref, first, devices):
@@ -175,20 +182,35 @@
             out_ref[peer, at : at + 2 * share, :] = jnp.concatenate(block, axis=0).astype(BF16)
 
 
-def turned(weight_ref):
-    return [jnp.transpose(weight_ref[k]) for k in range(weight_ref.shape[0])]
+def weight_kernel(entry_ref, exit_ref, leave_ref, couple_ref, out_entry, out_exit, out_leave, out_couple, rows_ref):
+    for t in range(entry_ref.shape[0]):
+        for k in range(entry_ref.shape[1]):
+            out_entry[t, k] = jnp.transpose(entry_ref[t, k])
+        out_leave[t] = jnp.transpose(leave_ref[t])
+    width = 32
+    rows_ref[...] = exit_ref[...].astype(F32)
+    leave = jnp.concatenate([rows_ref[pl.ds(e, width, stride=width), :] for e in range(width)], axis=0)
+    out_exit[...] = jnp.transpose(leave).astype(BF16)
+    for row in range(couple_ref.shape[0]):
+        out_couple[:, row * LANES : (row + 1) * LANES] = jnp.transpose(couple_ref[row])
 
 
 def outer_kernel(
-    got_ref, couple_ref, exit_ref, weight_ref,
+    got_ref, other_ref, couple_ref, exit_ref, weight_ref,
     out_ref, pair_ref, gate_ref, mask_ref,
     shared_ref, aux_ref, outer_ref,
 ):
-    devices, _, cols = got_ref.shape
-    rows, _, channels = couple_ref.shape
+    pairs, _, cols = got_ref.shape
+    devices = 2 * pairs
+    rows = couple_ref.shape[1] // cols
     held, width = 2, 32
-    shared_ref[...] = got_ref[:, : held * width, :].astype(F32).reshape(devices * held * width, cols)
-    aux_ref[...] = got_ref[:, held * width :, :].astype(F32).reshape(devices * 8, cols)
+    core = lax.rem(lax.axis_index("dap"), 2)
+    for side, ref in enumerate((got_ref, other_ref)):
+        shared = ref[:, : held * width, :].astype(F32).reshape(pairs * held * width, cols)
+        shared_ref[side * pairs * held * width : (side + 1) * pairs * held * width, :] = shared
+        aux = ref[:, held * width :, :].astype(F32)
+        aux = jnp.where(core == 0, aux[:, :8], aux[:, 8:])
+        aux_ref[side * pairs * 8 : (side + 1) * pairs * 8, :] = aux.reshape(pairs * 8, cols)
     lane = lax.broadcasted_iota(jnp.int32, (devices, LANES), 1)
     marks = []
     for row in range(0, 2 * held + 2, 2):
@@ -234,16 +256,12 @@
                 outer_ref[(e + step) * width : (e + step + 1) * width, i * cols : (i + 1) * cols] = result[
                     i * width : (i + 1) * width, step * cols : (step + 1) * cols
                 ]
-    shared_ref[...] = exit_ref[...].astype(F32)
-    leave = jnp.concatenate([shared_ref[pl.ds(e, width, stride=width), :] for e in range(width)], axis=0)
-    leave = jnp.transpose(leave.astype(BF16))
-    weights = turned(weight_ref.at[0])
+    weights = [weight_ref[0, k] for k in range(5)]
     for first in range(0, rows, 2):
         at = slice(first * cols, (first + 2) * cols)
-        update = dot(leave, outer_ref[:, at])
+        update = dot(exit_ref[...], outer_ref[:, at])
         per_pair = jnp.concatenate([scale[first : first + 1], scale[first + 1 : first + 2]], axis=1)
-        couple = jnp.concatenate([jnp.transpose(couple_ref[first + row].astype(F32)) for row in range(2)], axis=1)
-        pair = (couple + update * per_pair).astype(BF16)
+        pair = (couple_ref[:, at].astype(F32) + update * per_pair).astype(BF16)
         pair_ref[:, at] = pair
         project(pair.astype(F32), weights, mask_ref, out_ref, gate_ref, first, devices)
 
@@ -276,8 +294,8 @@
 
 def middle_kernel(got_ref, pair_ref, gate_ref, leave_ref, weight_ref, mask_ref, out_ref, next_ref, next_gate_ref):
     devices, _, cols = got_ref.shape
-    leave = jnp.transpose(leave_ref[0])
-    weights = turned(weight_ref.at[1])
+    leave = leave_ref[0]
+    weights = [weight_ref[1, k] for k in range(5)]
     for first in range(0, mask_ref.shape[0], 2):
         pair = updated(got_ref, pair_ref, gate_ref, leave, first).astype(BF16)
         next_ref[:, first * cols : (first + 2) * cols] = pair
@@ -286,7 +304,7 @@
 
 def last_kernel(got_ref, pair_ref, gate_ref, leave_ref, out_hbm, out_ref, sems):
     rows, cols, _ = out_ref.shape
-    leave = jnp.transpose(leave_ref[1])
+    leave = leave_ref[1]
     copies = []
     for first in range(0, rows, 2):
         pair = updated(got_ref, pair_ref, gate_ref, leave, first)
@@ -337,7 +355,7 @@
             genuine_amino_flag.reshape(1, cols),
             jnp.transpose(pairing_entry_matrices, (1, 2, 0)),
         ),
-        [shape((devices, held * width + 8, cols))],
+        [shape((devices // 2, held * width + 16, cols))],
         [
             pltpu.VMEM(homolog_embedding.shape, BF16),
             pltpu.VMEM(coverage_indicator.shape, jnp.int32),
@@ -348,8 +366,21 @@
         [HBM] * 4,
         limit=60,
     )
-    entry = jnp.transpose(trilateral_entry_matrices, (0, 2, 1, 3))
-    leave = trilateral_exit_matrices
+    packed, entry, leave_rows, exit_rows, couple_rows = lax.optimization_barrier(
+        (packed, trilateral_entry_matrices, trilateral_exit_matrices, pairing_exit_matrix, couple_embedding)
+    )
+    got = two_level(packed, devices)
+    entry, exit_matrix, leave, couple = call(
+        weight_kernel,
+        (jnp.transpose(entry, (0, 2, 1, 3)), exit_rows, leave_rows, couple_rows),
+        [
+            shape((2, 5, channels, channels)),
+            shape((channels, width * width)),
+            shape((2, channels, channels)),
+            shape((channels, rows * cols)),
+        ],
+        [pltpu.VMEM((width * width, channels), F32)],
+    )
     projected = [
         shape((devices, rows * 2 * part, cols)),
         shape((channels, rows * cols)),
@@ -357,7 +388,7 @@
     ]
     both, pair, gate, row_mask = call(
         outer_kernel,
-        (exchange(packed), couple_embedding, pairing_exit_matrix, entry),
+        (*got, couple, exit_matrix, entry),
         projected + [shape((rows, cols), F32)],
         [
             pltpu.VMEM((devices * held * width, cols), F32),
@@ -391,7 +422,8 @@
 def fits(devices, homolog_embedding, couple_embedding, pairing_entry_matrices):
     rows, cols, channels = couple_embedding.shape
     return (
-        homolog_embedding.shape[0] == 2
+        devices % 2 == 0
+        and homolog_embedding.shape[0] == 2
         and rows == 8
         and cols == LANES
         and channels == 8 * devices

time: 90 us -> 87.9 us (0.977)
  blocking collectives: 80.7 us -> 77.4 us
  local copies, waits for them, and re-layouts: 0.02 us -> 0.96 us
    all_to_all x5 -> x4, blocking collectives: 80.7 us -> 62.4 us  [exchange(): lax.all_to_all(blocks, 'dap', split_axis=0, concat_axis=0, tiled=True)]
    all_to_all x0 -> x1, blocking collectives: none -> 15 us  [two_level(): lax.all_to_all(blocks, 'dap', split_axis=0, concat_axis=0, tiled=True, ax...]
    unnamed x8, local copies, waits for them, and re-layouts: 0.02 us -> 0.96 us
    pallas_call x6 -> x7, Pallas kernels: 8.74 us -> 8.97 us  [call(): pl.pallas_call(kernel, out_shape=outputs, in_specs=in_specs or [VMEM] * l...]
  transfers between devices with their start and end apart: 0 -> 1, of which waited for: 0 -> 0; matrix products, arithmetic and copies ran while one was open for 0% -> 0% of each run, Pallas kernels for 0% -> 1%
where the time goes in v5:
time: 87.9 us; the launch traced here: 87.4 us
  blocking collectives  77.4 us (88%)
  Pallas kernels  8.97 us (10%)
  local copies, waits for them, and re-layouts  0.96 us (1%)
    all_to_all x4, blocking collectives, exchange(): lax.all_to_all(blocks, 'dap', split_axis=0, concat_axis=0, tiled=True)  62.4 us
    all_to_all x1, blocking collectives, two_level(): lax.all_to_all(blocks, 'dap', split_axis=0, concat_axis=0, tiled=True, ax...  15 us
    pallas_call x7, Pallas kernels, call(): pl.pallas_call(kernel, out_shape=outputs, in_specs=in_specs or [VMEM] * l...  8.97 us
  transfers between devices with their start and end apart: 1, of which 0 were waited for; matrix products, arithmetic and copies ran while one was open for 0% of the time, Pallas kernels for 1%

profile of v5, /device:TPU:0, one launch (start us, length us, event | category | flops | bytes accessed | tf_op | source)
XLA Modules:
  0.0 87.4 jit_solution(758173458624881476)
XLA Ops:
  0.0 0.0 copy-start
  0.0 0.0 copy-start.1
  0.0 2.1 %shard_map.82 = bf16[8,80,128]{2,1,0:T(8,128)(2,1)} custom-call(bf16[2,128,256]{2,1,0:T(8,128)(2,1)} %x_hbm.1, s32[2,128]{1,0:T(2,128)} %cover_hbm.1, s32[1,128]{1,0:T(1,128)} %bitcast.5, bf16[2,32,256]{2,1,0:T(8,128)(2,1)} %bitcast.4), custom_call_target="tpu_custom_call" | custom-call | tf_op jit(solution)/shard_map/pallas_call | solution.py:321
  2.1 0.0 copy-start.3
  2.1 15.0 %all_to_all.25.got_ref = bf16[8,80,128]{2,1,0:T(8,128)(2,1)S(1)} all-to-all(bf16[8,80,128]{2,1,0:T(8,128)(2,1)} %shard_map.82), channel_id=1, replica_groups={{0,2,4,6,8,10,12,14},{1,3,5,7,9,11,13,15},{16,18,20,22,24,26,28,30},{17..., dimensions={0} | all-to-all | bytes 327680 | tf_op jit(solution)/shard_map/all_to_all | solution.py:127
  17.1 0.0 collective-permute-start
  17.1 0.0 copy-done
  17.1 0.0 copy-done.1
  17.1 0.0 copy-done.3
  17.1 0.0 copy-start.2
  17.1 0.9 %copy-done.2 = bf16[8,128,128]{2,1,0:T(8,128)(2,1)S(1)} copy-done((bf16[8,128,128]{2,1,0:T(8,128)(2,1)S(1)}, bf16[8,128,128]{2,1,0:T(8,128)(2,1)}, u32[]{:S(2)}) %copy-start.2) | copy-done | bytes 262168
  18.1 0.5 shard_map.83
  18.6 0.0 collective-permute-done.other_ref
  18.6 2.8 %shard_map.84 = (bf16[16,128,128]{2,1,0:T(8,128)(2,1)S(1)}, bf16[128,1024]{1,0:T(8,128)(2,1)S(1)}, f32[128,1024]{1,0:T(8,128)S(1)}, f32[8,128]{1,0:T(8,128)S(1)}) custom-call(bf16[8,80,128]{2,1,0:T(8,128)(2,1)S(1)} %all_to_all.25.got_ref, bf16[8,80,128]{2,1,0:T(8,128)(2,1)S(1)} %collective-permute-done.other_ref, ...), custom_call_target="tpu_custom_call" | custom-call | tf_op jit(solution)/shard_map/pallas_call | solution.py:321
  21.4 17.3 %all_to_all.26.got_ref = bf16[16,128,128]{2,1,0:T(8,128)(2,1)S(1)} all-to-all(bf16[16,128,128]{2,1,0:T(8,128)(2,1)S(1)} %get-tuple-element.29), channel_id=1, replica_groups=mesh['crops'=2,'dap'=16] {'dap'}, dimensions={0} | all-to-all | bytes 1048576 | tf_op jit(solution)/shard_map/all_to_all | solution.py:42
  38.7 0.5 shard_map.85
  39.2 13.9 %all_to_all.27.got_ref = bf16[16,64,128]{2,1,0:T(8,128)(2,1)S(1)} all-to-all(bf16[16,64,128]{2,1,0:T(8,128)(2,1)S(1)} %shard_map.85), channel_id=1, replica_groups=mesh['crops'=2,'dap'=16] {'dap'}, dimensions={0} | all-to-all | bytes 524288 | tf_op jit(solution)/shard_map/all_to_all | solution.py:42
  53.2 1.5 %shard_map.86 = (bf16[16,128,128]{2,1,0:T(8,128)(2,1)S(1)}, bf16[128,1024]{1,0:T(8,128)(2,1)S(1)}, f32[128,1024]{1,0:T(8,128)S(1)}) custom-call(bf16[16,64,128]{2,1,0:T(8,128)(2,1)S(1)} %all_to_all.27.got_ref, bf16[128,1024]{1,0:T(8,128)(2,1)S(1)} %get-tuple-element.30.pair_ref, f32[128,1024]{1,0:T(8,128)S(1)} %get-tuple-element.31.gate_ref, ...), custom_call_target="tpu_custom_call" | custom-call | tf_op jit(solution)/shard_map/pallas_call | solution.py:321
  54.6 17.2 %all_to_all.28.got_ref = bf16[16,128,128]{2,1,0:T(8,128)(2,1)S(1)} all-to-all(bf16[16,128,128]{2,1,0:T(8,128)(2,1)S(1)} %get-tuple-element.34), channel_id=1, replica_groups=mesh['crops'=2,'dap'=16] {'dap'}, dimensions={0} | all-to-all | bytes 1048576 | tf_op jit(solution)/shard_map/all_to_all | solution.py:42
  71.9 0.5 shard_map.87
  72.4 13.9 %all_to_all.29.got_ref = bf16[16,64,128]{2,1,0:T(8,128)(2,1)S(1)} all-to-all(bf16[16,64,128]{2,1,0:T(8,128)(2,1)S(1)} %shard_map.87), channel_id=1, replica_groups=mesh['crops'=2,'dap'=16] {'dap'}, dimensions={0} | all-to-all | bytes 524288 | tf_op jit(solution)/shard_map/all_to_all | solution.py:42
  86.4 1.1 %shard_map.88 = bf16[8,128,128]{2,1,0:T(8,128)(2,1)} custom-call(bf16[16,64,128]{2,1,0:T(8,128)(2,1)S(1)} %all_to_all.29.got_ref, bf16[128,1024]{1,0:T(8,128)(2,1)S(1)} %get-tuple-element.35.pair_ref, f32[128,1024]{1,0:T(8,128)S(1)} %get-tuple-element.36.gate_ref, bf16[2,128,128]{2,1,0:T(8,128)(2,1)S(1)} %get-tuple-element.32.leave_ref), custom_call_target="tpu_custom_call" | custom-call | tf_op jit(solution)/shard_map/pallas_call | solution.py:321
Async XLA Ops:
  0.0 17.1 %copy-start = (bf16[2,128,5,128]{3,1,2,0:T(8,128)(2,1)S(1)}, bf16[2,128,5,128]{3,1,2,0:T(8,128)(2,1)}, u32[]{:S(2)}) copy-start(bf16[2,128,5,128]{3,1,2,0:T(8,128)(2,1)} %param.14) | copy-start | bytes 983044
  0.0 17.1 %copy-start.1 = (bf16[1024,128]{1,0:T(8,128)(2,1)S(1)}, bf16[1024,128]{1,0:T(8,128)(2,1)}, u32[]{:S(2)}) copy-start(bf16[1024,128]{1,0:T(8,128)(2,1)} %exit_ref) | copy-start | bytes 786436
  2.1 15.0 %copy-start.3 = (bf16[2,128,128]{2,1,0:T(8,128)(2,1)S(1)}, bf16[2,128,128]{2,1,0:T(8,128)(2,1)}, u32[]{:S(2)}) copy-start(bf16[2,128,128]{2,1,0:T(8,128)(2,1)} %leave_ref) | copy-start | bytes 196612
  17.1 1.5 %collective-permute-start = (bf16[8,80,128]{2,1,0:T(8,128)(2,1)S(1)}, bf16[8,80,128]{2,1,0:T(8,128)(2,1)S(1)}, u32[]{:S(2)}, u32[]{:S(2)}) collective-permute-start(bf16[8,80,128]{2,1,0:T(8,128)(2,1)S(1)} %all_to_all.25.got_ref), channel_id=1, source_target_pairs={{0,1},{1,0},{2,3},{3,2},{4,5},{5,4},{6,7},{7,6},{8,9},{9,8},{10,11... | collective-permute-start | bytes 491528 | tf_op jit(solution)/shard_map/ppermute | solution.py:128
  17.1 1.0 %copy-start.2 = (bf16[8,128,128]{2,1,0:T(8,128)(2,1)S(1)}, bf16[8,128,128]{2,1,0:T(8,128)(2,1)}, u32[]{:S(2)}) copy-start(bf16[8,128,128]{2,1,0:T(8,128)(2,1)} %couple_ref) | copy-start | bytes 786436

commit v6 on v5

--- a/solution.py
+++ b/solution.py
@@ -169,10 +169,11 @@
     share = pair_tile.shape[0] // devices
     normalized = norm(pair_tile, 0)
     mask = jnp.concatenate([mask_ref[first : first + 1], mask_ref[first + 1 : first + 2]], axis=1)
-    left, right = (
-        sigmoid(dot(weights[k], normalized)) * dot(weights[k + 1], normalized) * mask for k in (0, 2)
-    )
-    gate_ref[:, first * cols : (first + 2) * cols] = sigmoid(dot(weights[4], normalized))
+    size = pair_tile.shape[0]
+    entries = dot(weights, normalized)
+    entries = [entries[k * size : (k + 1) * size] for k in range(5)]
+    left, right = (sigmoid(entries[k]) * entries[k + 1] * mask for k in (0, 2))
+    gate_ref[:, first * cols : (first + 2) * cols] = sigmoid(entries[4])
     for peer in range(devices):
         for row in range(2):
             block = [
@@ -182,17 +183,14 @@
             out_ref[peer, at : at + 2 * share, :] = jnp.concatenate(block, axis=0).astype(BF16)
 
 
-def weight_kernel(entry_ref, exit_ref, leave_ref, couple_ref, out_entry, out_exit, out_leave, out_couple, rows_ref):
+def weight_kernel(entry_ref, exit_ref, out_entry, out_exit, rows_ref):
     for t in range(entry_ref.shape[0]):
         for k in range(entry_ref.shape[1]):
-            out_entry[t, k] = jnp.transpose(entry_ref[t, k])
-        out_leave[t] = jnp.transpose(leave_ref[t])
+            out_entry[t, k * LANES : (k + 1) * LANES, :] = jnp.transpose(entry_ref[t, k])
     width = 32
     rows_ref[...] = exit_ref[...].astype(F32)
     leave = jnp.concatenate([rows_ref[pl.ds(e, width, stride=width), :] for e in range(width)], axis=0)
     out_exit[...] = jnp.transpose(leave).astype(BF16)
-    for row in range(couple_ref.shape[0]):
-        out_couple[:, row * LANES : (row + 1) * LANES] = jnp.transpose(couple_ref[row])
 
 
 def outer_kernel(
@@ -202,7 +200,7 @@
 ):
     pairs, _, cols = got_ref.shape
     devices = 2 * pairs
-    rows = couple_ref.shape[1] // cols
+    rows = couple_ref.shape[0]
     held, width = 2, 32
     core = lax.rem(lax.axis_index("dap"), 2)
     for side, ref in enumerate((got_ref, other_ref)):
@@ -256,12 +254,13 @@
                 outer_ref[(e + step) * width : (e + step + 1) * width, i * cols : (i + 1) * cols] = result[
                     i * width : (i + 1) * width, step * cols : (step + 1) * cols
                 ]
-    weights = [weight_ref[0, k] for k in range(5)]
+    weights = weight_ref[0]
     for first in range(0, rows, 2):
         at = slice(first * cols, (first + 2) * cols)
         update = dot(exit_ref[...], outer_ref[:, at])
         per_pair = jnp.concatenate([scale[first : first + 1], scale[first + 1 : first + 2]], axis=1)
-        pair = (couple_ref[:, at].astype(F32) + update * per_pair).astype(BF16)
+        couple = jnp.concatenate([jnp.transpose(couple_ref[first + row]) for row in range(2)], axis=1)
+        pair = (couple.astype(F32) + update * per_pair).astype(BF16)
         pair_ref[:, at] = pair
         project(pair.astype(F32), weights, mask_ref, out_ref, gate_ref, first, devices)
 
@@ -294,8 +293,8 @@
 
 def middle_kernel(got_ref, pair_ref, gate_ref, leave_ref, weight_ref, mask_ref, out_ref, next_ref, next_gate_ref):
     devices, _, cols = got_ref.shape
-    leave = leave_ref[0]
-    weights = [weight_ref[1, k] for k in range(5)]
+    leave = jnp.transpose(leave_ref[0])
+    weights = weight_ref[1]
     for first in range(0, mask_ref.shape[0], 2):
         pair = updated(got_ref, pair_ref, gate_ref, leave, first).astype(BF16)
         next_ref[:, first * cols : (first + 2) * cols] = pair
@@ -304,7 +303,7 @@
 
 def last_kernel(got_ref, pair_ref, gate_ref, leave_ref, out_hbm, out_ref, sems):
     rows, cols, _ = out_ref.shape
-    leave = leave_ref[1]
+    leave = jnp.transpose(leave_ref[1])
     copies = []
     for first in range(0, rows, 2):
         pair = updated(got_ref, pair_ref, gate_ref, leave, first)
@@ -366,18 +365,14 @@
         [HBM] * 4,
         limit=60,
     )
-    packed, entry, leave_rows, exit_rows, couple_rows = lax.optimization_barrier(
-        (packed, trilateral_entry_matrices, trilateral_exit_matrices, pairing_exit_matrix, couple_embedding)
-    )
+    packed, entry, exit_rows = lax.optimization_barrier((packed, trilateral_entry_matrices, pairing_exit_matrix))
     got = two_level(packed, devices)
-    entry, exit_matrix, leave, couple = call(
+    entry, exit_matrix = call(
         weight_kernel,
-        (jnp.transpose(entry, (0, 2, 1, 3)), exit_rows, leave_rows, couple_rows),
+        (jnp.transpose(entry, (0, 2, 1, 3)), exit_rows),
         [
-            shape((2, 5, channels, channels)),
+            shape((2, 5 * channels, channels)),
             shape((channels, width * width)),
-            shape((2, channels, channels)),
-            shape((channels, rows * cols)),
         ],
         [pltpu.VMEM((width * width, channels), F32)],
     )
@@ -388,7 +383,7 @@
     ]
     both, pair, gate, row_mask = call(
         outer_kernel,
-        (*got, couple, exit_matrix, entry),
+        (*got, couple_embedding, exit_matrix, entry),
         projected + [shape((rows, cols), F32)],
         [
             pltpu.VMEM((devices * held * width, cols), F32),
@@ -407,11 +402,11 @@
         return exchange(products)
 
     got = multiply(both, False)
-    both, pair, gate = call(middle_kernel, (got, pair, gate, leave, entry, row_mask), projected)
+    both, pair, gate = call(middle_kernel, (got, pair, gate, trilateral_exit_matrices, entry, row_mask), projected)
     got = multiply(both, True)
     (pair_out,) = call(
         last_kernel,
-        (got, pair, gate, leave),
+        (got, pair, gate, trilateral_exit_matrices),
         [shape((rows, cols, channels))],
         [pltpu.VMEM((rows, cols, channels), BF16), pltpu.SemaphoreType.DMA((rows // 2,))],
         out_specs=[HBM],

time: 87.9 us -> 86.5 us (0.984)
  Pallas kernels: 8.97 us -> 7.76 us
  local copies, waits for them, and re-layouts: 0.96 us -> 0.02 us
  waiting for transfers between devices: 0.01 us -> 0.91 us
    pallas_call x7, Pallas kernels: 8.97 us -> 7.76 us  [call(): pl.pallas_call(kernel, out_shape=outputs, in_specs=in_specs or [VMEM] * l...]
    unnamed x8, local copies, waits for them, and re-layouts: 0.96 us -> 0.02 us
    ppermute x1, waiting for transfers between devices: 0.01 us -> 0.91 us  [two_level(): lax.ppermute(got, 'dap', [(at, at ^ 1) for at in range(devices)])]
  transfers between devices with their start and end apart: 1 -> 1, of which waited for: 0 -> 1; matrix products, arithmetic and copies ran while one was open for 0% -> 0% of each run, Pallas kernels for 1% -> 1%
where the time goes in v6:
time: 86.5 us; the launch traced here: 86.1 us
  blocking collectives  77.3 us (89%)
  Pallas kernels  7.76 us (9%)
  waiting for transfers between devices  0.91 us (1%)
    all_to_all x4, blocking collectives, exchange(): lax.all_to_all(blocks, 'dap', split_axis=0, concat_axis=0, tiled=True)  62.5 us
    all_to_all x1, blocking collectives, two_level(): lax.all_to_all(blocks, 'dap', split_axis=0, concat_axis=0, tiled=True, ax...  14.9 us
    pallas_call x7, Pallas kernels, call(): pl.pallas_call(kernel, out_shape=outputs, in_specs=in_specs or [VMEM] * l...  7.76 us
  transfers between devices with their start and end apart: 1, of which 1 were waited for; matrix products, arithmetic and copies ran while one was open for 0% of the time, Pallas kernels for 1%

profile of v6, /device:TPU:0, one launch (start us, length us, event | category | flops | bytes accessed | tf_op | source)
XLA Modules:
  0.0 86.1 jit_solution(955978649734240210)
XLA Ops:
  0.0 0.0 copy-start
  0.0 0.0 copy-start.1
  0.0 2.1 %shard_map.82 = bf16[8,80,128]{2,1,0:T(8,128)(2,1)} custom-call(bf16[2,128,256]{2,1,0:T(8,128)(2,1)} %x_hbm.1, s32[2,128]{1,0:T(2,128)} %cover_hbm.1, s32[1,128]{1,0:T(1,128)} %bitcast.5, bf16[2,32,256]{2,1,0:T(8,128)(2,1)} %bitcast.4), custom_call_target="tpu_custom_call" | custom-call | tf_op jit(solution)/shard_map/pallas_call | solution.py:320
  2.1 14.9 %all_to_all.25.got_ref = bf16[8,80,128]{2,1,0:T(8,128)(2,1)S(1)} all-to-all(bf16[8,80,128]{2,1,0:T(8,128)(2,1)} %shard_map.82), channel_id=1, replica_groups={{0,2,4,6,8,10,12,14},{1,3,5,7,9,11,13,15},{16,18,20,22,24,26,28,30},{17..., dimensions={0} | all-to-all | bytes 327680 | tf_op jit(solution)/shard_map/all_to_all | solution.py:127
  17.0 0.0 collective-permute-start
  17.0 0.0 copy-done
  17.0 0.0 copy-done.1
  17.0 0.0 copy-start.2
  17.0 0.5 shard_map.83
  17.4 0.9 %collective-permute-done.other_ref = bf16[8,80,128]{2,1,0:T(8,128)(2,1)S(1)} collective-permute-done((bf16[8,80,128]{2,1,0:T(8,128)(2,1)S(1)}, bf16[8,80,128]{2,1,0:T(8,128)(2,1)S(1)}, u32[]{:S(2)}, u32[]{:S(2)}) %collective-permute-start) | collective-permute-done | bytes 163872 | tf_op jit(solution)/shard_map/ppermute | solution.py:128
  18.3 0.0 copy-done.2
  18.4 2.0 %shard_map.84 = (bf16[16,128,128]{2,1,0:T(8,128)(2,1)S(1)}, bf16[128,1024]{1,0:T(8,128)(2,1)S(1)}, f32[128,1024]{1,0:T(8,128)S(1)}, f32[8,128]{1,0:T(8,128)S(1)}) custom-call(bf16[8,80,128]{2,1,0:T(8,128)(2,1)S(1)} %all_to_all.25.got_ref, bf16[8,80,128]{2,1,0:T(8,128)(2,1)S(1)} %collective-permute-done.other_ref, bf16[8,128,128]{2,1,0:T(8,128)(2,1)S(1)} %copy-done.2, ...), custom_call_target="tpu_custom_call" | custom-call | tf_op jit(solution)/shard_map/pallas_call | solution.py:320
  20.4 17.2 %all_to_all.26.got_ref = bf16[16,128,128]{2,1,0:T(8,128)(2,1)S(1)} all-to-all(bf16[16,128,128]{2,1,0:T(8,128)(2,1)S(1)} %get-tuple-element.22), channel_id=1, replica_groups=mesh['crops'=2,'dap'=16] {'dap'}, dimensions={0} | all-to-all | bytes 1048576 | tf_op jit(solution)/shard_map/all_to_all | solution.py:42
  37.6 0.5 shard_map.85
  38.1 0.0 copy-start.3
  38.1 14.1 %all_to_all.27.got_ref = bf16[16,64,128]{2,1,0:T(8,128)(2,1)S(1)} all-to-all(bf16[16,64,128]{2,1,0:T(8,128)(2,1)S(1)} %shard_map.85), channel_id=1, replica_groups=mesh['crops'=2,'dap'=16] {'dap'}, dimensions={0} | all-to-all | bytes 524288 | tf_op jit(solution)/shard_map/all_to_all | solution.py:42
  52.2 0.0 copy-done.3
  52.2 1.1 %shard_map.86 = (bf16[16,128,128]{2,1,0:T(8,128)(2,1)S(1)}, bf16[128,1024]{1,0:T(8,128)(2,1)S(1)}, f32[128,1024]{1,0:T(8,128)S(1)}) custom-call(bf16[16,64,128]{2,1,0:T(8,128)(2,1)S(1)} %all_to_all.27.got_ref, bf16[128,1024]{1,0:T(8,128)(2,1)S(1)} %get-tuple-element.23.pair_ref, f32[128,1024]{1,0:T(8,128)S(1)} %get-tuple-element.24.gate_ref, ...), custom_call_target="tpu_custom_call" | custom-call | tf_op jit(solution)/shard_map/pallas_call | solution.py:320
  53.3 17.2 %all_to_all.28.got_ref = bf16[16,128,128]{2,1,0:T(8,128)(2,1)S(1)} all-to-all(bf16[16,128,128]{2,1,0:T(8,128)(2,1)S(1)} %get-tuple-element.26), channel_id=1, replica_groups=mesh['crops'=2,'dap'=16] {'dap'}, dimensions={0} | all-to-all | bytes 1048576 | tf_op jit(solution)/shard_map/all_to_all | solution.py:42
  70.5 0.5 shard_map.87
  71.1 13.9 %all_to_all.29.got_ref = bf16[16,64,128]{2,1,0:T(8,128)(2,1)S(1)} all-to-all(bf16[16,64,128]{2,1,0:T(8,128)(2,1)S(1)} %shard_map.87), channel_id=1, replica_groups=mesh['crops'=2,'dap'=16] {'dap'}, dimensions={0} | all-to-all | bytes 524288 | tf_op jit(solution)/shard_map/all_to_all | solution.py:42
  85.0 1.1 %shard_map.88 = bf16[8,128,128]{2,1,0:T(8,128)(2,1)} custom-call(bf16[16,64,128]{2,1,0:T(8,128)(2,1)S(1)} %all_to_all.29.got_ref, bf16[128,1024]{1,0:T(8,128)(2,1)S(1)} %get-tuple-element.27.pair_ref, f32[128,1024]{1,0:T(8,128)S(1)} %get-tuple-element.28.gate_ref, bf16[2,128,128]{2,1,0:T(8,128)(2,1)S(1)} %copy-done.3), custom_call_target="tpu_custom_call" | custom-call | tf_op jit(solution)/shard_map/pallas_call | solution.py:320
Async XLA Ops:
  0.0 17.0 %copy-start = (bf16[2,128,5,128]{3,1,2,0:T(8,128)(2,1)S(1)}, bf16[2,128,5,128]{3,1,2,0:T(8,128)(2,1)}, u32[]{:S(2)}) copy-start(bf16[2,128,5,128]{3,1,2,0:T(8,128)(2,1)} %param.14) | copy-start | bytes 983044
  0.0 17.0 %copy-start.1 = (bf16[1024,128]{1,0:T(8,128)(2,1)S(1)}, bf16[1024,128]{1,0:T(8,128)(2,1)}, u32[]{:S(2)}) copy-start(bf16[1024,128]{1,0:T(8,128)(2,1)} %exit_ref) | copy-start | bytes 786436
  17.0 1.4 %collective-permute-start = (bf16[8,80,128]{2,1,0:T(8,128)(2,1)S(1)}, bf16[8,80,128]{2,1,0:T(8,128)(2,1)S(1)}, u32[]{:S(2)}, u32[]{:S(2)}) collective-permute-start(bf16[8,80,128]{2,1,0:T(8,128)(2,1)S(1)} %all_to_all.25.got_ref), channel_id=1, source_target_pairs={{0,1},{1,0},{2,3},{3,2},{4,5},{5,4},{6,7},{7,6},{8,9},{9,8},{10,11... | collective-permute-start | bytes 491528 | tf_op jit(solution)/shard_map/ppermute | solution.py:128
  17.0 1.4 %copy-start.2 = (bf16[8,128,128]{2,1,0:T(8,128)(2,1)S(1)}, bf16[8,128,128]{2,1,0:T(8,128)(2,1)}, u32[]{:S(2)}) copy-start(bf16[8,128,128]{2,1,0:T(8,128)(2,1)} %couple_ref.1) | copy-start | bytes 786436
  38.1 14.1 %copy-start.3 = (bf16[2,128,128]{2,1,0:T(8,128)(2,1)S(1)}, bf16[2,128,128]{2,1,0:T(8,128)(2,1)}, u32[]{:S(2)}) copy-start(bf16[2,128,128]{2,1,0:T(8,128)(2,1)} %leave_ref.3) | copy-start | bytes 196612

commit v7 on v6

--- a/solution.py
+++ b/solution.py
@@ -164,22 +164,23 @@
         out_ref[pair, held * width :, :] = block.astype(BF16)
 
 
-def project(pair_tile, weights, mask_ref, out_ref, gate_ref, first, devices):
-    cols = pair_tile.shape[1] // 2
-    share = pair_tile.shape[0] // devices
-    normalized = norm(pair_tile, 0)
-    mask = jnp.concatenate([mask_ref[first : first + 1], mask_ref[first + 1 : first + 2]], axis=1)
-    size = pair_tile.shape[0]
-    entries = dot(weights, normalized)
+def flat(rows):
+    return jnp.concatenate([rows[row : row + 1] for row in range(rows.shape[0])], axis=1)
+
+
+def project(pair, weights, mask_ref, out_ref, gate_ref):
+    size = pair.shape[0]
+    rows, cols = mask_ref.shape
+    share = size // out_ref.shape[0]
+    entries = dot(weights, norm(pair, 0))
     entries = [entries[k * size : (k + 1) * size] for k in range(5)]
+    mask = flat(mask_ref[...])
     left, right = (sigmoid(entries[k]) * entries[k + 1] * mask for k in (0, 2))
-    gate_ref[:, first * cols : (first + 2) * cols] = sigmoid(entries[4])
-    for peer in range(devices):
-        for row in range(2):
-            block = [
-                side[peer * share : (peer + 1) * share, row * cols : (row + 1) * cols] for side in (left, right)
-            ]
-            at = (first + row) * 2 * share
+    gate_ref[...] = sigmoid(entries[4])
+    for peer in range(out_ref.shape[0]):
+        for row in range(rows):
+            block = [side[peer * share : (peer + 1) * share, row * cols : (row + 1) * cols] for side in (left, right)]
+            at = row * 2 * share
             out_ref[peer, at : at + 2 * share, :] = jnp.concatenate(block, axis=0).astype(BF16)
 
 
@@ -254,15 +255,10 @@
                 outer_ref[(e + step) * width : (e + step + 1) * width, i * cols : (i + 1) * cols] = result[
                     i * width : (i + 1) * width, step * cols : (step + 1) * cols
                 ]
-    weights = weight_ref[0]
-    for first in range(0, rows, 2):
-        at = slice(first * cols, (first + 2) * cols)
-        update = dot(exit_ref[...], outer_ref[:, at])
-        per_pair = jnp.concatenate([scale[first : first + 1], scale[first + 1 : first + 2]], axis=1)
-        couple = jnp.concatenate([jnp.transpose(couple_ref[first + row]) for row in range(2)], axis=1)
-        pair = (couple.astype(F32) + update * per_pair).astype(BF16)
-        pair_ref[:, at] = pair
-        project(pair.astype(F32), weights, mask_ref, out_ref, gate_ref, first, devices)
+    couple = jnp.concatenate([jnp.transpose(couple_ref[row]) for row in range(rows)], axis=1)
+    pair = (couple.astype(F32) + dot(exit_ref[...], outer_ref[...]) * flat(scale)).astype(BF16)
+    pair_ref[...] = pair
+    project(pair.astype(F32), weight_ref[0], mask_ref, out_ref, gate_ref)
 
 
 def product_kernel(incoming, got_ref, out_ref, sides_ref, products_ref):
@@ -278,40 +274,32 @@
     out_ref[...] = products_ref[...].astype(BF16).reshape(out_ref.shape)
 
 
-def updated(got_ref, pair_ref, gate_ref, leave, first):
-    devices, _, cols = got_ref.shape
+def updated(got_ref, pair_ref, gate_ref, leave):
+    devices, size, cols = got_ref.shape
     part = 8
-    channels = devices * part
-    got = got_ref[:, first * part : (first + 2) * part, :].astype(F32)
-    products = jnp.concatenate(
-        [got[:, :part].reshape(channels, cols), got[:, part:].reshape(channels, cols)], axis=1
-    )
-    at = slice(first * cols, (first + 2) * cols)
-    update = dot(leave, norm(products, 0))
-    return pair_ref[:, at].astype(F32) + gate_ref[:, at] * update
+    products = [
+        got_ref[:, at : at + part, :].astype(F32).reshape(devices * part, cols) for at in range(0, size, part)
+    ]
+    update = dot(jnp.transpose(leave), norm(jnp.concatenate(products, axis=1), 0))
+    return pair_ref[...].astype(F32) + gate_ref[...] * update
 
 
 def middle_kernel(got_ref, pair_ref, gate_ref, leave_ref, weight_ref, mask_ref, out_ref, next_ref, next_gate_ref):
-    devices, _, cols = got_ref.shape
-    leave = jnp.transpose(leave_ref[0])
-    weights = weight_ref[1]
-    for first in range(0, mask_ref.shape[0], 2):
-        pair = updated(got_ref, pair_ref, gate_ref, leave, first).astype(BF16)
-        next_ref[:, first * cols : (first + 2) * cols] = pair
-        project(pair.astype(F32), weights, mask_ref, out_ref, next_gate_ref, first, devices)
+    pair = updated(got_ref, pair_ref, gate_ref, leave_ref[0]).astype(BF16)
+    next_ref[...] = pair
+    project(pair.astype(F32), weight_ref[1], mask_ref, out_ref, next_gate_ref)
 
 
 def last_kernel(got_ref, pair_ref, gate_ref, leave_ref, out_hbm, out_ref, sems):
     rows, cols, _ = out_ref.shape
-    leave = jnp.transpose(leave_ref[1])
+    pair = updated(got_ref, pair_ref, gate_ref, leave_ref[1])
     copies = []
-    for first in range(0, rows, 2):
-        pair = updated(got_ref, pair_ref, gate_ref, leave, first)
-        for row in range(2):
-            out_ref[first + row] = jnp.transpose(pair[:, row * cols : (row + 1) * cols]).astype(BF16)
-        part = pl.ds(first, 2)
-        copies.append(pltpu.make_async_copy(out_ref.at[part], out_hbm.at[part], sems.at[first // 2]))
-        copies[-1].start()
+    for row in range(rows):
+        out_ref[row] = jnp.transpose(pair[:, row * cols : (row + 1) * cols]).astype(BF16)
+        if row % 4 == 3:
+            part = pl.ds(row - 3, 4)
+            copies.append(pltpu.make_async_copy(out_ref.at[part], out_hbm.at[part], sems.at[row // 4]))
+            copies[-1].start()
     for copy in copies:
         copy.wait()
 
@@ -408,7 +396,7 @@
         last_kernel,
         (got, pair, gate, trilateral_exit_matrices),
         [shape((rows, cols, channels))],
-        [pltpu.VMEM((rows, cols, channels), BF16), pltpu.SemaphoreType.DMA((rows // 2,))],
+        [pltpu.VMEM((rows, cols, channels), BF16), pltpu.SemaphoreType.DMA((rows // 4,))],
         out_specs=[HBM],
     )
     return pair_out

time: 86.5 us -> 86 us (level)
  no operation moved by 1% of the time
where the time goes in v7:
time: 86 us; the launch traced here: 85.6 us
  blocking collectives  77.3 us (90%)
  Pallas kernels  7.29 us (8%)
  waiting for transfers between devices  0.91 us (1%)
    all_to_all x4, blocking collectives, exchange(): lax.all_to_all(blocks, 'dap', split_axis=0, concat_axis=0, tiled=True)  62.5 us
    all_to_all x1, blocking collectives, two_level(): lax.all_to_all(blocks, 'dap', split_axis=0, concat_axis=0, tiled=True, ax...  14.9 us
    pallas_call x7, Pallas kernels, call(): pl.pallas_call(kernel, out_shape=outputs, in_specs=in_specs or [VMEM] * l...  7.29 us
  transfers between devices with their start and end apart: 1, of which 1 were waited for; matrix products, arithmetic and copies ran while one was open for 0% of the time, Pallas kernels for 1%

profile of v7, /device:TPU:0, one launch (start us, length us, event | category | flops | bytes accessed | tf_op | source)
XLA Modules:
  0.0 85.6 jit_solution(30585028428368705)
XLA Ops:
  0.0 0.0 copy-start
  0.0 0.0 copy-start.1
  0.0 2.1 %shard_map.82 = bf16[8,80,128]{2,1,0:T(8,128)(2,1)} custom-call(bf16[2,128,256]{2,1,0:T(8,128)(2,1)} %x_hbm.1, s32[2,128]{1,0:T(2,128)} %cover_hbm.1, s32[1,128]{1,0:T(1,128)} %bitcast.5, bf16[2,32,256]{2,1,0:T(8,128)(2,1)} %bitcast.4), custom_call_target="tpu_custom_call" | custom-call | tf_op jit(solution)/shard_map/pallas_call | solution.py:308
  2.1 14.9 %all_to_all.25.got_ref = bf16[8,80,128]{2,1,0:T(8,128)(2,1)S(1)} all-to-all(bf16[8,80,128]{2,1,0:T(8,128)(2,1)} %shard_map.82), channel_id=1, replica_groups={{0,2,4,6,8,10,12,14},{1,3,5,7,9,11,13,15},{16,18,20,22,24,26,28,30},{17..., dimensions={0} | all-to-all | bytes 327680 | tf_op jit(solution)/shard_map/all_to_all | solution.py:127
  17.0 0.0 collective-permute-start
  17.0 0.0 copy-done
  17.0 0.0 copy-done.1
  17.0 0.0 copy-start.2
  17.0 0.5 shard_map.83
  17.4 0.9 %collective-permute-done.other_ref = bf16[8,80,128]{2,1,0:T(8,128)(2,1)S(1)} collective-permute-done((bf16[8,80,128]{2,1,0:T(8,128)(2,1)S(1)}, bf16[8,80,128]{2,1,0:T(8,128)(2,1)S(1)}, u32[]{:S(2)}, u32[]{:S(2)}) %collective-permute-start) | collective-permute-done | bytes 163872 | tf_op jit(solution)/shard_map/ppermute | solution.py:128
  18.3 0.0 copy-done.2
  18.4 1.7 %shard_map.84 = (bf16[16,128,128]{2,1,0:T(8,128)(2,1)S(1)}, bf16[128,1024]{1,0:T(8,128)(2,1)S(1)}, f32[128,1024]{1,0:T(8,128)S(1)}, f32[8,128]{1,0:T(8,128)S(1)}) custom-call(bf16[8,80,128]{2,1,0:T(8,128)(2,1)S(1)} %all_to_all.25.got_ref, bf16[8,80,128]{2,1,0:T(8,128)(2,1)S(1)} %collective-permute-done.other_ref, bf16[8,128,128]{2,1,0:T(8,128)(2,1)S(1)} %copy-done.2, ...), custom_call_target="tpu_custom_call" | custom-call | tf_op jit(solution)/shard_map/pallas_call | solution.py:308
  20.1 17.2 %all_to_all.26.got_ref = bf16[16,128,128]{2,1,0:T(8,128)(2,1)S(1)} all-to-all(bf16[16,128,128]{2,1,0:T(8,128)(2,1)S(1)} %get-tuple-element.22), channel_id=1, replica_groups=mesh['crops'=2,'dap'=16] {'dap'}, dimensions={0} | all-to-all | bytes 1048576 | tf_op jit(solution)/shard_map/all_to_all | solution.py:42
  37.3 0.5 shard_map.85
  37.8 0.0 copy-start.3
  37.8 14.1 %all_to_all.27.got_ref = bf16[16,64,128]{2,1,0:T(8,128)(2,1)S(1)} all-to-all(bf16[16,64,128]{2,1,0:T(8,128)(2,1)S(1)} %shard_map.85), channel_id=1, replica_groups=mesh['crops'=2,'dap'=16] {'dap'}, dimensions={0} | all-to-all | bytes 524288 | tf_op jit(solution)/shard_map/all_to_all | solution.py:42
  51.8 0.0 copy-done.3
  51.8 0.9 %shard_map.86 = (bf16[16,128,128]{2,1,0:T(8,128)(2,1)S(1)}, bf16[128,1024]{1,0:T(8,128)(2,1)S(1)}, f32[128,1024]{1,0:T(8,128)S(1)}) custom-call(bf16[16,64,128]{2,1,0:T(8,128)(2,1)S(1)} %all_to_all.27.got_ref, bf16[128,1024]{1,0:T(8,128)(2,1)S(1)} %get-tuple-element.23.pair_ref, f32[128,1024]{1,0:T(8,128)S(1)} %get-tuple-element.24.gate_ref, ...), custom_call_target="tpu_custom_call" | custom-call | tf_op jit(solution)/shard_map/pallas_call | solution.py:308
  52.8 17.2 %all_to_all.28.got_ref = bf16[16,128,128]{2,1,0:T(8,128)(2,1)S(1)} all-to-all(bf16[16,128,128]{2,1,0:T(8,128)(2,1)S(1)} %get-tuple-element.26), channel_id=1, replica_groups=mesh['crops'=2,'dap'=16] {'dap'}, dimensions={0} | all-to-all | bytes 1048576 | tf_op jit(solution)/shard_map/all_to_all | solution.py:42
  70.0 0.5 shard_map.87
  70.6 13.9 %all_to_all.29.got_ref = bf16[16,64,128]{2,1,0:T(8,128)(2,1)S(1)} all-to-all(bf16[16,64,128]{2,1,0:T(8,128)(2,1)S(1)} %shard_map.87), channel_id=1, replica_groups=mesh['crops'=2,'dap'=16] {'dap'}, dimensions={0} | all-to-all | bytes 524288 | tf_op jit(solution)/shard_map/all_to_all | solution.py:42
  84.5 1.1 %shard_map.88 = bf16[8,128,128]{2,1,0:T(8,128)(2,1)} custom-call(bf16[16,64,128]{2,1,0:T(8,128)(2,1)S(1)} %all_to_all.29.got_ref, bf16[128,1024]{1,0:T(8,128)(2,1)S(1)} %get-tuple-element.27.pair_ref, f32[128,1024]{1,0:T(8,128)S(1)} %get-tuple-element.28.gate_ref, bf16[2,128,128]{2,1,0:T(8,128)(2,1)S(1)} %copy-done.3), custom_call_target="tpu_custom_call" | custom-call | tf_op jit(solution)/shard_map/pallas_call | solution.py:308
Async XLA Ops:
  0.0 17.0 %copy-start = (bf16[2,128,5,128]{3,1,2,0:T(8,128)(2,1)S(1)}, bf16[2,128,5,128]{3,1,2,0:T(8,128)(2,1)}, u32[]{:S(2)}) copy-start(bf16[2,128,5,128]{3,1,2,0:T(8,128)(2,1)} %param.14) | copy-start | bytes 983044
  0.0 17.0 %copy-start.1 = (bf16[1024,128]{1,0:T(8,128)(2,1)S(1)}, bf16[1024,128]{1,0:T(8,128)(2,1)}, u32[]{:S(2)}) copy-start(bf16[1024,128]{1,0:T(8,128)(2,1)} %exit_ref) | copy-start | bytes 786436
  17.0 1.4 %collective-permute-start = (bf16[8,80,128]{2,1,0:T(8,128)(2,1)S(1)}, bf16[8,80,128]{2,1,0:T(8,128)(2,1)S(1)}, u32[]{:S(2)}, u32[]{:S(2)}) collective-permute-start(bf16[8,80,128]{2,1,0:T(8,128)(2,1)S(1)} %all_to_all.25.got_ref), channel_id=1, source_target_pairs={{0,1},{1,0},{2,3},{3,2},{4,5},{5,4},{6,7},{7,6},{8,9},{9,8},{10,11... | collective-permute-start | bytes 491528 | tf_op jit(solution)/shard_map/ppermute | solution.py:128
  17.0 1.4 %copy-start.2 = (bf16[8,128,128]{2,1,0:T(8,128)(2,1)S(1)}, bf16[8,128,128]{2,1,0:T(8,128)(2,1)}, u32[]{:S(2)}) copy-start(bf16[8,128,128]{2,1,0:T(8,128)(2,1)} %couple_ref.1) | copy-start | bytes 786436
  37.8 14.1 %copy-start.3 = (bf16[2,128,128]{2,1,0:T(8,128)(2,1)S(1)}, bf16[2,128,128]{2,1,0:T(8,128)(2,1)}, u32[]{:S(2)}) copy-start(bf16[2,128,128]{2,1,0:T(8,128)(2,1)} %leave_ref.3) | copy-start | bytes 196612

commit v8 on v7

--- a/solution.py
+++ b/solution.py
@@ -262,37 +262,40 @@
 
 
 def product_kernel(incoming, got_ref, out_ref, sides_ref, products_ref):
-    devices, _, cols = got_ref.shape
-    part = 8
+    cols = got_ref.shape[-1]
+    part = products_ref.shape[0] // cols
     total = sides_ref.shape[0] // (2 * part)
     sides_ref[...] = got_ref[...].astype(F32).reshape(total * 2 * part, cols)
     for h in range(part):
         left = sides_ref[pl.ds(h, total, stride=2 * part), :].astype(BF16)
         right = sides_ref[pl.ds(part + h, total, stride=2 * part), :].astype(BF16)
         result = dot(left, right, 0, 0) if incoming else dot(left, right, 1, 1)
-        products_ref[pl.ds(h, total, stride=part), :] = result
+        products_ref[pl.ds(h, cols, stride=part), :] = result
     out_ref[...] = products_ref[...].astype(BF16).reshape(out_ref.shape)
 
 
-def updated(got_ref, pair_ref, gate_ref, leave):
+def updated(got_ref, pair_ref, gate_ref, leave, parts):
     devices, size, cols = got_ref.shape
-    part = 8
-    products = [
-        got_ref[:, at : at + part, :].astype(F32).reshape(devices * part, cols) for at in range(0, size, part)
-    ]
+    senders = devices // parts
+    share = leave.shape[0] // senders
+    products = []
+    for at in range(0, size, share):
+        got = got_ref[:, at : at + share, :].astype(F32)
+        got = sum(got[begin : begin + senders] for begin in range(0, devices, senders))
+        products.append(got.reshape(senders * share, cols))
     update = dot(jnp.transpose(leave), norm(jnp.concatenate(products, axis=1), 0))
     return pair_ref[...].astype(F32) + gate_ref[...] * update
 
 
 def middle_kernel(got_ref, pair_ref, gate_ref, leave_ref, weight_ref, mask_ref, out_ref, next_ref, next_gate_ref):
-    pair = updated(got_ref, pair_ref, gate_ref, leave_ref[0]).astype(BF16)
+    pair = updated(got_ref, pair_ref, gate_ref, leave_ref[0], 1).astype(BF16)
     next_ref[...] = pair
     project(pair.astype(F32), weight_ref[1], mask_ref, out_ref, next_gate_ref)
 
 
 def last_kernel(got_ref, pair_ref, gate_ref, leave_ref, out_hbm, out_ref, sems):
     rows, cols, _ = out_ref.shape
-    pair = updated(got_ref, pair_ref, gate_ref, leave_ref[1])
+    pair = updated(got_ref, pair_ref, gate_ref, leave_ref[1], 2)
     copies = []
     for row in range(rows):
         out_ref[row] = jnp.transpose(pair[:, row * cols : (row + 1) * cols]).astype(BF16)
@@ -364,15 +367,17 @@
         ],
         [pltpu.VMEM((width * width, channels), F32)],
     )
-    projected = [
-        shape((devices, rows * 2 * part, cols)),
-        shape((channels, rows * cols)),
-        shape((channels, rows * cols), F32),
-    ]
+    def projected(peers):
+        return [
+            shape((peers, devices * rows * 2 * part // peers, cols)),
+            shape((channels, rows * cols)),
+            shape((channels, rows * cols), F32),
+        ]
+
     both, pair, gate, row_mask = call(
         outer_kernel,
         (*got, couple_embedding, exit_matrix, entry),
-        projected + [shape((rows, cols), F32)],
+        projected(devices) + [shape((rows, cols), F32)],
         [
             pltpu.VMEM((devices * held * width, cols), F32),
             pltpu.VMEM((devices * 8, cols), F32),
@@ -380,18 +385,22 @@
         ],
     )
 
-    def multiply(both, incoming):
+    def multiply(both, incoming, part):
         (products,) = call(
             functools.partial(product_kernel, incoming),
-            (exchange(both),),
+            (both,),
             [shape((devices, rows * part, cols))],
-            [pltpu.VMEM((devices * rows * 2 * part, cols), F32), pltpu.VMEM((devices * rows * part, cols), F32)],
+            [pltpu.VMEM((both.size // cols, cols), F32), pltpu.VMEM((devices * rows * part, cols), F32)],
         )
         return exchange(products)
 
-    got = multiply(both, False)
-    both, pair, gate = call(middle_kernel, (got, pair, gate, trilateral_exit_matrices, entry, row_mask), projected)
-    got = multiply(both, True)
+    got = multiply(exchange(both), False, part)
+    both, pair, gate = call(
+        middle_kernel, (got, pair, gate, trilateral_exit_matrices, entry, row_mask), projected(devices // 2)
+    )
+    halves_of = [list(range(begin, begin + devices // 2)) for begin in (0, devices // 2)]
+    both = lax.all_to_all(both, "dap", split_axis=0, concat_axis=0, tiled=True, axis_index_groups=halves_of)
+    got = multiply(both, True, 2 * part)
     (pair_out,) = call(
         last_kernel,
         (got, pair, gate, trilateral_exit_matrices),

time: 86 us -> 84.4 us (0.981)
  blocking collectives: 77.3 us -> 75.1 us
    all_to_all x4 -> x3, blocking collectives: 62.5 us -> 48.9 us  [exchange(): lax.all_to_all(blocks, 'dap', split_axis=0, concat_axis=0, tiled=True)]
    all_to_all x0 -> x1, blocking collectives: none -> 11.3 us  [fast(): lax.all_to_all(both, 'dap', split_axis=0, concat_axis=0, tiled=True, axis...]
where the time goes in v8:
time: 84.4 us; the launch traced here: 84 us
  blocking collectives  75.1 us (89%)
  Pallas kernels  7.88 us (9%)
  waiting for transfers between devices  0.91 us (1%)
    all_to_all x3, blocking collectives, exchange(): lax.all_to_all(blocks, 'dap', split_axis=0, concat_axis=0, tiled=True)  48.9 us
    all_to_all x1, blocking collectives, two_level(): lax.all_to_all(blocks, 'dap', split_axis=0, concat_axis=0, tiled=True, ax...  14.9 us
    all_to_all x1, blocking collectives, fast(): lax.all_to_all(both, 'dap', split_axis=0, concat_axis=0, tiled=True, axis...  11.3 us
    pallas_call x7, Pallas kernels, call(): pl.pallas_call(kernel, out_shape=outputs, in_specs=in_specs or [VMEM] * l...  7.88 us
  transfers between devices with their start and end apart: 1, of which 1 were waited for; matrix products, arithmetic and copies ran while one was open for 0% of the time, Pallas kernels for 1%

profile of v8, /device:TPU:0, one launch (start us, length us, event | category | flops | bytes accessed | tf_op | source)
XLA Modules:
  0.0 84.0 jit_solution(4247741279628324805)
XLA Ops:
  0.0 0.0 copy-start
  0.0 0.0 copy-start.2
  0.0 2.1 %shard_map.82 = bf16[8,80,128]{2,1,0:T(8,128)(2,1)} custom-call(bf16[2,128,256]{2,1,0:T(8,128)(2,1)} %x_hbm.1, s32[2,128]{1,0:T(2,128)} %cover_hbm.1, s32[1,128]{1,0:T(1,128)} %bitcast.5, bf16[2,32,256]{2,1,0:T(8,128)(2,1)} %bitcast.4), custom_call_target="tpu_custom_call" | custom-call | tf_op jit(solution)/shard_map/pallas_call | solution.py:311
  2.1 14.9 %all_to_all.25.got_ref = bf16[8,80,128]{2,1,0:T(8,128)(2,1)S(1)} all-to-all(bf16[8,80,128]{2,1,0:T(8,128)(2,1)} %shard_map.82), channel_id=1, replica_groups={{0,2,4,6,8,10,12,14},{1,3,5,7,9,11,13,15},{16,18,20,22,24,26,28,30},{17..., dimensions={0} | all-to-all | bytes 327680 | tf_op jit(solution)/shard_map/all_to_all | solution.py:127
  17.0 0.0 collective-permute-start
  17.0 0.0 copy-done
  17.0 0.0 copy-done.2
  17.0 0.0 copy-start.3
  17.0 0.5 shard_map.83
  17.4 0.9 %collective-permute-done.other_ref = bf16[8,80,128]{2,1,0:T(8,128)(2,1)S(1)} collective-permute-done((bf16[8,80,128]{2,1,0:T(8,128)(2,1)S(1)}, bf16[8,80,128]{2,1,0:T(8,128)(2,1)S(1)}, u32[]{:S(2)}, u32[]{:S(2)}) %collective-permute-start) | collective-permute-done | bytes 163872 | tf_op jit(solution)/shard_map/ppermute | solution.py:128
  18.3 0.0 copy-done.3
  18.4 1.7 %shard_map.84 = (bf16[16,128,128]{2,1,0:T(8,128)(2,1)S(1)}, bf16[128,1024]{1,0:T(8,128)(2,1)S(1)}, f32[128,1024]{1,0:T(8,128)S(1)}, f32[8,128]{1,0:T(8,128)S(1)}) custom-call(bf16[8,80,128]{2,1,0:T(8,128)(2,1)S(1)} %all_to_all.25.got_ref, bf16[8,80,128]{2,1,0:T(8,128)(2,1)S(1)} %collective-permute-done.other_ref, bf16[8,128,128]{2,1,0:T(8,128)(2,1)S(1)} %copy-done.3, ...), custom_call_target="tpu_custom_call" | custom-call | tf_op jit(solution)/shard_map/pallas_call | solution.py:311
  20.1 17.2 %all_to_all.26.got_ref = bf16[16,128,128]{2,1,0:T(8,128)(2,1)S(1)} all-to-all(bf16[16,128,128]{2,1,0:T(8,128)(2,1)S(1)} %get-tuple-element.22), channel_id=1, replica_groups=mesh['crops'=2,'dap'=16] {'dap'}, dimensions={0} | all-to-all | bytes 1048576 | tf_op jit(solution)/shard_map/all_to_all | solution.py:42
  37.3 0.5 shard_map.85
  37.8 0.0 copy-start.1
  37.8 14.1 %all_to_all.27.got_ref = bf16[16,64,128]{2,1,0:T(8,128)(2,1)S(1)} all-to-all(bf16[16,64,128]{2,1,0:T(8,128)(2,1)S(1)} %shard_map.85), channel_id=1, replica_groups=mesh['crops'=2,'dap'=16] {'dap'}, dimensions={0} | all-to-all | bytes 524288 | tf_op jit(solution)/shard_map/all_to_all | solution.py:42
  51.8 0.0 copy-done.1
  51.8 0.9 %shard_map.86 = (bf16[8,256,128]{2,1,0:T(8,128)(2,1)S(1)}, bf16[128,1024]{1,0:T(8,128)(2,1)S(1)}, f32[128,1024]{1,0:T(8,128)S(1)}) custom-call(bf16[16,64,128]{2,1,0:T(8,128)(2,1)S(1)} %all_to_all.27.got_ref, bf16[128,1024]{1,0:T(8,128)(2,1)S(1)} %get-tuple-element.23.pair_ref, f32[128,1024]{1,0:T(8,128)S(1)} %get-tuple-element.24.gate_ref, ...), custom_call_target="tpu_custom_call" | custom-call | tf_op jit(solution)/shard_map/pallas_call | solution.py:311
  52.8 11.3 %all_to_all.28.got_ref = bf16[8,256,128]{2,1,0:T(8,128)(2,1)S(1)} all-to-all(bf16[8,256,128]{2,1,0:T(8,128)(2,1)S(1)} %get-tuple-element.26), channel_id=1, replica_groups={{0,1,2,3,4,5,6,7},{8,9,10,11,12,13,14,15},{16,17,18,19,20,21,22,23},{24..., dimensions={0} | all-to-all | bytes 1048576 | tf_op jit(solution)/shard_map/all_to_all | solution.py:402
  64.1 1.1 %shard_map.87 = bf16[16,128,128]{2,1,0:T(8,128)(2,1)S(1)} custom-call(bf16[8,256,128]{2,1,0:T(8,128)(2,1)S(1)} %all_to_all.28.got_ref), custom_call_target="tpu_custom_call" | custom-call | tf_op jit(solution)/shard_map/pallas_call | solution.py:311
  65.2 17.6 %all_to_all.29.got_ref = bf16[16,128,128]{2,1,0:T(8,128)(2,1)S(1)} all-to-all(bf16[16,128,128]{2,1,0:T(8,128)(2,1)S(1)} %shard_map.87), channel_id=1, replica_groups=mesh['crops'=2,'dap'=16] {'dap'}, dimensions={0} | all-to-all | bytes 1048576 | tf_op jit(solution)/shard_map/all_to_all | solution.py:42
  82.9 1.1 %shard_map.88 = bf16[8,128,128]{2,1,0:T(8,128)(2,1)} custom-call(bf16[16,128,128]{2,1,0:T(8,128)(2,1)S(1)} %all_to_all.29.got_ref, bf16[128,1024]{1,0:T(8,128)(2,1)S(1)} %get-tuple-element.27.pair_ref, f32[128,1024]{1,0:T(8,128)S(1)} %get-tuple-element.28.gate_ref, bf16[2,128,128]{2,1,0:T(8,128)(2,1)S(1)} %copy-done.1), custom_call_target="tpu_custom_call" | custom-call | tf_op jit(solution)/shard_map/pallas_call | solution.py:311
Async XLA Ops:
  0.0 17.0 %copy-start = (bf16[2,128,5,128]{3,1,2,0:T(8,128)(2,1)S(1)}, bf16[2,128,5,128]{3,1,2,0:T(8,128)(2,1)}, u32[]{:S(2)}) copy-start(bf16[2,128,5,128]{3,1,2,0:T(8,128)(2,1)} %param.14) | copy-start | bytes 983044
  0.0 17.0 %copy-start.2 = (bf16[1024,128]{1,0:T(8,128)(2,1)S(1)}, bf16[1024,128]{1,0:T(8,128)(2,1)}, u32[]{:S(2)}) copy-start(bf16[1024,128]{1,0:T(8,128)(2,1)} %exit_ref) | copy-start | bytes 786436
  17.0 1.4 %collective-permute-start = (bf16[8,80,128]{2,1,0:T(8,128)(2,1)S(1)}, bf16[8,80,128]{2,1,0:T(8,128)(2,1)S(1)}, u32[]{:S(2)}, u32[]{:S(2)}) collective-permute-start(bf16[8,80,128]{2,1,0:T(8,128)(2,1)S(1)} %all_to_all.25.got_ref), channel_id=1, source_target_pairs={{0,1},{1,0},{2,3},{3,2},{4,5},{5,4},{6,7},{7,6},{8,9},{9,8},{10,11... | collective-permute-start | bytes 491528 | tf_op jit(solution)/shard_map/ppermute | solution.py:128
  17.0 1.4 %copy-start.3 = (bf16[8,128,128]{2,1,0:T(8,128)(2,1)S(1)}, bf16[8,128,128]{2,1,0:T(8,128)(2,1)}, u32[]{:S(2)}) copy-start(bf16[8,128,128]{2,1,0:T(8,128)(2,1)} %couple_ref.1) | copy-start | bytes 786436
  37.8 14.1 %copy-start.1 = (bf16[2,128,128]{2,1,0:T(8,128)(2,1)S(1)}, bf16[2,128,128]{2,1,0:T(8,128)(2,1)}, u32[]{:S(2)}) copy-start(bf16[2,128,128]{2,1,0:T(8,128)(2,1)} %leave_ref.3) | copy-start | bytes 196612

commit v9 on v8

--- a/solution.py
+++ b/solution.py
@@ -1,5 +1,3 @@
-import functools
-
 import jax
 import jax.numpy as jnp
 from jax import lax
@@ -261,41 +259,56 @@
     project(pair.astype(F32), weight_ref[0], mask_ref, out_ref, gate_ref)
 
 
-def product_kernel(incoming, got_ref, out_ref, sides_ref, products_ref):
+def side_rows(got_ref, sides_ref, part):
+    sides_ref[...] = got_ref[...].astype(F32).reshape(sides_ref.shape)
+    lines = sides_ref.shape[0] // (2 * part)
+    return lambda h: sides_ref[pl.ds(h, lines, stride=2 * part), :].astype(BF16)
+
+
+def outgoing_kernel(got_ref, out_ref, sides_ref, products_ref):
     cols = got_ref.shape[-1]
     part = products_ref.shape[0] // cols
-    total = sides_ref.shape[0] // (2 * part)
-    sides_ref[...] = got_ref[...].astype(F32).reshape(total * 2 * part, cols)
+    side = side_rows(got_ref, sides_ref, part)
     for h in range(part):
-        left = sides_ref[pl.ds(h, total, stride=2 * part), :].astype(BF16)
-        right = sides_ref[pl.ds(part + h, total, stride=2 * part), :].astype(BF16)
-        result = dot(left, right, 0, 0) if incoming else dot(left, right, 1, 1)
-        products_ref[pl.ds(h, cols, stride=part), :] = result
+        products_ref[pl.ds(h, cols, stride=part), :] = dot(side(h), side(part + h), 1, 1)
     out_ref[...] = products_ref[...].astype(BF16).reshape(out_ref.shape)
 
 
-def updated(got_ref, pair_ref, gate_ref, leave, parts):
-    devices, size, cols = got_ref.shape
-    senders = devices // parts
-    share = leave.shape[0] // senders
-    products = []
-    for at in range(0, size, share):
-        got = got_ref[:, at : at + share, :].astype(F32)
-        got = sum(got[begin : begin + senders] for begin in range(0, devices, senders))
-        products.append(got.reshape(senders * share, cols))
+def incoming_kernel(got_ref, out_ref, sides_ref):
+    peers, size, cols = out_ref.shape
+    rows = cols // peers
+    part = size // rows
+    side = side_rows(got_ref, sides_ref, part)
+    for h in range(0, part, 2):
+        results = [dot(side(at), side(part + at), 0, 0) for at in (h, h + 1)]
+        for peer in range(peers):
+            block = [result[peer * rows : (peer + 1) * rows] for result in results]
+            out_ref[peer, h * rows : (h + 2) * rows, :] = jnp.concatenate(block, axis=0).astype(BF16)
+
+
+def updated(products, pair_ref, gate_ref, leave):
     update = dot(jnp.transpose(leave), norm(jnp.concatenate(products, axis=1), 0))
     return pair_ref[...].astype(F32) + gate_ref[...] * update
 
 
 def middle_kernel(got_ref, pair_ref, gate_ref, leave_ref, weight_ref, mask_ref, out_ref, next_ref, next_gate_ref):
-    pair = updated(got_ref, pair_ref, gate_ref, leave_ref[0], 1).astype(BF16)
+    devices, size, cols = got_ref.shape
+    part = size // mask_ref.shape[0]
+    products = [
+        got_ref[:, at : at + part, :].astype(F32).reshape(devices * part, cols) for at in range(0, size, part)
+    ]
+    pair = updated(products, pair_ref, gate_ref, leave_ref[0]).astype(BF16)
     next_ref[...] = pair
     project(pair.astype(F32), weight_ref[1], mask_ref, out_ref, next_gate_ref)
 
 
-def last_kernel(got_ref, pair_ref, gate_ref, leave_ref, out_hbm, out_ref, sems):
-    rows, cols, _ = out_ref.shape
-    pair = updated(got_ref, pair_ref, gate_ref, leave_ref[1], 2)
+def last_kernel(got_ref, pair_ref, gate_ref, leave_ref, out_hbm, out_ref, sums_ref, sems):
+    rows, cols, channels = out_ref.shape
+    senders = got_ref.shape[0] // 2
+    sums = got_ref[:senders].astype(F32) + got_ref[senders:].astype(F32)
+    sums_ref[...] = sums.reshape(sums_ref.shape)
+    products = [sums_ref[pl.ds(row, channels, stride=rows), :] for row in range(rows)]
+    pair = updated(products, pair_ref, gate_ref, leave_ref[1])
     copies = []
     for row in range(rows):
         out_ref[row] = jnp.transpose(pair[:, row * cols : (row + 1) * cols]).astype(BF16)
@@ -385,27 +398,26 @@
         ],
     )
 
-    def multiply(both, incoming, part):
-        (products,) = call(
-            functools.partial(product_kernel, incoming),
-            (both,),
-            [shape((devices, rows * part, cols))],
-            [pltpu.VMEM((both.size // cols, cols), F32), pltpu.VMEM((devices * rows * part, cols), F32)],
-        )
-        return exchange(products)
-
-    got = multiply(exchange(both), False, part)
+    sides = pltpu.VMEM((devices * rows * 2 * part, cols), F32)
+    (products,) = call(
+        outgoing_kernel,
+        (exchange(both),),
+        [shape((devices, rows * part, cols))],
+        [sides, pltpu.VMEM((devices * rows * part, cols), F32)],
+    )
     both, pair, gate = call(
-        middle_kernel, (got, pair, gate, trilateral_exit_matrices, entry, row_mask), projected(devices // 2)
-    )
-    halves_of = [list(range(begin, begin + devices // 2)) for begin in (0, devices // 2)]
-    both = lax.all_to_all(both, "dap", split_axis=0, concat_axis=0, tiled=True, axis_index_groups=halves_of)
-    got = multiply(both, True, 2 * part)
+        middle_kernel,
+        (exchange(products), pair, gate, trilateral_exit_matrices, entry, row_mask),
+        projected(devices // 2),
+    )
+    groups = [list(range(begin, begin + devices // 2)) for begin in (0, devices // 2)]
+    both = lax.all_to_all(both, "dap", split_axis=0, concat_axis=0, tiled=True, axis_index_groups=groups)
+    (products,) = call(incoming_kernel, (both,), [shape((devices, rows * 2 * part, cols))], [sides])
     (pair_out,) = call(
         last_kernel,
-        (got, pair, gate, trilateral_exit_matrices),
+        (exchange(products), pair, gate, trilateral_exit_matrices),
         [shape((rows, cols, channels))],
-        [pltpu.VMEM((rows, cols, channels), BF16), pltpu.SemaphoreType.DMA((rows // 4,))],
+        [pltpu.VMEM((rows, cols, channels), BF16), pltpu.VMEM((channels * rows, cols), F32), pltpu.SemaphoreType.DMA((rows // 4,))],
         out_specs=[HBM],
     )
     return pair_out

time: 84.4 us -> 84.2 us (level)
  no operation moved by 1% of the time
where the time goes in v9:
time: 84.2 us; the launch traced here: 83.8 us
  blocking collectives  75.1 us (89%)
  Pallas kernels  7.68 us (9%)
  waiting for transfers between devices  0.91 us (1%)
    all_to_all x3, blocking collectives, exchange(): lax.all_to_all(blocks, 'dap', split_axis=0, concat_axis=0, tiled=True)  48.9 us
    all_to_all x1, blocking collectives, two_level(): lax.all_to_all(blocks, 'dap', split_axis=0, concat_axis=0, tiled=True, ax...  14.9 us
    all_to_all x1, blocking collectives, fast(): lax.all_to_all(both, 'dap', split_axis=0, concat_axis=0, tiled=True, axis...  11.3 us
    pallas_call x7, Pallas kernels, call(): pl.pallas_call(kernel, out_shape=outputs, in_specs=in_specs or [VMEM] * l...  7.68 us
  transfers between devices with their start and end apart: 1, of which 1 were waited for; matrix products, arithmetic and copies ran while one was open for 0% of the time, Pallas kernels for 1%

profile of v9, /device:TPU:0, one launch (start us, length us, event | category | flops | bytes accessed | tf_op | source)
XLA Modules:
  0.0 83.8 jit_solution(13802127491979199557)
XLA Ops:
  0.0 0.0 copy-start
  0.0 0.0 copy-start.2
  0.0 2.1 %shard_map.82 = bf16[8,80,128]{2,1,0:T(8,128)(2,1)} custom-call(bf16[2,128,256]{2,1,0:T(8,128)(2,1)} %x_hbm.1, s32[2,128]{1,0:T(2,128)} %cover_hbm.1, s32[1,128]{1,0:T(1,128)} %bitcast.5, bf16[2,32,256]{2,1,0:T(8,128)(2,1)} %bitcast.4), custom_call_target="tpu_custom_call" | custom-call | tf_op jit(solution)/shard_map/pallas_call | solution.py:324
  2.1 14.9 %all_to_all.25.got_ref = bf16[8,80,128]{2,1,0:T(8,128)(2,1)S(1)} all-to-all(bf16[8,80,128]{2,1,0:T(8,128)(2,1)} %shard_map.82), channel_id=1, replica_groups={{0,2,4,6,8,10,12,14},{1,3,5,7,9,11,13,15},{16,18,20,22,24,26,28,30},{17..., dimensions={0} | all-to-all | bytes 327680 | tf_op jit(solution)/shard_map/all_to_all | solution.py:125
  17.0 0.0 collective-permute-start
  17.0 0.0 copy-done
  17.0 0.0 copy-done.2
  17.0 0.0 copy-start.3
  17.0 0.5 shard_map.83
  17.4 0.9 %collective-permute-done.other_ref = bf16[8,80,128]{2,1,0:T(8,128)(2,1)S(1)} collective-permute-done((bf16[8,80,128]{2,1,0:T(8,128)(2,1)S(1)}, bf16[8,80,128]{2,1,0:T(8,128)(2,1)S(1)}, u32[]{:S(2)}, u32[]{:S(2)}) %collective-permute-start) | collective-permute-done | bytes 163872 | tf_op jit(solution)/shard_map/ppermute | solution.py:126
  18.3 0.0 copy-done.3
  18.4 1.7 %shard_map.84 = (bf16[16,128,128]{2,1,0:T(8,128)(2,1)S(1)}, bf16[128,1024]{1,0:T(8,128)(2,1)S(1)}, f32[128,1024]{1,0:T(8,128)S(1)}, f32[8,128]{1,0:T(8,128)S(1)}) custom-call(bf16[8,80,128]{2,1,0:T(8,128)(2,1)S(1)} %all_to_all.25.got_ref, bf16[8,80,128]{2,1,0:T(8,128)(2,1)S(1)} %collective-permute-done.other_ref, bf16[8,128,128]{2,1,0:T(8,128)(2,1)S(1)} %copy-done.3, ...), custom_call_target="tpu_custom_call" | custom-call | tf_op jit(solution)/shard_map/pallas_call | solution.py:324
  20.1 17.2 %all_to_all.26.got_ref = bf16[16,128,128]{2,1,0:T(8,128)(2,1)S(1)} all-to-all(bf16[16,128,128]{2,1,0:T(8,128)(2,1)S(1)} %get-tuple-element.22), channel_id=1, replica_groups=mesh['crops'=2,'dap'=16] {'dap'}, dimensions={0} | all-to-all | bytes 1048576 | tf_op jit(solution)/shard_map/all_to_all | solution.py:40
  37.3 0.5 shard_map.85
  37.8 0.0 copy-start.1
  37.8 14.1 %all_to_all.27.got_ref = bf16[16,64,128]{2,1,0:T(8,128)(2,1)S(1)} all-to-all(bf16[16,64,128]{2,1,0:T(8,128)(2,1)S(1)} %shard_map.85), channel_id=1, replica_groups=mesh['crops'=2,'dap'=16] {'dap'}, dimensions={0} | all-to-all | bytes 524288 | tf_op jit(solution)/shard_map/all_to_all | solution.py:40
  51.8 0.0 copy-done.1
  51.8 0.9 %shard_map.86 = (bf16[8,256,128]{2,1,0:T(8,128)(2,1)S(1)}, bf16[128,1024]{1,0:T(8,128)(2,1)S(1)}, f32[128,1024]{1,0:T(8,128)S(1)}) custom-call(bf16[16,64,128]{2,1,0:T(8,128)(2,1)S(1)} %all_to_all.27.got_ref, bf16[128,1024]{1,0:T(8,128)(2,1)S(1)} %get-tuple-element.23.pair_ref, f32[128,1024]{1,0:T(8,128)S(1)} %get-tuple-element.24.gate_ref, ...), custom_call_target="tpu_custom_call" | custom-call | tf_op jit(solution)/shard_map/pallas_call | solution.py:324
  52.8 11.3 %all_to_all.28.got_ref = bf16[8,256,128]{2,1,0:T(8,128)(2,1)S(1)} all-to-all(bf16[8,256,128]{2,1,0:T(8,128)(2,1)S(1)} %get-tuple-element.26), channel_id=1, replica_groups={{0,1,2,3,4,5,6,7},{8,9,10,11,12,13,14,15},{16,17,18,19,20,21,22,23},{24..., dimensions={0} | all-to-all | bytes 1048576 | tf_op jit(solution)/shard_map/all_to_all | solution.py:414
  64.1 0.8 %shard_map.87 = bf16[16,128,128]{2,1,0:T(8,128)(2,1)S(1)} custom-call(bf16[8,256,128]{2,1,0:T(8,128)(2,1)S(1)} %all_to_all.28.got_ref), custom_call_target="tpu_custom_call" | custom-call | tf_op jit(solution)/shard_map/pallas_call | solution.py:324
  64.9 17.6 %all_to_all.29.got_ref = bf16[16,128,128]{2,1,0:T(8,128)(2,1)S(1)} all-to-all(bf16[16,128,128]{2,1,0:T(8,128)(2,1)S(1)} %shard_map.87), channel_id=1, replica_groups=mesh['crops'=2,'dap'=16] {'dap'}, dimensions={0} | all-to-all | bytes 1048576 | tf_op jit(solution)/shard_map/all_to_all | solution.py:40
  82.6 1.2 %shard_map.88 = bf16[8,128,128]{2,1,0:T(8,128)(2,1)} custom-call(bf16[16,128,128]{2,1,0:T(8,128)(2,1)S(1)} %all_to_all.29.got_ref, bf16[128,1024]{1,0:T(8,128)(2,1)S(1)} %get-tuple-element.27.pair_ref, f32[128,1024]{1,0:T(8,128)S(1)} %get-tuple-element.28.gate_ref, bf16[2,128,128]{2,1,0:T(8,128)(2,1)S(1)} %copy-done.1), custom_call_target="tpu_custom_call" | custom-call | tf_op jit(solution)/shard_map/pallas_call | solution.py:324
Async XLA Ops:
  0.0 17.0 %copy-start = (bf16[2,128,5,128]{3,1,2,0:T(8,128)(2,1)S(1)}, bf16[2,128,5,128]{3,1,2,0:T(8,128)(2,1)}, u32[]{:S(2)}) copy-start(bf16[2,128,5,128]{3,1,2,0:T(8,128)(2,1)} %param.14) | copy-start | bytes 983044
  0.0 17.0 %copy-start.2 = (bf16[1024,128]{1,0:T(8,128)(2,1)S(1)}, bf16[1024,128]{1,0:T(8,128)(2,1)}, u32[]{:S(2)}) copy-start(bf16[1024,128]{1,0:T(8,128)(2,1)} %exit_ref) | copy-start | bytes 786436
  17.0 1.4 %collective-permute-start = (bf16[8,80,128]{2,1,0:T(8,128)(2,1)S(1)}, bf16[8,80,128]{2,1,0:T(8,128)(2,1)S(1)}, u32[]{:S(2)}, u32[]{:S(2)}) collective-permute-start(bf16[8,80,128]{2,1,0:T(8,128)(2,1)S(1)} %all_to_all.25.got_ref), channel_id=1, source_target_pairs={{0,1},{1,0},{2,3},{3,2},{4,5},{5,4},{6,7},{7,6},{8,9},{9,8},{10,11... | collective-permute-start | bytes 491528 | tf_op jit(solution)/shard_map/ppermute | solution.py:126
  17.0 1.4 %copy-start.3 = (bf16[8,128,128]{2,1,0:T(8,128)(2,1)S(1)}, bf16[8,128,128]{2,1,0:T(8,128)(2,1)}, u32[]{:S(2)}) copy-start(bf16[8,128,128]{2,1,0:T(8,128)(2,1)} %couple_ref.1) | copy-start | bytes 786436
  37.8 14.1 %copy-start.1 = (bf16[2,128,128]{2,1,0:T(8,128)(2,1)S(1)}, bf16[2,128,128]{2,1,0:T(8,128)(2,1)}, u32[]{:S(2)}) copy-start(bf16[2,128,128]{2,1,0:T(8,128)(2,1)} %leave_ref.3) | copy-start | bytes 196612

commit v10 on v9

--- a/solution.py
+++ b/solution.py
@@ -113,13 +113,6 @@
     return triangle(pair_two, row_mask, trilateral_entry_matrices[1], trilateral_exit_matrices[1], True, devices)
 
 
-def start_copies(pairs, sems):
-    copies = [pltpu.make_async_copy(source, target, sems.at[at]) for at, (source, target) in enumerate(pairs)]
-    for copy in copies:
-        copy.start()
-    return copies
-
-
 def two_level(blocks, devices):
     groups = [list(range(parity, devices, 2)) for parity in range(2)]
     got = lax.all_to_all(blocks, "dap", split_axis=0, concat_axis=0, tiled=True, axis_index_groups=groups)
@@ -130,34 +123,26 @@
     return [pltpu.roll(row, LANES // 2, 1), row]
 
 
-def entry_kernel(x_hbm, cover_hbm, flag_hbm, weight_hbm, out_ref, x_ref, cover_ref, flag_ref, weight_ref, sems):
-    copies = start_copies(
-        [(x_hbm, x_ref), (weight_hbm, weight_ref), (cover_hbm, cover_ref), (flag_hbm, flag_ref)], sems
-    )
-    for copy in copies:
-        copy.wait()
-    held, cols, _ = x_ref.shape
-    width = weight_ref.shape[1]
-    pairs = out_ref.shape[0]
-    cover = cover_ref[...].astype(F32)
-    columns = jnp.transpose(jnp.concatenate([cover, jnp.zeros((8 - held, cols), F32)], axis=0))
-    blank = jnp.zeros_like(weight_ref[0])
-    own = jnp.zeros((cols, LANES), F32)
+def entry_kernel(all_ref, out_ref):
+    pairs, _, cols = out_ref.shape
+    held, width = 2, 32
+    lines = held * cols
+    normalized = norm(all_ref[:lines].astype(F32), -1)
+    flags = all_ref[lines + 2 * width :, :cols].astype(F32)
+    cover = flags[:held]
+    entries = dot(all_ref[lines : lines + 2 * width], normalized, 1, 1) * flat(cover)
+    entries = [entries[:, s * cols : (s + 1) * cols] for s in range(held)]
+    shared = jnp.concatenate([values[width:] for values in entries], axis=0).astype(BF16)
+    blank = jnp.zeros((LANES - held * width, cols), F32)
+    own = jnp.transpose(jnp.concatenate([values[:width] for values in entries] + [blank], axis=0))
     marks = []
-    for s in range(held):
-        marks += halves(cover[s : s + 1])
-    marks += halves(flag_ref[...].astype(F32))
+    for row in range(held + 1):
+        marks += halves(flags[row : row + 1])
     marks = jnp.concatenate(marks + [jnp.zeros((8 - len(marks), cols), F32)], axis=0)
-    for s in range(held):
-        normalized = norm(x_ref[s].astype(F32), -1)
-        shared = (dot(weight_ref[1], normalized, 1, 1) * cover[s : s + 1]).astype(BF16)
-        for pair in range(pairs):
-            out_ref[pair, s * width : (s + 1) * width, :] = shared
-        weight = jnp.concatenate([weight_ref[0] if at == s else blank for at in range(LANES // width)], axis=0)
-        own = own + dot(normalized, weight, 1, 1) * columns[:, s : s + 1]
+    marks = jnp.concatenate([marks, marks], axis=0)
     lane = lax.broadcasted_iota(jnp.int32, (16, LANES), 1)
-    marks = jnp.concatenate([marks, marks], axis=0)
     for pair in range(pairs):
+        out_ref[pair, : held * width, :] = shared
         block = jnp.where(lane < held * width, own[pair * 16 : pair * 16 + 16], marks)
         out_ref[pair, held * width :, :] = block.astype(BF16)
 
@@ -294,9 +279,10 @@
 def middle_kernel(got_ref, pair_ref, gate_ref, leave_ref, weight_ref, mask_ref, out_ref, next_ref, next_gate_ref):
     devices, size, cols = got_ref.shape
     part = size // mask_ref.shape[0]
-    products = [
-        got_ref[:, at : at + part, :].astype(F32).reshape(devices * part, cols) for at in range(0, size, part)
-    ]
+    products = []
+    for at in range(0, size, 2 * part):
+        lines = got_ref[:, at : at + 2 * part, :].astype(F32)
+        products += [values.reshape(devices * part, cols) for values in (lines[:, :part], lines[:, part:])]
     pair = updated(products, pair_ref, gate_ref, leave_ref[0]).astype(BF16)
     next_ref[...] = pair
     project(pair.astype(F32), weight_ref[1], mask_ref, out_ref, next_gate_ref)
@@ -320,14 +306,14 @@
         copy.wait()
 
 
-def call(kernel, inputs, outputs, scratch=(), in_specs=None, out_specs=None, limit=40):
+def call(kernel, inputs, outputs, scratch=(), in_specs=None, out_specs=None):
     return pl.pallas_call(
         kernel,
         out_shape=outputs,
         in_specs=in_specs or [VMEM] * len(inputs),
         out_specs=out_specs or [VMEM] * len(outputs),
         scratch_shapes=list(scratch),
-        compiler_params=pltpu.CompilerParams(vmem_limit_bytes=limit * 1024 * 1024),
+        compiler_params=pltpu.CompilerParams(vmem_limit_bytes=40 * 1024 * 1024),
     )(*inputs)
 
 
@@ -350,25 +336,18 @@
     held = homolog_embedding.shape[0]
     width = pairing_entry_matrices.shape[2]
     part = channels // devices
-    (packed,) = call(
-        entry_kernel,
-        (
-            homolog_embedding,
-            coverage_indicator,
-            genuine_amino_flag.reshape(1, cols),
-            jnp.transpose(pairing_entry_matrices, (1, 2, 0)),
-        ),
-        [shape((devices // 2, held * width + 16, cols))],
+    depth = homolog_embedding.shape[2]
+    flags = jnp.concatenate([coverage_indicator, genuine_amino_flag.reshape(1, cols)], axis=0)
+    flags = jnp.pad(flags, ((0, 16 - held - 1), (0, depth - cols))).astype(BF16)
+    everything = jnp.concatenate(
         [
-            pltpu.VMEM(homolog_embedding.shape, BF16),
-            pltpu.VMEM(coverage_indicator.shape, jnp.int32),
-            pltpu.VMEM((1, cols), jnp.int32),
-            pltpu.VMEM((2, width, homolog_embedding.shape[2]), BF16),
-            pltpu.SemaphoreType.DMA((4,)),
+            homolog_embedding.reshape(held * cols, depth),
+            jnp.transpose(pairing_entry_matrices, (1, 2, 0)).reshape(2 * width, depth),
+            flags,
         ],
-        [HBM] * 4,
-        limit=60,
-    )
+        axis=0,
+    )
+    (packed,) = call(entry_kernel, (everything,), [shape((devices // 2, held * width + 16, cols))])
     packed, entry, exit_rows = lax.optimization_barrier((packed, trilateral_entry_matrices, pairing_exit_matrix))
     got = two_level(packed, devices)
     entry, exit_matrix = call(
@@ -433,6 +412,7 @@
         and channels == 8 * devices
         and channels == LANES
         and pairing_entry_matrices.shape[2] == 32
+        and homolog_embedding.shape[2] >= cols
     )
 
 

time: 84.2 us -> 84 us (level)
  other arithmetic: 0 us -> 1.65 us
  Pallas kernels: 7.68 us -> 6.06 us
    pallas_call x7, Pallas kernels: 7.68 us -> 6.06 us  [call(): pl.pallas_call(kernel, out_shape=outputs, in_specs=in_specs or [VMEM] * l...]
    concatenate x0 -> x2, other arithmetic: none -> 0.95 us  [the longest x1 0.94 us: fast(): jnp.concatenate([homolog_embedding.reshape(held * cols, depth), jnp.trans...]
where the time goes in v10:
time: 84 us; the launch traced here: 83.6 us
  blocking collectives  74.9 us (89%)
  Pallas kernels  6.06 us (7%)
  other arithmetic  1.65 us (2%)
  waiting for transfers between devices  0.91 us (1%)
    all_to_all x3, blocking collectives, exchange(): lax.all_to_all(blocks, 'dap', split_axis=0, concat_axis=0, tiled=True)  48.9 us
    all_to_all x1, blocking collectives, two_level(): lax.all_to_all(blocks, 'dap', split_axis=0, concat_axis=0, tiled=True, ax...  14.6 us
    all_to_all x1, blocking collectives, fast(): lax.all_to_all(both, 'dap', split_axis=0, concat_axis=0, tiled=True, axis...  11.3 us
    pallas_call x7, Pallas kernels, call(): pl.pallas_call(kernel, out_shape=outputs, in_specs=in_specs or [VMEM] * l...  6.06 us
  transfers between devices with their start and end apart: 1, of which 1 were waited for; matrix products, arithmetic and copies ran while one was open for 0% of the time, Pallas kernels for 1%

profile of v10, /device:TPU:0, one launch (start us, length us, event | category | flops | bytes accessed | tf_op | source)
XLA Modules:
  0.0 83.6 jit_solution(13172836300704772199)
XLA Ops:
  0.0 0.0 copy-start.4
  0.0 0.7 convert.9
  0.7 0.0 copy-done.4
  0.7 0.9 %pad_maximum_fusion.all_ref = bf16[336,256]{1,0:T(8,128)(2,1)S(1)} fusion(bf16[16,256]{1,0:T(8,128)(2,1)S(1)} %fusion.5, bf16[64,256]{1,0:T(8,128)(2,1)} %bitcast.9, bf16[256,256]{1,0:T(8,128)(2,1)} %bitcast.8), kind=kLoop, calls=%fused_computation | loop fusion | flops 516096 | bytes 344064 | tf_op jit(solution)/shard_map/concatenate | solution.py:342
  1.7 0.0 copy-start
  1.7 0.0 copy-start.2
  1.7 0.5 shard_map.82
  2.2 14.6 %all_to_all.25.got_ref = bf16[8,80,128]{2,1,0:T(8,128)(2,1)S(1)} all-to-all(bf16[8,80,128]{2,1,0:T(8,128)(2,1)S(1)} %shard_map.82), channel_id=1, replica_groups={{0,2,4,6,8,10,12,14},{1,3,5,7,9,11,13,15},{16,18,20,22,24,26,28,30},{17..., dimensions={0} | all-to-all | bytes 327680 | tf_op jit(solution)/shard_map/all_to_all | solution.py:118
  16.8 0.0 collective-permute-start
  16.8 0.0 copy-done
  16.8 0.0 copy-done.2
  16.8 0.0 copy-start.3
  16.8 0.5 shard_map.83
  17.3 0.9 %collective-permute-done.other_ref = bf16[8,80,128]{2,1,0:T(8,128)(2,1)S(1)} collective-permute-done((bf16[8,80,128]{2,1,0:T(8,128)(2,1)S(1)}, bf16[8,80,128]{2,1,0:T(8,128)(2,1)S(1)}, u32[]{:S(2)}, u32[]{:S(2)}) %collective-permute-start) | collective-permute-done | bytes 163872 | tf_op jit(solution)/shard_map/ppermute | solution.py:119
  18.2 0.0 copy-done.3
  18.2 1.7 %shard_map.84 = (bf16[16,128,128]{2,1,0:T(8,128)(2,1)S(1)}, bf16[128,1024]{1,0:T(8,128)(2,1)S(1)}, f32[128,1024]{1,0:T(8,128)S(1)}, f32[8,128]{1,0:T(8,128)S(1)}) custom-call(bf16[8,80,128]{2,1,0:T(8,128)(2,1)S(1)} %all_to_all.25.got_ref, bf16[8,80,128]{2,1,0:T(8,128)(2,1)S(1)} %collective-permute-done.other_ref, bf16[8,128,128]{2,1,0:T(8,128)(2,1)S(1)} %copy-done.3, ...), custom_call_target="tpu_custom_call" | custom-call | tf_op jit(solution)/shard_map/pallas_call | solution.py:310
  19.9 17.2 %all_to_all.26.got_ref = bf16[16,128,128]{2,1,0:T(8,128)(2,1)S(1)} all-to-all(bf16[16,128,128]{2,1,0:T(8,128)(2,1)S(1)} %get-tuple-element.22), channel_id=1, replica_groups=mesh['crops'=2,'dap'=16] {'dap'}, dimensions={0} | all-to-all | bytes 1048576 | tf_op jit(solution)/shard_map/all_to_all | solution.py:40
  37.1 0.5 shard_map.85
  37.6 0.0 copy-start.1
  37.6 14.1 %all_to_all.27.got_ref = bf16[16,64,128]{2,1,0:T(8,128)(2,1)S(1)} all-to-all(bf16[16,64,128]{2,1,0:T(8,128)(2,1)S(1)} %shard_map.85), channel_id=1, replica_groups=mesh['crops'=2,'dap'=16] {'dap'}, dimensions={0} | all-to-all | bytes 524288 | tf_op jit(solution)/shard_map/all_to_all | solution.py:40
  51.7 0.0 copy-done.1
  51.7 0.9 %shard_map.86 = (bf16[8,256,128]{2,1,0:T(8,128)(2,1)S(1)}, bf16[128,1024]{1,0:T(8,128)(2,1)S(1)}, f32[128,1024]{1,0:T(8,128)S(1)}) custom-call(bf16[16,64,128]{2,1,0:T(8,128)(2,1)S(1)} %all_to_all.27.got_ref, bf16[128,1024]{1,0:T(8,128)(2,1)S(1)} %get-tuple-element.23.pair_ref, f32[128,1024]{1,0:T(8,128)S(1)} %get-tuple-element.24.gate_ref, ...), custom_call_target="tpu_custom_call" | custom-call | tf_op jit(solution)/shard_map/pallas_call | solution.py:310
  52.6 11.3 %all_to_all.28.got_ref = bf16[8,256,128]{2,1,0:T(8,128)(2,1)S(1)} all-to-all(bf16[8,256,128]{2,1,0:T(8,128)(2,1)S(1)} %get-tuple-element.26), channel_id=1, replica_groups={{0,1,2,3,4,5,6,7},{8,9,10,11,12,13,14,15},{16,17,18,19,20,21,22,23},{24..., dimensions={0} | all-to-all | bytes 1048576 | tf_op jit(solution)/shard_map/all_to_all | solution.py:393
  63.9 0.8 %shard_map.87 = bf16[16,128,128]{2,1,0:T(8,128)(2,1)S(1)} custom-call(bf16[8,256,128]{2,1,0:T(8,128)(2,1)S(1)} %all_to_all.28.got_ref), custom_call_target="tpu_custom_call" | custom-call | tf_op jit(solution)/shard_map/pallas_call | solution.py:310
  64.8 17.6 %all_to_all.29.got_ref = bf16[16,128,128]{2,1,0:T(8,128)(2,1)S(1)} all-to-all(bf16[16,128,128]{2,1,0:T(8,128)(2,1)S(1)} %shard_map.87), channel_id=1, replica_groups=mesh['crops'=2,'dap'=16] {'dap'}, dimensions={0} | all-to-all | bytes 1048576 | tf_op jit(solution)/shard_map/all_to_all | solution.py:40
  82.4 1.2 %shard_map.88 = bf16[8,128,128]{2,1,0:T(8,128)(2,1)} custom-call(bf16[16,128,128]{2,1,0:T(8,128)(2,1)S(1)} %all_to_all.29.got_ref, bf16[128,1024]{1,0:T(8,128)(2,1)S(1)} %get-tuple-element.27.pair_ref, f32[128,1024]{1,0:T(8,128)S(1)} %get-tuple-element.28.gate_ref, bf16[2,128,128]{2,1,0:T(8,128)(2,1)S(1)} %copy-done.1), custom_call_target="tpu_custom_call" | custom-call | tf_op jit(solution)/shard_map/pallas_call | solution.py:310
  (2 shorter events, 0.0 us)
Async XLA Ops:
  0.0 0.7 copy-start.4
  1.7 15.2 %copy-start = (bf16[2,128,5,128]{3,1,2,0:T(8,128)(2,1)S(1)}, bf16[2,128,5,128]{3,1,2,0:T(8,128)(2,1)}, u32[]{:S(2)}) copy-start(bf16[2,128,5,128]{3,1,2,0:T(8,128)(2,1)} %param.14) | copy-start | bytes 983044
  1.7 15.1 %copy-start.2 = (bf16[1024,128]{1,0:T(8,128)(2,1)S(1)}, bf16[1024,128]{1,0:T(8,128)(2,1)}, u32[]{:S(2)}) copy-start(bf16[1024,128]{1,0:T(8,128)(2,1)} %exit_ref) | copy-start | bytes 786436
  16.8 1.4 %collective-permute-start = (bf16[8,80,128]{2,1,0:T(8,128)(2,1)S(1)}, bf16[8,80,128]{2,1,0:T(8,128)(2,1)S(1)}, u32[]{:S(2)}, u32[]{:S(2)}) collective-permute-start(bf16[8,80,128]{2,1,0:T(8,128)(2,1)S(1)} %all_to_all.25.got_ref), channel_id=1, source_target_pairs={{0,1},{1,0},{2,3},{3,2},{4,5},{5,4},{6,7},{7,6},{8,9},{9,8},{10,11... | collective-permute-start | bytes 491528 | tf_op jit(solution)/shard_map/ppermute | solution.py:119
  16.8 1.4 %copy-start.3 = (bf16[8,128,128]{2,1,0:T(8,128)(2,1)S(1)}, bf16[8,128,128]{2,1,0:T(8,128)(2,1)}, u32[]{:S(2)}) copy-start(bf16[8,128,128]{2,1,0:T(8,128)(2,1)} %couple_ref.1) | copy-start | bytes 786436
  37.6 14.1 %copy-start.1 = (bf16[2,128,128]{2,1,0:T(8,128)(2,1)S(1)}, bf16[2,128,128]{2,1,0:T(8,128)(2,1)}, u32[]{:S(2)}) copy-start(bf16[2,128,128]{2,1,0:T(8,128)(2,1)} %leave_ref.3) | copy-start | bytes 196612

commit v11 on v10

--- a/solution.py
+++ b/solution.py
@@ -9,6 +9,7 @@
 BF16 = jnp.bfloat16
 EPS = 1e-05
 LANES = 128
+GAP = 8
 VMEM = pl.BlockSpec(memory_space=pltpu.VMEM)
 HBM = pl.BlockSpec(memory_space=pltpu.HBM)
 
@@ -119,6 +120,14 @@
     return got, lax.ppermute(got, "dap", [(at, at ^ 1) for at in range(devices)])
 
 
+def spread(blocks, target_ref, first=0):
+    count, rows, _ = blocks.shape
+    for at in range(count):
+        begin = (first + at) * (rows + GAP)
+        target_ref[begin : begin + rows, :] = blocks[at]
+    return rows + GAP
+
+
 def halves(row):
     return [pltpu.roll(row, LANES // 2, 1), row]
 
@@ -172,8 +181,8 @@
         for k in range(entry_ref.shape[1]):
             out_entry[t, k * LANES : (k + 1) * LANES, :] = jnp.transpose(entry_ref[t, k])
     width = 32
-    rows_ref[...] = exit_ref[...].astype(F32)
-    leave = jnp.concatenate([rows_ref[pl.ds(e, width, stride=width), :] for e in range(width)], axis=0)
+    step = spread(exit_ref[...].astype(F32).reshape(width, width, LANES), rows_ref)
+    leave = jnp.concatenate([rows_ref[pl.ds(e, width, stride=step), :] for e in range(width)], axis=0)
     out_exit[...] = jnp.transpose(leave).astype(BF16)
 
 
@@ -188,8 +197,7 @@
     held, width = 2, 32
     core = lax.rem(lax.axis_index("dap"), 2)
     for side, ref in enumerate((got_ref, other_ref)):
-        shared = ref[:, : held * width, :].astype(F32).reshape(pairs * held * width, cols)
-        shared_ref[side * pairs * held * width : (side + 1) * pairs * held * width, :] = shared
+        step = spread(ref[:, : held * width, :].astype(F32), shared_ref, side * pairs)
         aux = ref[:, held * width :, :].astype(F32)
         aux = jnp.where(core == 0, aux[:, :8], aux[:, 8:])
         aux_ref[side * pairs * 8 : (side + 1) * pairs * 8, :] = aux.reshape(pairs * 8, cols)
@@ -222,21 +230,21 @@
     own = jnp.transpose(jnp.concatenate(tiles, axis=1)).astype(BF16)
     for e in range(0, width, 2):
         parts = []
-        for step in range(2):
+        for more in range(2):
             parts.append(
                 jnp.concatenate(
                     [
-                        shared_ref[pl.ds(s * width + e + step, devices, stride=held * width), :]
+                        shared_ref[pl.ds(s * width + e + more, devices, stride=step), :]
                         for s in range(held)
                     ],
                     axis=0,
                 )
             )
         result = dot(own, jnp.concatenate(parts, axis=1).astype(BF16)).astype(BF16)
-        for step in range(2):
+        for more in range(2):
             for i in range(rows):
-                outer_ref[(e + step) * width : (e + step + 1) * width, i * cols : (i + 1) * cols] = result[
-                    i * width : (i + 1) * width, step * cols : (step + 1) * cols
+                outer_ref[(e + more) * width : (e + more + 1) * width, i * cols : (i + 1) * cols] = result[
+                    i * width : (i + 1) * width, more * cols : (more + 1) * cols
                 ]
     couple = jnp.concatenate([jnp.transpose(couple_ref[row]) for row in range(rows)], axis=1)
     pair = (couple.astype(F32) + dot(exit_ref[...], outer_ref[...]) * flat(scale)).astype(BF16)
@@ -245,9 +253,9 @@
 
 
 def side_rows(got_ref, sides_ref, part):
-    sides_ref[...] = got_ref[...].astype(F32).reshape(sides_ref.shape)
-    lines = sides_ref.shape[0] // (2 * part)
-    return lambda h: sides_ref[pl.ds(h, lines, stride=2 * part), :].astype(BF16)
+    lines = got_ref.shape[0] * got_ref.shape[1] // (2 * part)
+    step = spread(got_ref[...].astype(F32).reshape(lines, 2 * part, got_ref.shape[2]), sides_ref)
+    return lambda h: sides_ref[pl.ds(h, lines, stride=step), :].astype(BF16)
 
 
 def outgoing_kernel(got_ref, out_ref, sides_ref, products_ref):
@@ -357,7 +365,7 @@
             shape((2, 5 * channels, channels)),
             shape((channels, width * width)),
         ],
-        [pltpu.VMEM((width * width, channels), F32)],
+        [pltpu.VMEM((width * (width + GAP), channels), F32)],
     )
     def projected(peers):
         return [
@@ -371,13 +379,13 @@
         (*got, couple_embedding, exit_matrix, entry),
         projected(devices) + [shape((rows, cols), F32)],
         [
-            pltpu.VMEM((devices * held * width, cols), F32),
+            pltpu.VMEM((devices * (held * width + GAP), cols), F32),
             pltpu.VMEM((devices * 8, cols), F32),
             pltpu.VMEM((width * width, rows * cols), BF16),
         ],
     )
 
-    sides = pltpu.VMEM((devices * rows * 2 * part, cols), F32)
+    sides = pltpu.VMEM((devices * rows * (2 * part + GAP), cols), F32)
     (products,) = call(
         outgoing_kernel,
         (exchange(both),),

time: 84 us -> 83.3 us (level)
  Pallas kernels: 6.06 us -> 5.21 us
    pallas_call x7, Pallas kernels: 6.06 us -> 5.21 us  [call(): pl.pallas_call(kernel, out_shape=outputs, in_specs=in_specs or [VMEM] * l...]
  transfers between devices with their start and end apart: 1 -> 1, of which waited for: 1 -> 1; matrix products, arithmetic and copies ran while one was open for 0% -> 0% of each run, Pallas kernels for 1% -> 0%
where the time goes in v11:
time: 83.3 us; the launch traced here: 83 us
  blocking collectives  74.9 us (90%)
  Pallas kernels  5.21 us (6%)
  other arithmetic  1.65 us (2%)
  waiting for transfers between devices  1.12 us (1%)
    all_to_all x3, blocking collectives, exchange(): lax.all_to_all(blocks, 'dap', split_axis=0, concat_axis=0, tiled=True)  48.9 us
    all_to_all x1, blocking collectives, two_level(): lax.all_to_all(blocks, 'dap', split_axis=0, concat_axis=0, tiled=True, ax...  14.6 us
    all_to_all x1, blocking collectives, fast(): lax.all_to_all(both, 'dap', split_axis=0, concat_axis=0, tiled=True, axis...  11.3 us
    pallas_call x7, Pallas kernels, call(): pl.pallas_call(kernel, out_shape=outputs, in_specs=in_specs or [VMEM] * l...  5.21 us
  transfers between devices with their start and end apart: 1, of which 1 were waited for; matrix products, arithmetic and copies ran while one was open for 0% of the time, Pallas kernels for 0%

profile of v11, /device:TPU:0, one launch (start us, length us, event | category | flops | bytes accessed | tf_op | source)
XLA Modules:
  0.0 83.0 jit_solution(7958920717174771610)
XLA Ops:
  0.0 0.0 copy-start.4
  0.0 0.7 convert.9
  0.7 0.0 copy-done.4
  0.7 0.9 %pad_maximum_fusion.all_ref = bf16[336,256]{1,0:T(8,128)(2,1)S(1)} fusion(bf16[16,256]{1,0:T(8,128)(2,1)S(1)} %fusion.5, bf16[64,256]{1,0:T(8,128)(2,1)} %bitcast.9, bf16[256,256]{1,0:T(8,128)(2,1)} %bitcast.8), kind=kLoop, calls=%fused_computation | loop fusion | flops 516096 | bytes 344064 | tf_op jit(solution)/shard_map/concatenate | solution.py:350
  1.7 0.0 copy-start
  1.7 0.0 copy-start.2
  1.7 0.5 shard_map.82
  2.2 14.6 %all_to_all.25.got_ref = bf16[8,80,128]{2,1,0:T(8,128)(2,1)S(1)} all-to-all(bf16[8,80,128]{2,1,0:T(8,128)(2,1)S(1)} %shard_map.82), channel_id=1, replica_groups={{0,2,4,6,8,10,12,14},{1,3,5,7,9,11,13,15},{16,18,20,22,24,26,28,30},{17..., dimensions={0} | all-to-all | bytes 327680 | tf_op jit(solution)/shard_map/all_to_all | solution.py:119
  16.8 0.0 collective-permute-start
  16.8 0.0 copy-done
  16.8 0.0 copy-done.2
  16.8 0.0 copy-start.3
  16.8 0.2 shard_map.83
  17.1 1.1 %collective-permute-done.other_ref = bf16[8,80,128]{2,1,0:T(8,128)(2,1)S(1)} collective-permute-done((bf16[8,80,128]{2,1,0:T(8,128)(2,1)S(1)}, bf16[8,80,128]{2,1,0:T(8,128)(2,1)S(1)}, u32[]{:S(2)}, u32[]{:S(2)}) %collective-permute-start) | collective-permute-done | bytes 163872 | tf_op jit(solution)/shard_map/ppermute | solution.py:120
  18.2 0.0 copy-done.3
  18.2 1.6 %shard_map.84 = (bf16[16,128,128]{2,1,0:T(8,128)(2,1)S(1)}, bf16[128,1024]{1,0:T(8,128)(2,1)S(1)}, f32[128,1024]{1,0:T(8,128)S(1)}, f32[8,128]{1,0:T(8,128)S(1)}) custom-call(bf16[8,80,128]{2,1,0:T(8,128)(2,1)S(1)} %all_to_all.25.got_ref, bf16[8,80,128]{2,1,0:T(8,128)(2,1)S(1)} %collective-permute-done.other_ref, bf16[8,128,128]{2,1,0:T(8,128)(2,1)S(1)} %copy-done.3, ...), custom_call_target="tpu_custom_call" | custom-call | tf_op jit(solution)/shard_map/pallas_call | solution.py:318
  19.9 17.2 %all_to_all.26.got_ref = bf16[16,128,128]{2,1,0:T(8,128)(2,1)S(1)} all-to-all(bf16[16,128,128]{2,1,0:T(8,128)(2,1)S(1)} %get-tuple-element.22), channel_id=1, replica_groups=mesh['crops'=2,'dap'=16] {'dap'}, dimensions={0} | all-to-all | bytes 1048576 | tf_op jit(solution)/shard_map/all_to_all | solution.py:41
  37.1 0.4 shard_map.85
  37.4 0.0 copy-start.1
  37.4 14.1 %all_to_all.27.got_ref = bf16[16,64,128]{2,1,0:T(8,128)(2,1)S(1)} all-to-all(bf16[16,64,128]{2,1,0:T(8,128)(2,1)S(1)} %shard_map.85), channel_id=1, replica_groups=mesh['crops'=2,'dap'=16] {'dap'}, dimensions={0} | all-to-all | bytes 524288 | tf_op jit(solution)/shard_map/all_to_all | solution.py:41
  51.5 0.0 copy-done.1
  51.5 0.9 %shard_map.86 = (bf16[8,256,128]{2,1,0:T(8,128)(2,1)S(1)}, bf16[128,1024]{1,0:T(8,128)(2,1)S(1)}, f32[128,1024]{1,0:T(8,128)S(1)}) custom-call(bf16[16,64,128]{2,1,0:T(8,128)(2,1)S(1)} %all_to_all.27.got_ref, bf16[128,1024]{1,0:T(8,128)(2,1)S(1)} %get-tuple-element.23.pair_ref, f32[128,1024]{1,0:T(8,128)S(1)} %get-tuple-element.24.gate_ref, ...), custom_call_target="tpu_custom_call" | custom-call | tf_op jit(solution)/shard_map/pallas_call | solution.py:318
  52.5 11.3 %all_to_all.28.got_ref = bf16[8,256,128]{2,1,0:T(8,128)(2,1)S(1)} all-to-all(bf16[8,256,128]{2,1,0:T(8,128)(2,1)S(1)} %get-tuple-element.26), channel_id=1, replica_groups={{0,1,2,3,4,5,6,7},{8,9,10,11,12,13,14,15},{16,17,18,19,20,21,22,23},{24..., dimensions={0} | all-to-all | bytes 1048576 | tf_op jit(solution)/shard_map/all_to_all | solution.py:401
  63.8 0.4 shard_map.87
  64.2 17.6 %all_to_all.29.got_ref = bf16[16,128,128]{2,1,0:T(8,128)(2,1)S(1)} all-to-all(bf16[16,128,128]{2,1,0:T(8,128)(2,1)S(1)} %shard_map.87), channel_id=1, replica_groups=mesh['crops'=2,'dap'=16] {'dap'}, dimensions={0} | all-to-all | bytes 1048576 | tf_op jit(solution)/shard_map/all_to_all | solution.py:41
  81.8 1.2 %shard_map.88 = bf16[8,128,128]{2,1,0:T(8,128)(2,1)} custom-call(bf16[16,128,128]{2,1,0:T(8,128)(2,1)S(1)} %all_to_all.29.got_ref, bf16[128,1024]{1,0:T(8,128)(2,1)S(1)} %get-tuple-element.27.pair_ref, f32[128,1024]{1,0:T(8,128)S(1)} %get-tuple-element.28.gate_ref, bf16[2,128,128]{2,1,0:T(8,128)(2,1)S(1)} %copy-done.1), custom_call_target="tpu_custom_call" | custom-call | tf_op jit(solution)/shard_map/pallas_call | solution.py:318
  (2 shorter events, 0.0 us)
Async XLA Ops:
  0.0 0.7 copy-start.4
  1.7 15.2 %copy-start = (bf16[2,128,5,128]{3,1,2,0:T(8,128)(2,1)S(1)}, bf16[2,128,5,128]{3,1,2,0:T(8,128)(2,1)}, u32[]{:S(2)}) copy-start(bf16[2,128,5,128]{3,1,2,0:T(8,128)(2,1)} %param.14) | copy-start | bytes 983044
  1.7 15.1 %copy-start.2 = (bf16[1024,128]{1,0:T(8,128)(2,1)S(1)}, bf16[1024,128]{1,0:T(8,128)(2,1)}, u32[]{:S(2)}) copy-start(bf16[1024,128]{1,0:T(8,128)(2,1)} %exit_ref) | copy-start | bytes 786436
  16.8 1.4 %collective-permute-start = (bf16[8,80,128]{2,1,0:T(8,128)(2,1)S(1)}, bf16[8,80,128]{2,1,0:T(8,128)(2,1)S(1)}, u32[]{:S(2)}, u32[]{:S(2)}) collective-permute-start(bf16[8,80,128]{2,1,0:T(8,128)(2,1)S(1)} %all_to_all.25.got_ref), channel_id=1, source_target_pairs={{0,1},{1,0},{2,3},{3,2},{4,5},{5,4},{6,7},{7,6},{8,9},{9,8},{10,11... | collective-permute-start | bytes 491528 | tf_op jit(solution)/shard_map/ppermute | solution.py:120
  16.8 1.4 %copy-start.3 = (bf16[8,128,128]{2,1,0:T(8,128)(2,1)S(1)}, bf16[8,128,128]{2,1,0:T(8,128)(2,1)}, u32[]{:S(2)}) copy-start(bf16[8,128,128]{2,1,0:T(8,128)(2,1)} %couple_ref.1) | copy-start | bytes 786436
  37.4 14.1 %copy-start.1 = (bf16[2,128,128]{2,1,0:T(8,128)(2,1)S(1)}, bf16[2,128,128]{2,1,0:T(8,128)(2,1)}, u32[]{:S(2)}) copy-start(bf16[2,128,128]{2,1,0:T(8,128)(2,1)} %leave_ref.3) | copy-start | bytes 196612

commit v12 on v11

--- a/solution.py
+++ b/solution.py
@@ -133,13 +133,16 @@
 
 
 def entry_kernel(all_ref, out_ref):
+    lines = all_ref.shape[0] - out_ref.shape[0]
+    out_ref[...] = dot(all_ref[lines:], norm(all_ref[:lines].astype(F32), -1), 1, 1)
+
+
+def pack_kernel(entries_ref, cover_ref, flag_ref, out_ref):
     pairs, _, cols = out_ref.shape
     held, width = 2, 32
-    lines = held * cols
-    normalized = norm(all_ref[:lines].astype(F32), -1)
-    flags = all_ref[lines + 2 * width :, :cols].astype(F32)
-    cover = flags[:held]
-    entries = dot(all_ref[lines : lines + 2 * width], normalized, 1, 1) * flat(cover)
+    cover = cover_ref[...].astype(F32)
+    flags = jnp.concatenate([cover, flag_ref[...].astype(F32)], axis=0)
+    entries = entries_ref[...] * flat(cover)
     entries = [entries[:, s * cols : (s + 1) * cols] for s in range(held)]
     shared = jnp.concatenate([values[width:] for values in entries], axis=0).astype(BF16)
     blank = jnp.zeros((LANES - held * width, cols), F32)
@@ -345,17 +348,19 @@
     width = pairing_entry_matrices.shape[2]
     part = channels // devices
     depth = homolog_embedding.shape[2]
-    flags = jnp.concatenate([coverage_indicator, genuine_amino_flag.reshape(1, cols)], axis=0)
-    flags = jnp.pad(flags, ((0, 16 - held - 1), (0, depth - cols))).astype(BF16)
     everything = jnp.concatenate(
         [
             homolog_embedding.reshape(held * cols, depth),
             jnp.transpose(pairing_entry_matrices, (1, 2, 0)).reshape(2 * width, depth),
-            flags,
         ],
         axis=0,
     )
-    (packed,) = call(entry_kernel, (everything,), [shape((devices // 2, held * width + 16, cols))])
+    (entries,) = call(entry_kernel, (everything,), [shape((2 * width, held * cols), F32)])
+    (packed,) = call(
+        pack_kernel,
+        (entries, coverage_indicator, genuine_amino_flag.reshape(1, cols)),
+        [shape((devices // 2, held * width + 16, cols))],
+    )
     packed, entry, exit_rows = lax.optimization_barrier((packed, trilateral_entry_matrices, pairing_exit_matrix))
     got = two_level(packed, devices)
     entry, exit_matrix = call(

time: 83.3 us -> 82.7 us (level)
    pallas_call x7 -> x8, Pallas kernels: 5.21 us -> 5.22 us  [call(): pl.pallas_call(kernel, out_shape=outputs, in_specs=in_specs or [VMEM] * l...]
where the time goes in v12:
time: 82.7 us; the launch traced here: 82.3 us
  blocking collectives  74.9 us (91%)
  Pallas kernels  5.22 us (6%)
  waiting for transfers between devices  1.12 us (1%)
  other arithmetic  0.96 us (1%)
    all_to_all x3, blocking collectives, exchange(): lax.all_to_all(blocks, 'dap', split_axis=0, concat_axis=0, tiled=True)  48.9 us
    all_to_all x1, blocking collectives, two_level(): lax.all_to_all(blocks, 'dap', split_axis=0, concat_axis=0, tiled=True, ax...  14.6 us
    all_to_all x1, blocking collectives, fast(): lax.all_to_all(both, 'dap', split_axis=0, concat_axis=0, tiled=True, axis...  11.3 us
    pallas_call x8, Pallas kernels, call(): pl.pallas_call(kernel, out_shape=outputs, in_specs=in_specs or [VMEM] * l...  5.22 us
  transfers between devices with their start and end apart: 1, of which 1 were waited for; matrix products, arithmetic and copies ran while one was open for 0% of the time, Pallas kernels for 0%

profile of v12, /device:TPU:0, one launch (start us, length us, event | category | flops | bytes accessed | tf_op | source)
XLA Modules:
  0.0 82.3 jit_solution(16599845085349274140)
XLA Ops:
  0.0 0.0 copy-start.4
  0.0 0.0 copy-start.5
  0.0 1.0 %pad_maximum_fusion.all_ref = bf16[320,256]{1,0:T(8,128)(2,1)S(1)} fusion(bf16[64,256]{1,0:T(8,128)(2,1)} %bitcast.9, bf16[256,256]{1,0:T(8,128)(2,1)} %bitcast.8), kind=kLoop, calls=%fused_computation | loop fusion | flops 327680 | bytes 327680 | tf_op jit(solution)/shard_map/concatenate | solution.py:351
  1.0 0.0 copy-start.2
  1.0 0.4 shard_map.82.entries_ref
  1.4 0.0 copy-start
  1.4 0.0 copy-done.4
  1.4 0.0 copy-done.5
  1.4 0.1 shard_map.83
  1.5 14.6 %all_to_all.25.got_ref = bf16[8,80,128]{2,1,0:T(8,128)(2,1)S(1)} all-to-all(bf16[8,80,128]{2,1,0:T(8,128)(2,1)S(1)} %shard_map.83), channel_id=1, replica_groups={{0,2,4,6,8,10,12,14},{1,3,5,7,9,11,13,15},{16,18,20,22,24,26,28,30},{17..., dimensions={0} | all-to-all | bytes 327680 | tf_op jit(solution)/shard_map/all_to_all | solution.py:119
  16.1 0.0 collective-permute-start
  16.1 0.0 copy-done.2
  16.1 0.0 copy-done
  16.1 0.0 copy-start.3
  16.2 0.2 shard_map.84
  16.4 1.1 %collective-permute-done.other_ref = bf16[8,80,128]{2,1,0:T(8,128)(2,1)S(1)} collective-permute-done((bf16[8,80,128]{2,1,0:T(8,128)(2,1)S(1)}, bf16[8,80,128]{2,1,0:T(8,128)(2,1)S(1)}, u32[]{:S(2)}, u32[]{:S(2)}) %collective-permute-start) | collective-permute-done | bytes 163872 | tf_op jit(solution)/shard_map/ppermute | solution.py:120
  17.5 0.0 copy-done.3
  17.5 1.6 %shard_map.85 = (bf16[16,128,128]{2,1,0:T(8,128)(2,1)S(1)}, bf16[128,1024]{1,0:T(8,128)(2,1)S(1)}, f32[128,1024]{1,0:T(8,128)S(1)}, f32[8,128]{1,0:T(8,128)S(1)}) custom-call(bf16[8,80,128]{2,1,0:T(8,128)(2,1)S(1)} %all_to_all.25.got_ref, bf16[8,80,128]{2,1,0:T(8,128)(2,1)S(1)} %collective-permute-done.other_ref, bf16[8,128,128]{2,1,0:T(8,128)(2,1)S(1)} %copy-done.3, ...), custom_call_target="tpu_custom_call" | custom-call | tf_op jit(solution)/shard_map/pallas_call | solution.py:321
  19.2 17.2 %all_to_all.26.got_ref = bf16[16,128,128]{2,1,0:T(8,128)(2,1)S(1)} all-to-all(bf16[16,128,128]{2,1,0:T(8,128)(2,1)S(1)} %get-tuple-element.22), channel_id=1, replica_groups=mesh['crops'=2,'dap'=16] {'dap'}, dimensions={0} | all-to-all | bytes 1048576 | tf_op jit(solution)/shard_map/all_to_all | solution.py:41
  36.4 0.4 shard_map.86
  36.8 0.0 copy-start.1
  36.8 14.1 %all_to_all.27.got_ref = bf16[16,64,128]{2,1,0:T(8,128)(2,1)S(1)} all-to-all(bf16[16,64,128]{2,1,0:T(8,128)(2,1)S(1)} %shard_map.86), channel_id=1, replica_groups=mesh['crops'=2,'dap'=16] {'dap'}, dimensions={0} | all-to-all | bytes 524288 | tf_op jit(solution)/shard_map/all_to_all | solution.py:41
  50.8 0.0 copy-done.1
  50.8 0.9 %shard_map.87 = (bf16[8,256,128]{2,1,0:T(8,128)(2,1)S(1)}, bf16[128,1024]{1,0:T(8,128)(2,1)S(1)}, f32[128,1024]{1,0:T(8,128)S(1)}) custom-call(bf16[16,64,128]{2,1,0:T(8,128)(2,1)S(1)} %all_to_all.27.got_ref, bf16[128,1024]{1,0:T(8,128)(2,1)S(1)} %get-tuple-element.23.pair_ref, f32[128,1024]{1,0:T(8,128)S(1)} %get-tuple-element.24.gate_ref, ...), custom_call_target="tpu_custom_call" | custom-call | tf_op jit(solution)/shard_map/pallas_call | solution.py:321
  51.8 11.3 %all_to_all.28.got_ref = bf16[8,256,128]{2,1,0:T(8,128)(2,1)S(1)} all-to-all(bf16[8,256,128]{2,1,0:T(8,128)(2,1)S(1)} %get-tuple-element.26), channel_id=1, replica_groups={{0,1,2,3,4,5,6,7},{8,9,10,11,12,13,14,15},{16,17,18,19,20,21,22,23},{24..., dimensions={0} | all-to-all | bytes 1048576 | tf_op jit(solution)/shard_map/all_to_all | solution.py:406
  63.1 0.4 shard_map.88
  63.5 17.6 %all_to_all.29.got_ref = bf16[16,128,128]{2,1,0:T(8,128)(2,1)S(1)} all-to-all(bf16[16,128,128]{2,1,0:T(8,128)(2,1)S(1)} %shard_map.88), channel_id=1, replica_groups=mesh['crops'=2,'dap'=16] {'dap'}, dimensions={0} | all-to-all | bytes 1048576 | tf_op jit(solution)/shard_map/all_to_all | solution.py:41
  81.1 1.2 %shard_map.89 = bf16[8,128,128]{2,1,0:T(8,128)(2,1)} custom-call(bf16[16,128,128]{2,1,0:T(8,128)(2,1)S(1)} %all_to_all.29.got_ref, bf16[128,1024]{1,0:T(8,128)(2,1)S(1)} %get-tuple-element.27.pair_ref, f32[128,1024]{1,0:T(8,128)S(1)} %get-tuple-element.28.gate_ref, bf16[2,128,128]{2,1,0:T(8,128)(2,1)S(1)} %copy-done.1), custom_call_target="tpu_custom_call" | custom-call | tf_op jit(solution)/shard_map/pallas_call | solution.py:321
Async XLA Ops:
  0.0 1.4 %copy-start.4 = (s32[2,128]{1,0:T(2,128)S(1)}, s32[2,128]{1,0:T(2,128)}, u32[]{:S(2)}) copy-start(s32[2,128]{1,0:T(2,128)} %cover_ref.1) | copy-start | bytes 3076
  0.0 1.4 %copy-start.5 = (s32[128]{0:T(128)S(1)}, s32[128]{0:T(128)}, u32[]{:S(2)}) copy-start(s32[128]{0:T(128)} %param.10) | copy-start | bytes 1540
  1.0 15.2 %copy-start.2 = (bf16[1024,128]{1,0:T(8,128)(2,1)S(1)}, bf16[1024,128]{1,0:T(8,128)(2,1)}, u32[]{:S(2)}) copy-start(bf16[1024,128]{1,0:T(8,128)(2,1)} %exit_ref) | copy-start | bytes 786436
  1.4 14.8 %copy-start = (bf16[2,128,5,128]{3,1,2,0:T(8,128)(2,1)S(1)}, bf16[2,128,5,128]{3,1,2,0:T(8,128)(2,1)}, u32[]{:S(2)}) copy-start(bf16[2,128,5,128]{3,1,2,0:T(8,128)(2,1)} %param.14) | copy-start | bytes 983044
  16.1 1.4 %collective-permute-start = (bf16[8,80,128]{2,1,0:T(8,128)(2,1)S(1)}, bf16[8,80,128]{2,1,0:T(8,128)(2,1)S(1)}, u32[]{:S(2)}, u32[]{:S(2)}) collective-permute-start(bf16[8,80,128]{2,1,0:T(8,128)(2,1)S(1)} %all_to_all.25.got_ref), channel_id=1, source_target_pairs={{0,1},{1,0},{2,3},{3,2},{4,5},{5,4},{6,7},{7,6},{8,9},{9,8},{10,11... | collective-permute-start | bytes 491528 | tf_op jit(solution)/shard_map/ppermute | solution.py:120
  16.1 1.4 %copy-start.3 = (bf16[8,128,128]{2,1,0:T(8,128)(2,1)S(1)}, bf16[8,128,128]{2,1,0:T(8,128)(2,1)}, u32[]{:S(2)}) copy-start(bf16[8,128,128]{2,1,0:T(8,128)(2,1)} %couple_ref.1) | copy-start | bytes 786436
  36.8 14.1 %copy-start.1 = (bf16[2,128,128]{2,1,0:T(8,128)(2,1)S(1)}, bf16[2,128,128]{2,1,0:T(8,128)(2,1)}, u32[]{:S(2)}) copy-start(bf16[2,128,128]{2,1,0:T(8,128)(2,1)} %leave_ref.3) | copy-start | bytes 196612

commit v13 on v12

--- a/solution.py
+++ b/solution.py
@@ -18,8 +18,8 @@
     return lax.dot_general(a, b, (((left,), (right,)), ((), ())), preferred_element_type=F32)
 
 
-def sigmoid(values):
-    return 0.5 * jnp.tanh(0.5 * values) + 0.5
+def sigmoid(values, half_scale):
+    return 0.5 * jnp.tanh(values * half_scale) + 0.5
 
 
 def norm(values, axis):
@@ -28,6 +28,13 @@
     centered = values - average
     variance = jnp.sum(centered * centered, axis=axis, keepdims=True) * (1.0 / size)
     return (centered * lax.rsqrt(variance + EPS)).astype(BF16)
+
+
+def centre(values):
+    size = values.shape[0]
+    centered = values - jnp.sum(values, axis=0, keepdims=True) * (1.0 / size)
+    variance = jnp.sum(centered * centered, axis=0, keepdims=True) * (1.0 / size)
+    return centered.astype(BF16), lax.rsqrt(variance + EPS)
 
 
 def standardize_features(values, axis):
@@ -167,11 +174,13 @@
     size = pair.shape[0]
     rows, cols = mask_ref.shape
     share = size // out_ref.shape[0]
-    entries = dot(weights, norm(pair, 0))
+    centered, scale = centre(pair)
+    entries = dot(weights, centered)
     entries = [entries[k * size : (k + 1) * size] for k in range(5)]
-    mask = flat(mask_ref[...])
-    left, right = (sigmoid(entries[k]) * entries[k + 1] * mask for k in (0, 2))
-    gate_ref[...] = sigmoid(entries[4])
+    half = 0.5 * scale
+    mask = flat(mask_ref[...]) * scale
+    left, right = (sigmoid(entries[k], half) * entries[k + 1] * mask for k in (0, 2))
+    gate_ref[...] = sigmoid(entries[4], half)
     for peer in range(out_ref.shape[0]):
         for row in range(rows):
             block = [side[peer * share : (peer + 1) * share, row * cols : (row + 1) * cols] for side in (left, right)]
@@ -283,8 +292,8 @@
 
 
 def updated(products, pair_ref, gate_ref, leave):
-    update = dot(jnp.transpose(leave), norm(jnp.concatenate(products, axis=1), 0))
-    return pair_ref[...].astype(F32) + gate_ref[...] * update
+    centered, scale = centre(jnp.concatenate(products, axis=1))
+    return pair_ref[...].astype(F32) + gate_ref[...] * scale * dot(jnp.transpose(leave), centered)
 
 
 def middle_kernel(got_ref, pair_ref, gate_ref, leave_ref, weight_ref, mask_ref, out_ref, next_ref, next_gate_ref):

time: 82.7 us -> 82.5 us (level)
  no operation moved by 1% of the time
where the time goes in v13:
time: 82.5 us; the launch traced here: 82.2 us
  blocking collectives  74.9 us (91%)
  Pallas kernels  5.06 us (6%)
  waiting for transfers between devices  1.12 us (1%)
  other arithmetic  0.96 us (1%)
    all_to_all x3, blocking collectives, exchange(): lax.all_to_all(blocks, 'dap', split_axis=0, concat_axis=0, tiled=True)  48.9 us
    all_to_all x1, blocking collectives, two_level(): lax.all_to_all(blocks, 'dap', split_axis=0, concat_axis=0, tiled=True, ax...  14.6 us
    all_to_all x1, blocking collectives, fast(): lax.all_to_all(both, 'dap', split_axis=0, concat_axis=0, tiled=True, axis...  11.3 us
    pallas_call x8, Pallas kernels, call(): pl.pallas_call(kernel, out_shape=outputs, in_specs=in_specs or [VMEM] * l...  5.06 us
  transfers between devices with their start and end apart: 1, of which 1 were waited for; matrix products, arithmetic and copies ran while one was open for 0% of the time, Pallas kernels for 0%

profile of v13, /device:TPU:0, one launch (start us, length us, event | category | flops | bytes accessed | tf_op | source)
XLA Modules:
  0.0 82.2 jit_solution(4647913370213064620)
XLA Ops:
  0.0 0.0 copy-start.4
  0.0 0.0 copy-start.5
  0.0 1.0 %pad_maximum_fusion.all_ref = bf16[320,256]{1,0:T(8,128)(2,1)S(1)} fusion(bf16[64,256]{1,0:T(8,128)(2,1)} %bitcast.9, bf16[256,256]{1,0:T(8,128)(2,1)} %bitcast.8), kind=kLoop, calls=%fused_computation | loop fusion | flops 327680 | bytes 327680 | tf_op jit(solution)/shard_map/concatenate | solution.py:360
  1.0 0.0 copy-start.2
  1.0 0.4 shard_map.82.entries_ref
  1.4 0.0 copy-start
  1.4 0.0 copy-done.4
  1.4 0.0 copy-done.5
  1.4 0.1 shard_map.83
  1.5 14.6 %all_to_all.25.got_ref = bf16[8,80,128]{2,1,0:T(8,128)(2,1)S(1)} all-to-all(bf16[8,80,128]{2,1,0:T(8,128)(2,1)S(1)} %shard_map.83), channel_id=1, replica_groups={{0,2,4,6,8,10,12,14},{1,3,5,7,9,11,13,15},{16,18,20,22,24,26,28,30},{17..., dimensions={0} | all-to-all | bytes 327680 | tf_op jit(solution)/shard_map/all_to_all | solution.py:126
  16.1 0.0 collective-permute-start
  16.1 0.0 copy-done.2
  16.1 0.0 copy-done
  16.1 0.0 copy-start.3
  16.2 0.2 shard_map.84
  16.4 1.1 %collective-permute-done.other_ref = bf16[8,80,128]{2,1,0:T(8,128)(2,1)S(1)} collective-permute-done((bf16[8,80,128]{2,1,0:T(8,128)(2,1)S(1)}, bf16[8,80,128]{2,1,0:T(8,128)(2,1)S(1)}, u32[]{:S(2)}, u32[]{:S(2)}) %collective-permute-start) | collective-permute-done | bytes 163872 | tf_op jit(solution)/shard_map/ppermute | solution.py:127
  17.5 0.0 copy-done.3
  17.5 1.6 %shard_map.85 = (bf16[16,128,128]{2,1,0:T(8,128)(2,1)S(1)}, bf16[128,1024]{1,0:T(8,128)(2,1)S(1)}, f32[128,1024]{1,0:T(8,128)S(1)}, f32[8,128]{1,0:T(8,128)S(1)}) custom-call(bf16[8,80,128]{2,1,0:T(8,128)(2,1)S(1)} %all_to_all.25.got_ref, bf16[8,80,128]{2,1,0:T(8,128)(2,1)S(1)} %collective-permute-done.other_ref, bf16[8,128,128]{2,1,0:T(8,128)(2,1)S(1)} %copy-done.3, ...), custom_call_target="tpu_custom_call" | custom-call | tf_op jit(solution)/shard_map/pallas_call | solution.py:330
  19.1 17.2 %all_to_all.26.got_ref = bf16[16,128,128]{2,1,0:T(8,128)(2,1)S(1)} all-to-all(bf16[16,128,128]{2,1,0:T(8,128)(2,1)S(1)} %get-tuple-element.22), channel_id=1, replica_groups=mesh['crops'=2,'dap'=16] {'dap'}, dimensions={0} | all-to-all | bytes 1048576 | tf_op jit(solution)/shard_map/all_to_all | solution.py:48
  36.4 0.4 shard_map.86
  36.7 0.0 copy-start.1
  36.7 14.1 %all_to_all.27.got_ref = bf16[16,64,128]{2,1,0:T(8,128)(2,1)S(1)} all-to-all(bf16[16,64,128]{2,1,0:T(8,128)(2,1)S(1)} %shard_map.86), channel_id=1, replica_groups=mesh['crops'=2,'dap'=16] {'dap'}, dimensions={0} | all-to-all | bytes 524288 | tf_op jit(solution)/shard_map/all_to_all | solution.py:48
  50.8 0.0 copy-done.1
  50.8 0.9 %shard_map.87 = (bf16[8,256,128]{2,1,0:T(8,128)(2,1)S(1)}, bf16[128,1024]{1,0:T(8,128)(2,1)S(1)}, f32[128,1024]{1,0:T(8,128)S(1)}) custom-call(bf16[16,64,128]{2,1,0:T(8,128)(2,1)S(1)} %all_to_all.27.got_ref, bf16[128,1024]{1,0:T(8,128)(2,1)S(1)} %get-tuple-element.23.pair_ref, f32[128,1024]{1,0:T(8,128)S(1)} %get-tuple-element.24.gate_ref, ...), custom_call_target="tpu_custom_call" | custom-call | tf_op jit(solution)/shard_map/pallas_call | solution.py:330
  51.7 11.3 %all_to_all.28.got_ref = bf16[8,256,128]{2,1,0:T(8,128)(2,1)S(1)} all-to-all(bf16[8,256,128]{2,1,0:T(8,128)(2,1)S(1)} %get-tuple-element.26), channel_id=1, replica_groups={{0,1,2,3,4,5,6,7},{8,9,10,11,12,13,14,15},{16,17,18,19,20,21,22,23},{24..., dimensions={0} | all-to-all | bytes 1048576 | tf_op jit(solution)/shard_map/all_to_all | solution.py:415
  63.0 0.4 shard_map.88
  63.4 17.6 %all_to_all.29.got_ref = bf16[16,128,128]{2,1,0:T(8,128)(2,1)S(1)} all-to-all(bf16[16,128,128]{2,1,0:T(8,128)(2,1)S(1)} %shard_map.88), channel_id=1, replica_groups=mesh['crops'=2,'dap'=16] {'dap'}, dimensions={0} | all-to-all | bytes 1048576 | tf_op jit(solution)/shard_map/all_to_all | solution.py:48
  81.0 1.1 %shard_map.89 = bf16[8,128,128]{2,1,0:T(8,128)(2,1)} custom-call(bf16[16,128,128]{2,1,0:T(8,128)(2,1)S(1)} %all_to_all.29.got_ref, bf16[128,1024]{1,0:T(8,128)(2,1)S(1)} %get-tuple-element.27.pair_ref, f32[128,1024]{1,0:T(8,128)S(1)} %get-tuple-element.28.gate_ref, bf16[2,128,128]{2,1,0:T(8,128)(2,1)S(1)} %copy-done.1), custom_call_target="tpu_custom_call" | custom-call | tf_op jit(solution)/shard_map/pallas_call | solution.py:330
Async XLA Ops:
  0.0 1.4 %copy-start.4 = (s32[2,128]{1,0:T(2,128)S(1)}, s32[2,128]{1,0:T(2,128)}, u32[]{:S(2)}) copy-start(s32[2,128]{1,0:T(2,128)} %cover_ref.1) | copy-start | bytes 3076
  0.0 1.4 %copy-start.5 = (s32[128]{0:T(128)S(1)}, s32[128]{0:T(128)}, u32[]{:S(2)}) copy-start(s32[128]{0:T(128)} %param.10) | copy-start | bytes 1540
  1.0 15.2 %copy-start.2 = (bf16[1024,128]{1,0:T(8,128)(2,1)S(1)}, bf16[1024,128]{1,0:T(8,128)(2,1)}, u32[]{:S(2)}) copy-start(bf16[1024,128]{1,0:T(8,128)(2,1)} %exit_ref) | copy-start | bytes 786436
  1.4 14.8 %copy-start = (bf16[2,128,5,128]{3,1,2,0:T(8,128)(2,1)S(1)}, bf16[2,128,5,128]{3,1,2,0:T(8,128)(2,1)}, u32[]{:S(2)}) copy-start(bf16[2,128,5,128]{3,1,2,0:T(8,128)(2,1)} %param.14) | copy-start | bytes 983044
  16.1 1.4 %collective-permute-start = (bf16[8,80,128]{2,1,0:T(8,128)(2,1)S(1)}, bf16[8,80,128]{2,1,0:T(8,128)(2,1)S(1)}, u32[]{:S(2)}, u32[]{:S(2)}) collective-permute-start(bf16[8,80,128]{2,1,0:T(8,128)(2,1)S(1)} %all_to_all.25.got_ref), channel_id=1, source_target_pairs={{0,1},{1,0},{2,3},{3,2},{4,5},{5,4},{6,7},{7,6},{8,9},{9,8},{10,11... | collective-permute-start | bytes 491528 | tf_op jit(solution)/shard_map/ppermute | solution.py:127
  16.1 1.4 %copy-start.3 = (bf16[8,128,128]{2,1,0:T(8,128)(2,1)S(1)}, bf16[8,128,128]{2,1,0:T(8,128)(2,1)}, u32[]{:S(2)}) copy-start(bf16[8,128,128]{2,1,0:T(8,128)(2,1)} %couple_ref.1) | copy-start | bytes 786436
  36.7 14.1 %copy-start.1 = (bf16[2,128,128]{2,1,0:T(8,128)(2,1)S(1)}, bf16[2,128,128]{2,1,0:T(8,128)(2,1)}, u32[]{:S(2)}) copy-start(bf16[2,128,128]{2,1,0:T(8,128)(2,1)} %leave_ref.3) | copy-start | bytes 196612

commit v14 on v13

--- a/solution.py
+++ b/solution.py
@@ -188,7 +188,7 @@
             out_ref[peer, at : at + 2 * share, :] = jnp.concatenate(block, axis=0).astype(BF16)
 
 
-def weight_kernel(entry_ref, exit_ref, out_entry, out_exit, rows_ref):
+def weight_kernel(entry_ref, exit_ref, couple_ref, out_entry, out_exit, out_couple, rows_ref):
     for t in range(entry_ref.shape[0]):
         for k in range(entry_ref.shape[1]):
             out_entry[t, k * LANES : (k + 1) * LANES, :] = jnp.transpose(entry_ref[t, k])
@@ -196,6 +196,8 @@
     step = spread(exit_ref[...].astype(F32).reshape(width, width, LANES), rows_ref)
     leave = jnp.concatenate([rows_ref[pl.ds(e, width, stride=step), :] for e in range(width)], axis=0)
     out_exit[...] = jnp.transpose(leave).astype(BF16)
+    for row in range(couple_ref.shape[0]):
+        out_couple[:, row * LANES : (row + 1) * LANES] = jnp.transpose(couple_ref[row])
 
 
 def outer_kernel(
@@ -205,7 +207,7 @@
 ):
     pairs, _, cols = got_ref.shape
     devices = 2 * pairs
-    rows = couple_ref.shape[0]
+    rows = couple_ref.shape[1] // cols
     held, width = 2, 32
     core = lax.rem(lax.axis_index("dap"), 2)
     for side, ref in enumerate((got_ref, other_ref)):
@@ -258,8 +260,7 @@
                 outer_ref[(e + more) * width : (e + more + 1) * width, i * cols : (i + 1) * cols] = result[
                     i * width : (i + 1) * width, more * cols : (more + 1) * cols
                 ]
-    couple = jnp.concatenate([jnp.transpose(couple_ref[row]) for row in range(rows)], axis=1)
-    pair = (couple.astype(F32) + dot(exit_ref[...], outer_ref[...]) * flat(scale)).astype(BF16)
+    pair = (couple_ref[...].astype(F32) + dot(exit_ref[...], outer_ref[...]) * flat(scale)).astype(BF16)
     pair_ref[...] = pair
     project(pair.astype(F32), weight_ref[0], mask_ref, out_ref, gate_ref)
 
@@ -370,14 +371,17 @@
         (entries, coverage_indicator, genuine_amino_flag.reshape(1, cols)),
         [shape((devices // 2, held * width + 16, cols))],
     )
-    packed, entry, exit_rows = lax.optimization_barrier((packed, trilateral_entry_matrices, pairing_exit_matrix))
+    packed, entry, exit_rows, couple_rows = lax.optimization_barrier(
+        (packed, trilateral_entry_matrices, pairing_exit_matrix, couple_embedding)
+    )
     got = two_level(packed, devices)
-    entry, exit_matrix = call(
+    entry, exit_matrix, couple = call(
         weight_kernel,
-        (jnp.transpose(entry, (0, 2, 1, 3)), exit_rows),
+        (jnp.transpose(entry, (0, 2, 1, 3)), exit_rows, couple_rows),
         [
             shape((2, 5 * channels, channels)),
             shape((channels, width * width)),
+            shape((channels, rows * cols)),
         ],
         [pltpu.VMEM((width * (width + GAP), channels), F32)],
     )
@@ -390,7 +394,7 @@
 
     both, pair, gate, row_mask = call(
         outer_kernel,
-        (*got, couple_embedding, exit_matrix, entry),
+        (*got, couple, exit_matrix, entry),
         projected(devices) + [shape((rows, cols), F32)],
         [
             pltpu.VMEM((devices * (held * width + GAP), cols), F32),

time: 82.5 us -> 82.5 us (level)
  no operation moved by 1% of the time
where the time goes in v14:
time: 82.5 us; the launch traced here: 82.2 us
  blocking collectives  74.9 us (91%)
  Pallas kernels  5.12 us (6%)
  waiting for transfers between devices  1.05 us (1%)
  other arithmetic  0.98 us (1%)
    all_to_all x3, blocking collectives, exchange(): lax.all_to_all(blocks, 'dap', split_axis=0, concat_axis=0, tiled=True)  48.9 us
    all_to_all x1, blocking collectives, two_level(): lax.all_to_all(blocks, 'dap', split_axis=0, concat_axis=0, tiled=True, ax...  14.6 us
    all_to_all x1, blocking collectives, fast(): lax.all_to_all(both, 'dap', split_axis=0, concat_axis=0, tiled=True, axis...  11.3 us
    pallas_call x8, Pallas kernels, call(): pl.pallas_call(kernel, out_shape=outputs, in_specs=in_specs or [VMEM] * l...  5.12 us
  transfers between devices with their start and end apart: 1, of which 1 were waited for; matrix products, arithmetic and copies ran while one was open for 0% of the time, Pallas kernels for 0%

profile of v14, /device:TPU:0, one launch (start us, length us, event | category | flops | bytes accessed | tf_op | source)
XLA Modules:
  0.0 82.2 jit_solution(2755312733412940143)
XLA Ops:
  0.0 0.0 copy-start.4
  0.0 0.0 copy-start.5
  0.0 0.0 copy-start.3
  0.0 1.0 %pad_maximum_fusion.all_ref = bf16[320,256]{1,0:T(8,128)(2,1)S(1)} fusion(bf16[64,256]{1,0:T(8,128)(2,1)} %bitcast.9, bf16[256,256]{1,0:T(8,128)(2,1)} %bitcast.8), kind=kLoop, calls=%fused_computation | loop fusion | flops 327680 | bytes 327680 | tf_op jit(solution)/shard_map/concatenate | solution.py:361
  1.0 0.0 copy-start.2
  1.0 0.4 shard_map.82.entries_ref
  1.4 0.0 copy-start
  1.4 0.0 copy-done.4
  1.4 0.0 copy-done.5
  1.4 0.1 shard_map.83
  1.5 14.6 %all_to_all.25.got_ref = bf16[8,80,128]{2,1,0:T(8,128)(2,1)S(1)} all-to-all(bf16[8,80,128]{2,1,0:T(8,128)(2,1)S(1)} %shard_map.83), channel_id=1, replica_groups={{0,2,4,6,8,10,12,14},{1,3,5,7,9,11,13,15},{16,18,20,22,24,26,28,30},{17..., dimensions={0} | all-to-all | bytes 327680 | tf_op jit(solution)/shard_map/all_to_all | solution.py:126
  16.2 0.0 collective-permute-start
  16.2 0.0 copy-done.3
  16.2 0.0 copy-done.2
  16.2 0.0 copy-done
  16.2 0.3 shard_map.84
  16.5 1.1 %collective-permute-done.other_ref = bf16[8,80,128]{2,1,0:T(8,128)(2,1)S(1)} collective-permute-done((bf16[8,80,128]{2,1,0:T(8,128)(2,1)S(1)}, bf16[8,80,128]{2,1,0:T(8,128)(2,1)S(1)}, u32[]{:S(2)}, u32[]{:S(2)}) %collective-permute-start) | collective-permute-done | bytes 163872 | tf_op jit(solution)/shard_map/ppermute | solution.py:127
  17.6 1.6 %shard_map.85 = (bf16[16,128,128]{2,1,0:T(8,128)(2,1)S(1)}, bf16[128,1024]{1,0:T(8,128)(2,1)S(1)}, f32[128,1024]{1,0:T(8,128)S(1)}, f32[8,128]{1,0:T(8,128)S(1)}) custom-call(bf16[8,80,128]{2,1,0:T(8,128)(2,1)S(1)} %all_to_all.25.got_ref, bf16[8,80,128]{2,1,0:T(8,128)(2,1)S(1)} %collective-permute-done.other_ref, ...), custom_call_target="tpu_custom_call" | custom-call | tf_op jit(solution)/shard_map/pallas_call | solution.py:331
  19.2 17.2 %all_to_all.26.got_ref = bf16[16,128,128]{2,1,0:T(8,128)(2,1)S(1)} all-to-all(bf16[16,128,128]{2,1,0:T(8,128)(2,1)S(1)} %get-tuple-element.26), channel_id=1, replica_groups=mesh['crops'=2,'dap'=16] {'dap'}, dimensions={0} | all-to-all | bytes 1048576 | tf_op jit(solution)/shard_map/all_to_all | solution.py:48
  36.4 0.4 shard_map.86
  36.7 0.0 copy-start.1
  36.8 14.1 %all_to_all.27.got_ref = bf16[16,64,128]{2,1,0:T(8,128)(2,1)S(1)} all-to-all(bf16[16,64,128]{2,1,0:T(8,128)(2,1)S(1)} %shard_map.86), channel_id=1, replica_groups=mesh['crops'=2,'dap'=16] {'dap'}, dimensions={0} | all-to-all | bytes 524288 | tf_op jit(solution)/shard_map/all_to_all | solution.py:48
  50.8 0.0 copy-done.1
  50.8 0.9 %shard_map.87 = (bf16[8,256,128]{2,1,0:T(8,128)(2,1)S(1)}, bf16[128,1024]{1,0:T(8,128)(2,1)S(1)}, f32[128,1024]{1,0:T(8,128)S(1)}) custom-call(bf16[16,64,128]{2,1,0:T(8,128)(2,1)S(1)} %all_to_all.27.got_ref, bf16[128,1024]{1,0:T(8,128)(2,1)S(1)} %get-tuple-element.27.pair_ref, f32[128,1024]{1,0:T(8,128)S(1)} %get-tuple-element.28.gate_ref, ...), custom_call_target="tpu_custom_call" | custom-call | tf_op jit(solution)/shard_map/pallas_call | solution.py:331
  51.7 11.3 %all_to_all.28.got_ref = bf16[8,256,128]{2,1,0:T(8,128)(2,1)S(1)} all-to-all(bf16[8,256,128]{2,1,0:T(8,128)(2,1)S(1)} %get-tuple-element.30), channel_id=1, replica_groups={{0,1,2,3,4,5,6,7},{8,9,10,11,12,13,14,15},{16,17,18,19,20,21,22,23},{24..., dimensions={0} | all-to-all | bytes 1048576 | tf_op jit(solution)/shard_map/all_to_all | solution.py:419
  63.0 0.4 shard_map.88
  63.4 17.6 %all_to_all.29.got_ref = bf16[16,128,128]{2,1,0:T(8,128)(2,1)S(1)} all-to-all(bf16[16,128,128]{2,1,0:T(8,128)(2,1)S(1)} %shard_map.88), channel_id=1, replica_groups=mesh['crops'=2,'dap'=16] {'dap'}, dimensions={0} | all-to-all | bytes 1048576 | tf_op jit(solution)/shard_map/all_to_all | solution.py:48
  81.0 1.1 %shard_map.89 = bf16[8,128,128]{2,1,0:T(8,128)(2,1)} custom-call(bf16[16,128,128]{2,1,0:T(8,128)(2,1)S(1)} %all_to_all.29.got_ref, bf16[128,1024]{1,0:T(8,128)(2,1)S(1)} %get-tuple-element.31.pair_ref, f32[128,1024]{1,0:T(8,128)S(1)} %get-tuple-element.32.gate_ref, bf16[2,128,128]{2,1,0:T(8,128)(2,1)S(1)} %copy-done.1), custom_call_target="tpu_custom_call" | custom-call | tf_op jit(solution)/shard_map/pallas_call | solution.py:331
Async XLA Ops:
  0.0 1.4 %copy-start.4 = (s32[2,128]{1,0:T(2,128)S(1)}, s32[2,128]{1,0:T(2,128)}, u32[]{:S(2)}) copy-start(s32[2,128]{1,0:T(2,128)} %cover_ref.1) | copy-start | bytes 3076
  0.0 1.4 %copy-start.5 = (s32[128]{0:T(128)S(1)}, s32[128]{0:T(128)}, u32[]{:S(2)}) copy-start(s32[128]{0:T(128)} %param.10) | copy-start | bytes 1540
  0.0 16.2 %copy-start.3 = (bf16[8,128,128]{2,1,0:T(8,128)(2,1)S(1)}, bf16[8,128,128]{2,1,0:T(8,128)(2,1)}, u32[]{:S(2)}) copy-start(bf16[8,128,128]{2,1,0:T(8,128)(2,1)} %couple_ref) | copy-start | bytes 786436
  1.0 15.2 %copy-start.2 = (bf16[1024,128]{1,0:T(8,128)(2,1)S(1)}, bf16[1024,128]{1,0:T(8,128)(2,1)}, u32[]{:S(2)}) copy-start(bf16[1024,128]{1,0:T(8,128)(2,1)} %exit_ref) | copy-start | bytes 786436
  1.4 14.8 %copy-start = (bf16[2,128,5,128]{3,1,2,0:T(8,128)(2,1)S(1)}, bf16[2,128,5,128]{3,1,2,0:T(8,128)(2,1)}, u32[]{:S(2)}) copy-start(bf16[2,128,5,128]{3,1,2,0:T(8,128)(2,1)} %param.14) | copy-start | bytes 983044
  16.2 1.4 %collective-permute-start = (bf16[8,80,128]{2,1,0:T(8,128)(2,1)S(1)}, bf16[8,80,128]{2,1,0:T(8,128)(2,1)S(1)}, u32[]{:S(2)}, u32[]{:S(2)}) collective-permute-start(bf16[8,80,128]{2,1,0:T(8,128)(2,1)S(1)} %all_to_all.25.got_ref), channel_id=1, source_target_pairs={{0,1},{1,0},{2,3},{3,2},{4,5},{5,4},{6,7},{7,6},{8,9},{9,8},{10,11... | collective-permute-start | bytes 491528 | tf_op jit(solution)/shard_map/ppermute | solution.py:127
  36.7 14.1 %copy-start.1 = (bf16[2,128,128]{2,1,0:T(8,128)(2,1)S(1)}, bf16[2,128,128]{2,1,0:T(8,128)(2,1)}, u32[]{:S(2)}) copy-start(bf16[2,128,128]{2,1,0:T(8,128)(2,1)} %leave_ref.3) | copy-start | bytes 196612
